TPU v7x, 32 devices: a whole 2x2x4 slice. The times are simulated.
32 devices in a mesh: sector: 4 (over y, core), owner: 8 (over z, x).
Axes of the slice: x: 2, y: 2, z: 4, core: 2. Of those that a mesh axis runs over, the one named last changes fastest.
Arguments:
- broadcast_ops: float32 [4, 4, 1024, 1024], P('sector', None, 'owner'), may hold values from -0.1875 to 0.1875
- resident_ops: float32 [4, 8, 1024, 1024], P('sector', 'owner'), may hold values from -6 to 6
- integrals: float32 [4, 8, 4, 4], P('sector', 'owner'), may hold values from -3 to 3
- owner_list: int32 [8, 4], P('owner'), may hold values from 0 to 3, as said below
Outputs:
- complementary: float32 [4, 8, 2, 1024, 1024], P('sector', 'owner')
Inputs may be any that keep to these rules, and one draw needn't show every extreme that they name: `owner_list`: in each row one sector group is named exactly 2 times, one is not named, and every other is named once.
All inputs are finite; a program needn't handle non-finite values.
Results may differ from a plain program's by a relative error of at most 0.012.
Values may be sent and summed in bfloat16 or wider, within the bound.
No kernel may reach another device: no remote copies, remote signals or barrier semaphores. Data moves between devices by JAX's collectives and lax.ppermute only.
A program may use at most 64 MiB of HBM per device.

v0:
```python
import jax
import jax.numpy as jnp
from jax import lax
from jax.sharding import PartitionSpec as P

CAP = 2


def shards(broadcast_ops, resident_ops, integrals, owner_list):
    highest = lax.Precision.HIGHEST
    shared = broadcast_ops[0]
    resident = resident_ops[0, 0]
    weights = integrals[0, 0]
    owners = owner_list[0]
    pair_count = owners.shape[0]
    slot_count = CAP
    products = jnp.einsum(
        "krj,jn->krn",
        lax.all_gather(shared.astype(jnp.bfloat16), "owner", axis=1, tiled=True).astype(
            jnp.float32
        ),
        resident,
        precision=highest,
    )
    pair_index = jnp.arange(pair_count)
    same_owner = owners[:, None] == owners[None, :]
    earlier = pair_index[:, None] < pair_index[None, :]
    slot_rank = jnp.sum((same_owner & earlier).astype(jnp.int32), axis=0)
    slot_index = jnp.arange(slot_count * lax.axis_size("sector"))
    target_sector = slot_index // slot_count
    target_slot = slot_index % slot_count
    selector = (
        (owners[None, :] == target_sector[:, None]) & (slot_rank[None, :] == target_slot[:, None])
    ).astype(jnp.float32)
    chosen = jnp.dot(selector, weights, precision=highest)
    result = lax.psum_scatter(
        jnp.einsum("jk,kmn->jmn", chosen, products, precision=highest).astype(jnp.bfloat16),
        "sector",
        scatter_dimension=0,
        tiled=True,
    ).astype(jnp.float32)
    return result[None, None]


def solution(mesh):
    in_specs = (
        P("sector", None, "owner", None),
        P("sector", "owner", None, None),
        P("sector", "owner", None, None),
        P("owner", None),
    )
    out_specs = P("sector", "owner", None, None, None)
    return jax.shard_map(shards, mesh=mesh, in_specs=in_specs, out_specs=out_specs, check_vma=False)
```

profile of v0, /device:TPU:0, one launch (start us, length us, event | category | flops | bytes accessed | tf_op | source)
XLA Modules:
  0.0 368.5 jit_solution(6293870826038606774)
XLA Ops:
  6.5 0.0 copy-start
  6.5 0.0 all-gather.3.cloned.1.call-start
  6.5 2.7 convert_element_type.16
  9.3 0.0 all-gather.3.cloned.1.call-update
  9.3 0.0 reduce-scatter.2.cloned.1.call-start
  9.4 0.8 convert_reduce_fusion
  10.2 0.0 copy-done
  10.2 0.8 convolution_bitcast_fusion
  11.0 126.2 %all-gather.3.cloned.1.call-done = bf16[1,4,1024,1024]{3,2,1,0:T(8,128)(2,1)} async-done(((bf16[1,4,128,1024]{3,2,1,0:T(8,128)(2,1)}), bf16[1,4,1024,1024]{3,2,1,0:T(8,128)(2,1)}) %all-gather.3.cloned.1.call-update) | async-done | bytes 8388624 | tf_op jit(solution)/shard_map/all_gather | solution.py:19
  137.2 31.5 %fusion.5 = f32[4,1024,1024]{2,1,0:T(8,128)S(1)} fusion(bf16[1,4,1024,1024]{3,2,1,0:T(8,128)(2,1)} %all-gather.3.cloned.1.call-done, f32[1,1,1024,1024]{3,2,1,0:T(8,128)} %param.5), kind=kOutput, calls=%fused_computation.3 | convolution fusion | flops 51539607552 | bytes 29360128 | tf_op jit(solution)/shard_map/krj,jn->krn/dot_general | solution.py:17
  168.7 41.2 %fusion.2 = bf16[8,1024,1024]{2,0,1:T(8,128)(2,1)S(1)} fusion(f32[8,4,1]{0,1,2:T(4,128)S(1)} %convolution_bitcast_fusion, f32[4,1024,1024]{2,1,0:T(8,128)S(1)} %fusion.5), kind=kOutput, calls=%fused_computation.2 | convolution fusion | flops 411041792 | bytes 33554560 | tf_op jit(solution)/shard_map/jk,kmn->jmn/dot_general | solution.py:37
  209.9 20.6 %copy.8 = bf16[8,1024,1024]{2,1,0:T(8,128)(2,1)} copy(bf16[8,1024,1024]{2,0,1:T(8,128)(2,1)S(1)} %fusion.2) | data formatting | bytes 33554432 | tf_op jit(solution)/shard_map/convert_element_type | solution.py:37
  230.6 0.0 reduce-scatter.2.cloned.1.call-update
  230.6 0.0 copy-start.1
  230.6 124.4 %reduce-scatter.2.cloned.1.call-done = bf16[2,1024,1024]{2,1,0:T(8,128)(2,1)} async-done(((bf16[8,1024,1024]{2,1,0:T(8,128)(2,1)}), bf16[2,1024,1024]{2,1,0:T(8,128)(2,1)}) %reduce-scatter.2.cloned.1.call-update) | async-done | bytes 4194320 | tf_op jit(solution)/shard_map/reduce_scatter | solution.py:36
  355.0 6.6 %bitcast_convert_fusion = f32[1,1,2,1024,1024]{4,3,2,1,0:T(8,128)} fusion(bf16[2,1024,1024]{2,1,0:T(8,128)(2,1)} %reduce-scatter.2.cloned.1.call-done), kind=kLoop, calls=%fused_computation.5 | loop fusion | flops 2097152 | bytes 12582912 | tf_op jit(solution)/shard_map/broadcast_in_dim | solution.py:42
  361.7 0.0 copy-done.1
  (1 shorter events, 0.0 us)
Async XLA Ops:
  6.5 3.6 copy-start
  6.5 130.7 %all-gather.3.cloned.1.call-start = ((), (), s32[]{:S(2)}) async-start(), calls=%async_computation.2 | async-start | bytes 9437184 | tf_op jit(solution)/shard_map/all_gather | solution.py:19
  9.3 345.7 %reduce-scatter.2.cloned.1.call-start = ((), (), s32[]{:S(2)}) async-start(), calls=%async_computation.1 | async-start | bytes 20971520 | tf_op jit(solution)/shard_map/reduce_scatter | solution.py:36
  230.6 131.1 %copy-start.1 = (f32[1,1,4,4]{3,2,1,0:T(4,128)S(1)}, f32[1,1,4,4]{3,2,1,0:T(4,128)}, u32[]{:S(2)}) copy-start(f32[1,1,4,4]{3,2,1,0:T(4,128)} %param.6) | copy-start | bytes 196
Sparse Core Ops, SparseCore 0:
  9.5 127.5 all-gather.2
  230.7 124.2 reduce-scatter.1
where the time goes:
time: 369 us
  waiting for transfers between devices  251 us (68%)
  matrix products  73.6 us (20%)
  local copies, waits for them, and re-layouts  20.7 us (6%)
  between operations  13.4 us (4%)
  other arithmetic  10.2 us (3%)
    all_gather x1, waiting for transfers between devices, shards(): lax.all_gather(shared.astype(jnp.bfloat16), 'owner', axis=1, tiled=True)  126 us
    reduce_scatter x1, waiting for transfers between devices, shards(): lax.psum_scatter(jnp.einsum('jk,kmn->jmn', chosen, products, precision=hi...  124 us
    dot_general x1, matrix products, shards(): jnp.einsum('jk,kmn->jmn', chosen, products, precision=highest)  41.2 us
    dot_general x1, matrix products, shards(): jnp.einsum('krj,jn->krn', lax.all_gather(shared.astype(jnp.bfloat16), 'ow...  31.5 us
    convert_element_type x1, local copies, waits for them, and re-layouts, shards(): jnp.einsum('jk,kmn->jmn', chosen, products, precision=highest)  20.6 us
  transfers between devices with their start and end apart: 2, of which 2 were waited for; matrix products, arithmetic and copies ran while one was open for 0% of the time, Pallas kernels for 0%

commit v1 on v0

v1 whole, which is shorter than its diff:
```python
import functools

import jax
import jax.numpy as jnp
from jax import lax
from jax.experimental import pallas as pl
from jax.experimental.pallas import tpu as pltpu
from jax.sharding import PartitionSpec as P

CAP = 2
BF16 = jnp.bfloat16
F32 = jnp.float32


def ring_order(n):
    return list(range(0, n, 2)) + list(range(1, n, 2))[::-1]


def plan_of(owners_ref, side):
    n = owners_ref.shape[1]
    own = [owners_ref[0, p] for p in range(n)]
    rank, key = [], []
    for p in range(n):
        r = jnp.int32(0)
        for q in range(p):
            r = r + (own[q] == own[p]).astype(jnp.int32)
        rank.append(r)
        key.append(own[p] * CAP + r)
    place = []
    for p in range(n):
        r = jnp.int32(0)
        for q in range(n):
            if q != p:
                r = r + (key[q] < key[p]).astype(jnp.int32)
        place.append(jnp.where(side == 0, r, n - 1 - r))
    pair_at = []
    for i in range(n):
        r = jnp.int32(0)
        for p in range(n):
            r = r + jnp.where(place[p] == i, p, 0)
        pair_at.append(r)

    def slot_place(sector, slot):
        r = jnp.int32(-1)
        for p in range(n):
            r = jnp.where((own[p] == sector) & (rank[p] == slot), place[p], r)
        return r

    return pair_at, slot_place


def step_kernel(cfg, *refs):
    names = cfg["names"]
    r = dict(zip(names, refs, strict=True))
    lanes, half, n_owner = cfg["lanes"], cfg["half"], cfg["n_owner"]
    pairs, sent = cfg["pairs"], cfg["sent"]
    ids = r["ids"]
    side, core, q = ids[0], ids[1], ids[2]
    pair_at, slot_place = plan_of(r["owners"], side)
    sector = side * 2 + core
    other = side * 2 + 1 - core
    m, depth = cfg["m"], cfg["m"]
    if cfg["compute"] is not None:
        loads = []
        for t in range(cfg["tiles"]):
            w = m // cfg["tiles"]
            for s, name in enumerate(("res0", "res1")):
                c = pltpu.make_async_copy(
                    r[name].at[:, pl.ds(t * w, w)],
                    r["rbuf"].at[t, pl.ds(s * depth, depth), :],
                    r["rsem"].at[t, s],
                )
                c.start()
                loads.append(c)

    def rows_of(step, lane, which):
        turn, start, _ = lanes[lane]
        at = lax.rem(q - turn * step + 2 * n_owner, n_owner)
        owner = jnp.where(at < n_owner // 2, 2 * at, 2 * (n_owner - 1 - at) + 1)
        return pl.multiple_of(owner * (2 * half) + which * half + start, 8)

    stores = []

    def store(buf, step, which, sem):
        for lane, (_, start, rows) in enumerate(lanes):
            c = pltpu.make_async_copy(
                r[buf].at[:, pl.ds(start, rows), :],
                r["out"].at[:, pl.ds(rows_of(step, lane, which), rows), :],
                r["osem"].at[sem, lane],
            )
            c.start()
            stores.append(c)

    if cfg["finish"] is not None:
        for slot in range(CAP):
            place = slot_place(other, slot)
            i = jnp.maximum(place, 0)
            v = r["kept_in"][i] + r["crossed"][sent - 1 - i].astype(F32)
            r["swap_out"][slot] = v.astype(BF16)
        for slot in range(CAP):
            place = slot_place(sector, slot)
            i = jnp.maximum(place, 0)
            v = r["kept_in"][i] + r["crossed"][sent - 1 - i].astype(F32)
            r["fin"][slot] = jnp.where(place >= 0, v, 0.0)
        store("fin", cfg["finish"], core, 0)
    if cfg["place"] is not None:
        for slot in range(CAP):
            place = slot_place(sector, slot)
            r["fin2"][slot] = jnp.where(place >= 0, r["swapped"][slot].astype(F32), 0.0)
        store("fin2", cfg["place"], 1 - core, 1)

    if cfg["compute"] is not None:
        nb = cfg["nb"]
        for s, wname in enumerate(("w0", "w1")):
            for lane, (_, start, rows) in enumerate(lanes):
                x = [r[f"x{lane}"][s, k].astype(F32) for k in range(nb)]
                for i in range(pairs):
                    a = r[wname][pair_at[i], 0] * x[0]
                    for k in range(1, nb):
                        a = a + r[wname][pair_at[i], k] * x[k]
                    r["abuf"][pl.ds(i * half + start, rows), pl.ds(s * depth, depth)] = a.astype(BF16)
        w = m // cfg["tiles"]
        for t in range(cfg["tiles"]):
            loads[2 * t].wait()
            loads[2 * t + 1].wait()
            y = jnp.dot(r["abuf"][...], r["rbuf"][t], preferred_element_type=F32)
            y = y.reshape(pairs, half, w)
            r["send"][:, :, pl.ds(t * w, w)] = y[pairs - sent :].astype(BF16)
            r["kept"][:, :, pl.ds(t * w, w)] = y[:sent]
    for c in stores:
        c.wait()


def step_call(static, compute, finish, place, common, xs, res, kept, crossed, swapped, out):
    m, half, lanes, pairs, sent = (static[k] for k in ("m", "half", "lanes", "pairs", "sent"))
    smem = pl.BlockSpec(memory_space=pltpu.SMEM)
    vmem = pl.BlockSpec(memory_space=pltpu.VMEM)
    anym = pl.BlockSpec(memory_space=pl.ANY)
    names, args, specs = [], [], []

    def add(name, arg, spec):
        names.append(name)
        args.append(arg)
        specs.append(spec)

    for name in ("ids", "owners"):
        add(name, common[name], smem)
    if compute is not None:
        for name in ("w0", "w1"):
            add(name, common[name], smem)
        for lane, x in enumerate(xs):
            add(f"x{lane}", x, vmem)
        add("res0", res[0], anym)
        add("res1", res[1], anym)
    if finish is not None:
        add("kept_in", kept, vmem)
        add("crossed", crossed, vmem)
    if place is not None:
        add("swapped", swapped, vmem)
    aliases = {}
    writes = finish is not None or place is not None
    if writes and out is not None:
        aliases[len(names)] = "out"
        add("out_in", out, anym)
    outs, shapes, ospecs = [], [], []

    def give(name, shape, dtype, spec):
        outs.append(name)
        shapes.append(jax.ShapeDtypeStruct(shape, dtype))
        ospecs.append(spec)

    if compute is not None:
        give("send", (sent, half, m), BF16, vmem)
        give("kept", (sent, half, m), F32, vmem)
    if finish is not None:
        give("swap_out", (CAP, half, m), BF16, vmem)
    if writes:
        give("out", (CAP, m, m), F32, anym)
    aliases = {i: outs.index(n) for i, n in aliases.items()}
    scratch, snames = [], []

    def hold(name, s):
        snames.append(name)
        scratch.append(s)

    tiles = 4
    if compute is not None:
        hold("abuf", pltpu.VMEM((pairs * half, 2 * m), BF16))
        hold("rbuf", pltpu.VMEM((tiles, 2 * m, m // tiles), BF16))
        hold("rsem", pltpu.SemaphoreType.DMA((tiles, 2)))
    if finish is not None:
        hold("fin", pltpu.VMEM((CAP, half, m), F32))
    if place is not None:
        hold("fin2", pltpu.VMEM((CAP, half, m), F32))
    if writes:
        hold("osem", pltpu.SemaphoreType.DMA((2, len(lanes))))
    cfg = dict(static, compute=compute, finish=finish, place=place, tiles=tiles, names=names + outs + snames)
    flops = 2 * pairs * half * 2 * m * m if compute is not None else 2 * half * m
    got = pl.pallas_call(
        functools.partial(step_kernel, cfg),
        in_specs=specs,
        out_specs=ospecs,
        out_shape=shapes,
        scratch_shapes=scratch,
        input_output_aliases=aliases,
        compiler_params=pltpu.CompilerParams(vmem_limit_bytes=32 * 1024 * 1024),
        cost_estimate=pl.CostEstimate(flops=flops, bytes_accessed=8 * m * m, transcendentals=0),
    )(*args)
    return dict(zip(outs, got, strict=True))


def shards(broadcast_ops, resident_ops, integrals, owner_list):
    n_sector = lax.axis_size("sector")
    n_owner = lax.axis_size("owner")
    sector = lax.axis_index("sector")
    owner = lax.axis_index("owner")
    nb, rows, m = broadcast_ops.shape[1:]
    pairs = owner_list.shape[1]
    half = rows // 2
    core = sector % 2
    swap_core = [(i, i ^ 1) for i in range(n_sector)]
    swap_side = [(i, (i + 2) % n_sector) for i in range(n_sector)]
    order = ring_order(n_owner)
    up = [(order[i], order[(i + 1) % n_owner]) for i in range(n_owner)]
    down = [(b, a) for a, b in up]
    if half % 32 == 0:
        lanes = ((1, 0, half // 2), (-1, half // 2, half // 2))
    else:
        lanes = ((1, 0, half),)
    static = dict(m=m, nb=nb, half=half, lanes=lanes, n_owner=n_owner, pairs=pairs, sent=min(pairs, CAP + 1))

    shared = broadcast_ops[0]
    theirs = lax.dynamic_slice_in_dim(shared, (1 - core) * half, half, 1).astype(BF16)
    mine = lax.dynamic_slice_in_dim(shared, core * half, half, 1).astype(BF16)
    arrived = lax.ppermute(theirs, "sector", swap_core)
    res_own = resident_ops[0, 0].astype(BF16)
    w_own = integrals[0, 0]
    w_other = lax.ppermute(w_own, "sector", swap_core)
    res_other = lax.ppermute(res_own, "sector", swap_core)
    xs = [jnp.stack([mine[:, a : a + n], arrived[:, a : a + n]]) for _, a, n in lanes]
    q = jnp.where(owner % 2 == 0, owner // 2, n_owner - 1 - owner // 2)
    common = {
        "ids": jnp.stack([sector // 2, core, q]).astype(jnp.int32),
        "owners": owner_list,
        "w0": w_own,
        "w1": w_other,
    }
    res = (res_own, res_other)
    out, kept, crossed, swapped = None, None, None, None
    for step in range(n_owner + 2):
        compute = step if step < n_owner else None
        finish = step - 1 if 1 <= step <= n_owner else None
        place = step - 2 if step >= 2 else None
        later = xs
        if step < n_owner - 1:
            later = [
                lax.ppermute(x, "owner", up if turn == 1 else down) for x, (turn, _, _) in zip(xs, lanes, strict=True)
            ]
        got = step_call(static, compute, finish, place, common, xs, res, kept, crossed, swapped, out)
        if compute is not None:
            kept, crossed = got["kept"], lax.ppermute(got["send"], "sector", swap_side)
        if finish is not None:
            swapped = lax.ppermute(got["swap_out"], "sector", swap_core)
        if "out" in got:
            out = got["out"]
        xs = later
    return out[None, None]


def solution(mesh):
    in_specs = (
        P("sector", None, "owner", None),
        P("sector", "owner", None, None),
        P("sector", "owner", None, None),
        P("owner", None),
    )
    out_specs = P("sector", "owner", None, None, None)
    return jax.shard_map(shards, mesh=mesh, in_specs=in_specs, out_specs=out_specs, check_vma=False)
```

time: 369 us -> 127 us (0.34)
  waiting for transfers between devices: 251 us -> 54.5 us
  matrix products: 73.6 us -> 0 us
  Pallas kernels: 0 us -> 41 us
  starting transfers between devices: 0.04 us -> 26.7 us
  local copies, waits for them, and re-layouts: 20.7 us -> 1.77 us
  between operations: 13.4 us -> 0.36 us
  other arithmetic: 10.2 us -> 2.71 us
    all_gather x1 -> x0, waiting for transfers between devices: 126 us -> none  [shards(): lax.all_gather(shared.astype(jnp.bfloat16), 'owner', axis=1, tiled=True)]
    reduce_scatter x1 -> x0, waiting for transfers between devices: 124 us -> none  [shards(): lax.psum_scatter(jnp.einsum('jk,kmn->jmn', chosen, products, precision=hi...]
    dot_general x3 -> x0, matrix products: 73.6 us -> none  [the longest x1 41.2 us: shards(): jnp.einsum('jk,kmn->jmn', chosen, products, precision=highest)]
    ppermute x0 -> x33, waiting for transfers between devices: none -> 54.5 us  [the longest x8 35.5 us: shards(): lax.ppermute(got['send'], 'sector', swap_side)]
    pallas_call x0 -> x10, Pallas kernels: none -> 41 us  [step_call(): pl.pallas_call(functools.partial(step_kernel, cfg), in_specs=specs, out_s...]
    ppermute x0 -> x33, starting transfers between devices: none -> 26.7 us  [the longest x14 15.2 us: shards(): lax.ppermute(x, 'owner', up if turn == 1 else down)]
    convert_element_type x1, local copies, waits for them, and re-layouts: 20.6 us -> 1.69 us  [shards(): mine = lax.dynamic_slice_in_dim(shared, core * half, half, 1).astype(BF16)]
    broadcast_in_dim x1 -> x0, other arithmetic: 6.63 us -> none  [shards(): return result[None, None]]
  transfers between devices with their start and end apart: 2 -> 33, of which waited for: 2 -> 19; matrix products, arithmetic and copies ran while one was open for 0% -> 2% of each run, Pallas kernels for 0% -> 26%
where the time goes in v1:
time: 127 us
  waiting for transfers between devices  54.5 us (43%)
  Pallas kernels  41 us (32%)
  starting transfers between devices  26.7 us (21%)
  other arithmetic  2.71 us (2%)
  local copies, waits for them, and re-layouts  1.77 us (1%)
    pallas_call x10, Pallas kernels, step_call(): pl.pallas_call(functools.partial(step_kernel, cfg), in_specs=specs, out_s...  41 us
    ppermute x8, waiting for transfers between devices, shards(): lax.ppermute(got['send'], 'sector', swap_side)  35.5 us
    ppermute x14, starting transfers between devices, shards(): lax.ppermute(x, 'owner', up if turn == 1 else down)  15.2 us
    ppermute x14, waiting for transfers between devices, shards(): lax.ppermute(x, 'owner', up if turn == 1 else down)  12.2 us
    ppermute x8, starting transfers between devices, shards(): lax.ppermute(got['send'], 'sector', swap_side)  10.7 us
    ppermute x8, waiting for transfers between devices, shards(): swapped = lax.ppermute(got['swap_out'], 'sector', swap_core)  3.07 us
    ppermute x1, waiting for transfers between devices, shards(): arrived = lax.ppermute(theirs, 'sector', swap_core)  2.68 us
  transfers between devices with their start and end apart: 33, of which 19 were waited for; matrix products, arithmetic and copies ran while one was open for 2% of the time, Pallas kernels for 26%

profile of v1, /device:TPU:0, one launch (start us, length us, event | category | flops | bytes accessed | tf_op | source)
XLA Modules:
  0.0 127.1 jit_solution(10133270523998403223)
XLA Ops:
  0.0 2.5 %convert_bitcast_fusion.refs_6_ = bf16[1024,1024]{1,0:T(8,128)(2,1)S(1)} fusion(f32[1,1,1024,1024]{3,2,1,0:T(8,128)} %param.5), kind=kLoop, calls=%fused_computation | loop fusion | flops 1048576 | bytes 6291456 | tf_op jit(solution)/shard_map/convert_element_type | solution.py:236
  3.1 1.7 %fusion = (bf16[4,64,1024]{2,1,0:T(8,128)(2,1)S(1)}, bf16[4,64,1024]{2,1,0:T(8,128)(2,1)S(1)}) fusion(f32[1,4,128,1024]{3,2,1,0:T(8,128)} %param.4, s32[]{:T(128)S(6)} %select_n.33, s32[]{:T(128)S(6)} %select_n.34), kind=kLoop, calls=%fused_computation.3 | loop fusion | bytes 2097160 | tf_op jit(solution)/shard_map/convert_element_type | solution.py:234
  4.9 2.7 %collective-permute-done.1 = bf16[4,64,1024]{2,1,0:T(8,128)(2,1)S(1)} collective-permute-done((bf16[4,64,1024]{2,1,0:T(8,128)(2,1)S(1)}, bf16[4,64,1024]{2,1,0:T(8,128)(2,1)S(1)}, u32[]{:S(2)}, u32[]{:S(2)}) %collective-permute-start.1) | collective-permute-done | bytes 524320 | tf_op jit(solution)/shard_map/ppermute | solution.py:235
  7.7 2.9 %collective-permute-start.9 = (bf16[2,4,32,1024]{3,2,1,0:T(8,128)(2,1)S(1)}, bf16[2,4,32,1024]{3,2,1,0:T(8,128)(2,1)}, u32[]{:S(2)}, u32[]{:S(2)}) collective-permute-start(bf16[2,4,32,1024]{3,2,1,0:T(8,128)(2,1)S(1)} %pad_maximum_fusion.1.refs_5_), channel_id=1, source_target_pairs={{2,0},{4,2},{6,4},{7,6},{5,7},{3,5},{1,3},{0,1},{10,8},{12,10},{14... | collective-permute-start | bytes 1572872 | tf_op jit(solution)/shard_map/ppermute | solution.py:257
  12.0 4.6 %shard_map.46 = (bf16[3,64,1024]{2,1,0:T(8,128)(2,1)S(1)}, f32[3,64,1024]{2,1,0:T(8,128)S(1)}) custom-call(s32[3]{0:T(128)S(1)} %pad_add_fusion.refs_0_, s32[1,4]{1,0:T(1,128)S(1)} %copy-done.1, f32[4,4]{1,0:T(4,128)S(1)} %bitcast.20, f32[4,4]{1,0:T(4,128)S(1)} %collective-permute-done.refs_3_, bf16[2,4,32,1024]{3,2,1,0:T(8,128)(2,1)S(1)} %pad_maximum_fusion.refs_4_, ...), custom_call_target="tpu_custom_call" | custom-call | flops 1073741824 | bytes 8388608 | tf_op jit(solution)/shard_map/pallas_call | solution.py:199
  16.6 2.0 %collective-permute-start.17 = (bf16[3,64,1024]{2,1,0:T(8,128)(2,1)S(1)}, bf16[3,64,1024]{2,1,0:T(8,128)(2,1)S(1)}, u32[]{:S(2)}, u32[]{:S(2)}) collective-permute-start(bf16[3,64,1024]{2,1,0:T(8,128)(2,1)S(1)} %get-tuple-element.38), channel_id=1, source_target_pairs={{0,16},{8,24},{16,0},{24,8},{1,17},{9,25},{17,1},{25,9},{2,18},{10... | collective-permute-start | bytes 1179656 | tf_op jit(solution)/shard_map/ppermute | solution.py:261
  18.6 4.4 %collective-permute-done.9.refs_5_ = bf16[2,4,32,1024]{3,2,1,0:T(8,128)(2,1)} collective-permute-done((bf16[2,4,32,1024]{3,2,1,0:T(8,128)(2,1)S(1)}, bf16[2,4,32,1024]{3,2,1,0:T(8,128)(2,1)}, u32[]{:S(2)}, u32[]{:S(2)}) %collective-permute-start.9) | collective-permute-done | bytes 524320 | tf_op jit(solution)/shard_map/ppermute | solution.py:257
  23.0 1.7 %collective-permute-start.10 = (bf16[2,4,32,1024]{3,2,1,0:T(8,128)(2,1)}, bf16[2,4,32,1024]{3,2,1,0:T(8,128)(2,1)S(1)}, u32[]{:S(2)}, u32[]{:S(2)}) collective-permute-start(bf16[2,4,32,1024]{3,2,1,0:T(8,128)(2,1)} %collective-permute-done.9.refs_5_), channel_id=1, source_target_pairs={{2,0},{4,2},{6,4},{7,6},{5,7},{3,5},{1,3},{0,1},{10,8},{12,10},{14... | collective-permute-start | bytes 1572872 | tf_op jit(solution)/shard_map/ppermute | solution.py:257
  25.1 3.0 %collective-permute-done.17.refs_9_ = bf16[3,64,1024]{2,1,0:T(8,128)(2,1)S(1)} collective-permute-done((bf16[3,64,1024]{2,1,0:T(8,128)(2,1)S(1)}, bf16[3,64,1024]{2,1,0:T(8,128)(2,1)S(1)}, u32[]{:S(2)}, u32[]{:S(2)}) %collective-permute-start.17) | collective-permute-done | bytes 393248 | tf_op jit(solution)/shard_map/ppermute | solution.py:261
  28.1 5.2 %shard_map.47 = (bf16[3,64,1024]{2,1,0:T(8,128)(2,1)S(1)}, f32[3,64,1024]{2,1,0:T(8,128)S(1)}, bf16[2,64,1024]{2,1,0:T(8,128)(2,1)S(1)}, f32[2,1024,1024]{2,1,0:T(8,128)}) custom-call(s32[3]{0:T(128)S(1)} %pad_add_fusion.refs_0_, s32[1,4]{1,0:T(1,128)S(1)} %copy-done.1, f32[4,4]{1,0:T(4,128)S(1)} %bitcast.21, f32[4,4]{1,0:T(4,128)S(1)} %collective-permute-done.refs_3_, ...), custom_call_target="tpu_custom_call" | custom-call | flops 1073741824 | bytes 8388608 | tf_op jit(solution)/shard_map/pallas_call | solution.py:199
  33.3 1.8 %collective-permute-start.18 = (bf16[3,64,1024]{2,1,0:T(8,128)(2,1)S(1)}, bf16[3,64,1024]{2,1,0:T(8,128)(2,1)S(1)}, u32[]{:S(2)}, u32[]{:S(2)}) collective-permute-start(bf16[3,64,1024]{2,1,0:T(8,128)(2,1)S(1)} %get-tuple-element.40), channel_id=1, source_target_pairs={{0,16},{8,24},{16,0},{24,8},{1,17},{9,25},{17,1},{25,9},{2,18},{10... | collective-permute-start | bytes 1179656 | tf_op jit(solution)/shard_map/ppermute | solution.py:261
  35.1 1.6 %collective-permute-done.10.refs_5_ = bf16[2,4,32,1024]{3,2,1,0:T(8,128)(2,1)S(1)} collective-permute-done((bf16[2,4,32,1024]{3,2,1,0:T(8,128)(2,1)}, bf16[2,4,32,1024]{3,2,1,0:T(8,128)(2,1)S(1)}, u32[]{:S(2)}, u32[]{:S(2)}) %collective-permute-start.10) | collective-permute-done | bytes 524320 | tf_op jit(solution)/shard_map/ppermute | solution.py:257
  38.7 5.3 %collective-permute-done.18.refs_9_ = bf16[3,64,1024]{2,1,0:T(8,128)(2,1)S(1)} collective-permute-done((bf16[3,64,1024]{2,1,0:T(8,128)(2,1)S(1)}, bf16[3,64,1024]{2,1,0:T(8,128)(2,1)S(1)}, u32[]{:S(2)}, u32[]{:S(2)}) %collective-permute-start.18) | collective-permute-done | bytes 393248 | tf_op jit(solution)/shard_map/ppermute | solution.py:261
  44.0 4.7 %shard_map.48 = (bf16[3,64,1024]{2,1,0:T(8,128)(2,1)S(1)}, f32[3,64,1024]{2,1,0:T(8,128)S(1)}, bf16[2,64,1024]{2,1,0:T(8,128)(2,1)S(1)}, f32[2,1024,1024]{2,1,0:T(8,128)}) custom-call(s32[3]{0:T(128)S(1)} %pad_add_fusion.refs_0_, s32[1,4]{1,0:T(1,128)S(1)} %copy-done.1, f32[4,4]{1,0:T(4,128)S(1)} %bitcast.22, ...), custom_call_target="tpu_custom_call", output_to_operand_aliasing={{3}: (11, {})} | custom-call | flops 1073741824 | bytes 8388608 | tf_op jit(solution)/shard_map/pallas_call | solution.py:199
  48.7 1.6 %collective-permute-start.20 = (bf16[3,64,1024]{2,1,0:T(8,128)(2,1)S(1)}, bf16[3,64,1024]{2,1,0:T(8,128)(2,1)S(1)}, u32[]{:S(2)}, u32[]{:S(2)}) collective-permute-start(bf16[3,64,1024]{2,1,0:T(8,128)(2,1)S(1)} %get-tuple-element.44), channel_id=1, source_target_pairs={{0,16},{8,24},{16,0},{24,8},{1,17},{9,25},{17,1},{25,9},{2,18},{10... | collective-permute-start | bytes 1179656 | tf_op jit(solution)/shard_map/ppermute | solution.py:261
  52.3 6.2 %collective-permute-done.20.refs_9_ = bf16[3,64,1024]{2,1,0:T(8,128)(2,1)S(1)} collective-permute-done((bf16[3,64,1024]{2,1,0:T(8,128)(2,1)S(1)}, bf16[3,64,1024]{2,1,0:T(8,128)(2,1)S(1)}, u32[]{:S(2)}, u32[]{:S(2)}) %collective-permute-start.20) | collective-permute-done | bytes 393248 | tf_op jit(solution)/shard_map/ppermute | solution.py:261
  58.4 4.7 %shard_map.49 = (bf16[3,64,1024]{2,1,0:T(8,128)(2,1)S(1)}, f32[3,64,1024]{2,1,0:T(8,128)S(1)}, bf16[2,64,1024]{2,1,0:T(8,128)(2,1)S(1)}, f32[2,1024,1024]{2,1,0:T(8,128)}) custom-call(s32[3]{0:T(128)S(1)} %pad_add_fusion.refs_0_, s32[1,4]{1,0:T(1,128)S(1)} %copy-done.1, f32[4,4]{1,0:T(4,128)S(1)} %bitcast.23, ...), custom_call_target="tpu_custom_call", output_to_operand_aliasing={{3}: (11, {})} | custom-call | flops 1073741824 | bytes 8388608 | tf_op jit(solution)/shard_map/pallas_call | solution.py:199
  64.6 1.5 %collective-permute-start.13 = (bf16[2,4,32,1024]{3,2,1,0:T(8,128)(2,1)S(1)}, bf16[2,4,32,1024]{3,2,1,0:T(8,128)(2,1)S(1)}, u32[]{:S(2)}, u32[]{:S(2)}) collective-permute-start(bf16[2,4,32,1024]{3,2,1,0:T(8,128)(2,1)S(1)} %collective-permute-done.12.refs_5_), channel_id=1, source_target_pairs={{2,0},{4,2},{6,4},{7,6},{5,7},{3,5},{1,3},{0,1},{10,8},{12,10},{14... | collective-permute-start | bytes 1572872 | tf_op jit(solution)/shard_map/ppermute | solution.py:257
  66.6 5.3 %collective-permute-done.22.refs_9_ = bf16[3,64,1024]{2,1,0:T(8,128)(2,1)S(1)} collective-permute-done((bf16[3,64,1024]{2,1,0:T(8,128)(2,1)S(1)}, bf16[3,64,1024]{2,1,0:T(8,128)(2,1)S(1)}, u32[]{:S(2)}, u32[]{:S(2)}) %collective-permute-start.22) | collective-permute-done | bytes 393248 | tf_op jit(solution)/shard_map/ppermute | solution.py:261
  72.0 4.7 %shard_map.50 = (bf16[3,64,1024]{2,1,0:T(8,128)(2,1)S(1)}, f32[3,64,1024]{2,1,0:T(8,128)S(1)}, bf16[2,64,1024]{2,1,0:T(8,128)(2,1)S(1)}, f32[2,1024,1024]{2,1,0:T(8,128)}) custom-call(s32[3]{0:T(128)S(1)} %pad_add_fusion.refs_0_, s32[1,4]{1,0:T(1,128)S(1)} %copy-done.1, f32[4,4]{1,0:T(4,128)S(1)} %bitcast.24, ...), custom_call_target="tpu_custom_call", output_to_operand_aliasing={{3}: (11, {})} | custom-call | flops 1073741824 | bytes 8388608 | tf_op jit(solution)/shard_map/pallas_call | solution.py:199
  80.8 3.8 %collective-permute-done.24.refs_9_ = bf16[3,64,1024]{2,1,0:T(8,128)(2,1)S(1)} collective-permute-done((bf16[3,64,1024]{2,1,0:T(8,128)(2,1)S(1)}, bf16[3,64,1024]{2,1,0:T(8,128)(2,1)S(1)}, u32[]{:S(2)}, u32[]{:S(2)}) %collective-permute-start.24) | collective-permute-done | bytes 393248 | tf_op jit(solution)/shard_map/ppermute | solution.py:261
  84.6 4.7 %shard_map.51 = (bf16[3,64,1024]{2,1,0:T(8,128)(2,1)S(1)}, f32[3,64,1024]{2,1,0:T(8,128)S(1)}, bf16[2,64,1024]{2,1,0:T(8,128)(2,1)S(1)}, f32[2,1024,1024]{2,1,0:T(8,128)}) custom-call(s32[3]{0:T(128)S(1)} %pad_add_fusion.refs_0_, s32[1,4]{1,0:T(1,128)S(1)} %copy-done.1, f32[4,4]{1,0:T(4,128)S(1)} %bitcast.25, ...), custom_call_target="tpu_custom_call", output_to_operand_aliasing={{3}: (11, {})} | custom-call | flops 1073741824 | bytes 8388608 | tf_op jit(solution)/shard_map/pallas_call | solution.py:199
  90.3 1.9 %collective-permute-done.14.refs_5_ = bf16[2,4,32,1024]{3,2,1,0:T(8,128)(2,1)S(1)} collective-permute-done((bf16[2,4,32,1024]{3,2,1,0:T(8,128)(2,1)S(1)}, bf16[2,4,32,1024]{3,2,1,0:T(8,128)(2,1)S(1)}, u32[]{:S(2)}, u32[]{:S(2)}) %collective-permute-start.14) | collective-permute-done | bytes 524320 | tf_op jit(solution)/shard_map/ppermute | solution.py:257
  94.2 2.9 %collective-permute-done.26.refs_9_ = bf16[3,64,1024]{2,1,0:T(8,128)(2,1)S(1)} collective-permute-done((bf16[3,64,1024]{2,1,0:T(8,128)(2,1)S(1)}, bf16[3,64,1024]{2,1,0:T(8,128)(2,1)S(1)}, u32[]{:S(2)}, u32[]{:S(2)}) %collective-permute-start.26) | collective-permute-done | bytes 393248 | tf_op jit(solution)/shard_map/ppermute | solution.py:261
  97.1 4.7 %shard_map.52 = (bf16[3,64,1024]{2,1,0:T(8,128)(2,1)S(1)}, f32[3,64,1024]{2,1,0:T(8,128)S(1)}, bf16[2,64,1024]{2,1,0:T(8,128)(2,1)S(1)}, f32[2,1024,1024]{2,1,0:T(8,128)}) custom-call(s32[3]{0:T(128)S(1)} %pad_add_fusion.refs_0_, s32[1,4]{1,0:T(1,128)S(1)} %copy-done.1, f32[4,4]{1,0:T(4,128)S(1)} %bitcast.26, ...), custom_call_target="tpu_custom_call", output_to_operand_aliasing={{3}: (11, {})} | custom-call | flops 1073741824 | bytes 8388608 | tf_op jit(solution)/shard_map/pallas_call | solution.py:199
  102.8 1.9 %collective-permute-done.15.refs_5_ = bf16[2,4,32,1024]{3,2,1,0:T(8,128)(2,1)S(1)} collective-permute-done((bf16[2,4,32,1024]{3,2,1,0:T(8,128)(2,1)S(1)}, bf16[2,4,32,1024]{3,2,1,0:T(8,128)(2,1)S(1)}, u32[]{:S(2)}, u32[]{:S(2)}) %collective-permute-start.15) | collective-permute-done | bytes 524320 | tf_op jit(solution)/shard_map/ppermute | solution.py:257
  105.9 3.8 %collective-permute-done.28.refs_9_ = bf16[3,64,1024]{2,1,0:T(8,128)(2,1)S(1)} collective-permute-done((bf16[3,64,1024]{2,1,0:T(8,128)(2,1)S(1)}, bf16[3,64,1024]{2,1,0:T(8,128)(2,1)S(1)}, u32[]{:S(2)}, u32[]{:S(2)}) %collective-permute-start.28) | collective-permute-done | bytes 393248 | tf_op jit(solution)/shard_map/ppermute | solution.py:261
  109.7 4.7 %shard_map.53 = (bf16[3,64,1024]{2,1,0:T(8,128)(2,1)S(1)}, f32[3,64,1024]{2,1,0:T(8,128)S(1)}, bf16[2,64,1024]{2,1,0:T(8,128)(2,1)S(1)}, f32[2,1024,1024]{2,1,0:T(8,128)}) custom-call(s32[3]{0:T(128)S(1)} %pad_add_fusion.refs_0_, s32[1,4]{1,0:T(1,128)S(1)} %copy-done.1, f32[4,4]{1,0:T(4,128)S(1)} %bitcast.27, ...), custom_call_target="tpu_custom_call", output_to_operand_aliasing={{3}: (11, {})} | custom-call | flops 1073741824 | bytes 8388608 | tf_op jit(solution)/shard_map/pallas_call | solution.py:199
  115.3 1.5 %collective-permute-done.31.refs_4_ = bf16[2,64,1024]{2,1,0:T(8,128)(2,1)S(1)} collective-permute-done((bf16[2,64,1024]{2,1,0:T(8,128)(2,1)S(1)}, bf16[2,64,1024]{2,1,0:T(8,128)(2,1)S(1)}, u32[]{:S(2)}, u32[]{:S(2)}) %collective-permute-start.31) | collective-permute-done | bytes 262176 | tf_op jit(solution)/shard_map/ppermute | solution.py:263
  116.9 5.3 %collective-permute-done.30.refs_3_ = bf16[3,64,1024]{2,1,0:T(8,128)(2,1)S(1)} collective-permute-done((bf16[3,64,1024]{2,1,0:T(8,128)(2,1)S(1)}, bf16[3,64,1024]{2,1,0:T(8,128)(2,1)S(1)}, u32[]{:S(2)}, u32[]{:S(2)}) %collective-permute-start.30) | collective-permute-done | bytes 393248 | tf_op jit(solution)/shard_map/ppermute | solution.py:261
  122.2 1.6 %shard_map.54 = (bf16[2,64,1024]{2,1,0:T(8,128)(2,1)S(1)}, f32[2,1024,1024]{2,1,0:T(8,128)}) custom-call(s32[3]{0:T(128)S(1)} %pad_add_fusion.refs_0_, s32[1,4]{1,0:T(1,128)S(1)} %copy-done.1, f32[3,64,1024]{2,1,0:T(8,128)S(1)} %get-tuple-element.63.refs_2_, ...), custom_call_target="tpu_custom_call", output_to_operand_aliasing={{1}: (5, {})} | custom-call | flops 131072 | bytes 8388608 | tf_op jit(solution)/shard_map/pallas_call | solution.py:199
  123.9 1.5 %collective-permute-done.32.refs_2_ = bf16[2,64,1024]{2,1,0:T(8,128)(2,1)S(1)} collective-permute-done((bf16[2,64,1024]{2,1,0:T(8,128)(2,1)S(1)}, bf16[2,64,1024]{2,1,0:T(8,128)(2,1)S(1)}, u32[]{:S(2)}, u32[]{:S(2)}) %collective-permute-start.32) | collective-permute-done | bytes 262176 | tf_op jit(solution)/shard_map/ppermute | solution.py:263
  (55 shorter events, 20.4 us)
Async XLA Ops:
  2.5 9.4 %collective-permute-start.16 = (bf16[1024,1024]{1,0:T(8,128)(2,1)S(1)}, bf16[1024,1024]{1,0:T(8,128)(2,1)}, u32[]{:S(2)}, u32[]{:S(2)}) collective-permute-start(bf16[1024,1024]{1,0:T(8,128)(2,1)S(1)} %convert_bitcast_fusion.refs_6_), channel_id=1, source_target_pairs={{0,8},{8,0},{16,24},{24,16},{1,9},{9,1},{17,25},{25,17},{2,10},{10... | collective-permute-start | bytes 6291464 | tf_op jit(solution)/shard_map/ppermute | solution.py:239
  4.8 2.8 %collective-permute-start.1 = (bf16[4,64,1024]{2,1,0:T(8,128)(2,1)S(1)}, bf16[4,64,1024]{2,1,0:T(8,128)(2,1)S(1)}, u32[]{:S(2)}, u32[]{:S(2)}) collective-permute-start(bf16[4,64,1024]{2,1,0:T(8,128)(2,1)S(1)} %get-tuple-element.70), channel_id=1, source_target_pairs={{0,8},{8,0},{16,24},{24,16},{1,9},{9,1},{17,25},{25,17},{2,10},{10... | collective-permute-start | bytes 1572872 | tf_op jit(solution)/shard_map/ppermute | solution.py:235
  7.7 15.3 %collective-permute-start.9 = (bf16[2,4,32,1024]{3,2,1,0:T(8,128)(2,1)S(1)}, bf16[2,4,32,1024]{3,2,1,0:T(8,128)(2,1)}, u32[]{:S(2)}, u32[]{:S(2)}) collective-permute-start(bf16[2,4,32,1024]{3,2,1,0:T(8,128)(2,1)S(1)} %pad_maximum_fusion.1.refs_5_), channel_id=1, source_target_pairs={{2,0},{4,2},{6,4},{7,6},{5,7},{3,5},{1,3},{0,1},{10,8},{12,10},{14... | collective-permute-start | bytes 1572872 | tf_op jit(solution)/shard_map/ppermute | solution.py:257
  10.7 14.0 %collective-permute-start.2 = (bf16[2,4,32,1024]{3,2,1,0:T(8,128)(2,1)S(1)}, bf16[2,4,32,1024]{3,2,1,0:T(8,128)(2,1)}, u32[]{:S(2)}, u32[]{:S(2)}) collective-permute-start(bf16[2,4,32,1024]{3,2,1,0:T(8,128)(2,1)S(1)} %pad_maximum_fusion.refs_4_), channel_id=1, source_target_pairs={{0,2},{2,4},{4,6},{6,7},{7,5},{5,3},{3,1},{1,0},{8,10},{10,12},{12... | collective-permute-start | bytes 1572872 | tf_op jit(solution)/shard_map/ppermute | solution.py:257
  16.6 11.5 %collective-permute-start.17 = (bf16[3,64,1024]{2,1,0:T(8,128)(2,1)S(1)}, bf16[3,64,1024]{2,1,0:T(8,128)(2,1)S(1)}, u32[]{:S(2)}, u32[]{:S(2)}) collective-permute-start(bf16[3,64,1024]{2,1,0:T(8,128)(2,1)S(1)} %get-tuple-element.38), channel_id=1, source_target_pairs={{0,16},{8,24},{16,0},{24,8},{1,17},{9,25},{17,1},{25,9},{2,18},{10... | collective-permute-start | bytes 1179656 | tf_op jit(solution)/shard_map/ppermute | solution.py:261
  23.0 13.7 %collective-permute-start.10 = (bf16[2,4,32,1024]{3,2,1,0:T(8,128)(2,1)}, bf16[2,4,32,1024]{3,2,1,0:T(8,128)(2,1)S(1)}, u32[]{:S(2)}, u32[]{:S(2)}) collective-permute-start(bf16[2,4,32,1024]{3,2,1,0:T(8,128)(2,1)} %collective-permute-done.9.refs_5_), channel_id=1, source_target_pairs={{2,0},{4,2},{6,4},{7,6},{5,7},{3,5},{1,3},{0,1},{10,8},{12,10},{14... | collective-permute-start | bytes 1572872 | tf_op jit(solution)/shard_map/ppermute | solution.py:257
  24.7 13.3 %collective-permute-start.3 = (bf16[2,4,32,1024]{3,2,1,0:T(8,128)(2,1)}, bf16[2,4,32,1024]{3,2,1,0:T(8,128)(2,1)S(1)}, u32[]{:S(2)}, u32[]{:S(2)}) collective-permute-start(bf16[2,4,32,1024]{3,2,1,0:T(8,128)(2,1)} %collective-permute-done.2.refs_4_), channel_id=1, source_target_pairs={{0,2},{2,4},{4,6},{6,7},{7,5},{5,3},{3,1},{1,0},{8,10},{10,12},{12... | collective-permute-start | bytes 1572872 | tf_op jit(solution)/shard_map/ppermute | solution.py:257
  33.3 10.7 %collective-permute-start.18 = (bf16[3,64,1024]{2,1,0:T(8,128)(2,1)S(1)}, bf16[3,64,1024]{2,1,0:T(8,128)(2,1)S(1)}, u32[]{:S(2)}, u32[]{:S(2)}) collective-permute-start(bf16[3,64,1024]{2,1,0:T(8,128)(2,1)S(1)} %get-tuple-element.40), channel_id=1, source_target_pairs={{0,16},{8,24},{16,0},{24,8},{1,17},{9,25},{17,1},{25,9},{2,18},{10... | collective-permute-start | bytes 1179656 | tf_op jit(solution)/shard_map/ppermute | solution.py:261
  35.1 3.6 %collective-permute-start.19 = (bf16[2,64,1024]{2,1,0:T(8,128)(2,1)S(1)}, bf16[2,64,1024]{2,1,0:T(8,128)(2,1)S(1)}, u32[]{:S(2)}, u32[]{:S(2)}) collective-permute-start(bf16[2,64,1024]{2,1,0:T(8,128)(2,1)S(1)} %get-tuple-element.41), channel_id=1, source_target_pairs={{0,8},{8,0},{16,24},{24,16},{1,9},{9,1},{17,25},{25,17},{2,10},{10... | collective-permute-start | bytes 786440 | tf_op jit(solution)/shard_map/ppermute | solution.py:263
  36.7 13.6 %collective-permute-start.11 = (bf16[2,4,32,1024]{3,2,1,0:T(8,128)(2,1)S(1)}, bf16[2,4,32,1024]{3,2,1,0:T(8,128)(2,1)S(1)}, u32[]{:S(2)}, u32[]{:S(2)}) collective-permute-start(bf16[2,4,32,1024]{3,2,1,0:T(8,128)(2,1)S(1)} %collective-permute-done.10.refs_5_), channel_id=1, source_target_pairs={{2,0},{4,2},{6,4},{7,6},{5,7},{3,5},{1,3},{0,1},{10,8},{12,10},{14... | collective-permute-start | bytes 1572872 | tf_op jit(solution)/shard_map/ppermute | solution.py:257
  38.0 13.7 %collective-permute-start.4 = (bf16[2,4,32,1024]{3,2,1,0:T(8,128)(2,1)S(1)}, bf16[2,4,32,1024]{3,2,1,0:T(8,128)(2,1)S(1)}, u32[]{:S(2)}, u32[]{:S(2)}) collective-permute-start(bf16[2,4,32,1024]{3,2,1,0:T(8,128)(2,1)S(1)} %collective-permute-done.3.refs_4_), channel_id=1, source_target_pairs={{0,2},{2,4},{4,6},{6,7},{7,5},{5,3},{3,1},{1,0},{8,10},{10,12},{12... | collective-permute-start | bytes 1572872 | tf_op jit(solution)/shard_map/ppermute | solution.py:257
  48.7 9.8 %collective-permute-start.20 = (bf16[3,64,1024]{2,1,0:T(8,128)(2,1)S(1)}, bf16[3,64,1024]{2,1,0:T(8,128)(2,1)S(1)}, u32[]{:S(2)}, u32[]{:S(2)}) collective-permute-start(bf16[3,64,1024]{2,1,0:T(8,128)(2,1)S(1)} %get-tuple-element.44), channel_id=1, source_target_pairs={{0,16},{8,24},{16,0},{24,8},{1,17},{9,25},{17,1},{25,9},{2,18},{10... | collective-permute-start | bytes 1179656 | tf_op jit(solution)/shard_map/ppermute | solution.py:261
  50.2 2.0 %collective-permute-start.21 = (bf16[2,64,1024]{2,1,0:T(8,128)(2,1)S(1)}, bf16[2,64,1024]{2,1,0:T(8,128)(2,1)S(1)}, u32[]{:S(2)}, u32[]{:S(2)}) collective-permute-start(bf16[2,64,1024]{2,1,0:T(8,128)(2,1)S(1)} %get-tuple-element.45), channel_id=1, source_target_pairs={{0,8},{8,0},{16,24},{24,16},{1,9},{9,1},{17,25},{25,17},{2,10},{10... | collective-permute-start | bytes 786440 | tf_op jit(solution)/shard_map/ppermute | solution.py:263
  50.2 14.3 %collective-permute-start.12 = (bf16[2,4,32,1024]{3,2,1,0:T(8,128)(2,1)S(1)}, bf16[2,4,32,1024]{3,2,1,0:T(8,128)(2,1)S(1)}, u32[]{:S(2)}, u32[]{:S(2)}) collective-permute-start(bf16[2,4,32,1024]{3,2,1,0:T(8,128)(2,1)S(1)} %collective-permute-done.11.refs_5_), channel_id=1, source_target_pairs={{2,0},{4,2},{6,4},{7,6},{5,7},{3,5},{1,3},{0,1},{10,8},{12,10},{14... | collective-permute-start | bytes 1572872 | tf_op jit(solution)/shard_map/ppermute | solution.py:257
  51.7 14.3 %collective-permute-start.5 = (bf16[2,4,32,1024]{3,2,1,0:T(8,128)(2,1)S(1)}, bf16[2,4,32,1024]{3,2,1,0:T(8,128)(2,1)S(1)}, u32[]{:S(2)}, u32[]{:S(2)}) collective-permute-start(bf16[2,4,32,1024]{3,2,1,0:T(8,128)(2,1)S(1)} %collective-permute-done.4.refs_4_), channel_id=1, source_target_pairs={{0,2},{2,4},{4,6},{6,7},{7,5},{5,3},{3,1},{1,0},{8,10},{10,12},{12... | collective-permute-start | bytes 1572872 | tf_op jit(solution)/shard_map/ppermute | solution.py:257
  63.1 8.8 %collective-permute-start.22 = (bf16[3,64,1024]{2,1,0:T(8,128)(2,1)S(1)}, bf16[3,64,1024]{2,1,0:T(8,128)(2,1)S(1)}, u32[]{:S(2)}, u32[]{:S(2)}) collective-permute-start(bf16[3,64,1024]{2,1,0:T(8,128)(2,1)S(1)} %get-tuple-element.48), channel_id=1, source_target_pairs={{0,16},{8,24},{16,0},{24,8},{1,17},{9,25},{17,1},{25,9},{2,18},{10... | collective-permute-start | bytes 1179656 | tf_op jit(solution)/shard_map/ppermute | solution.py:261
  64.4 2.2 %collective-permute-start.23 = (bf16[2,64,1024]{2,1,0:T(8,128)(2,1)S(1)}, bf16[2,64,1024]{2,1,0:T(8,128)(2,1)S(1)}, u32[]{:S(2)}, u32[]{:S(2)}) collective-permute-start(bf16[2,64,1024]{2,1,0:T(8,128)(2,1)S(1)} %get-tuple-element.49), channel_id=1, source_target_pairs={{0,8},{8,0},{16,24},{24,16},{1,9},{9,1},{17,25},{25,17},{2,10},{10... | collective-permute-start | bytes 786440 | tf_op jit(solution)/shard_map/ppermute | solution.py:263
  64.6 14.2 %collective-permute-start.13 = (bf16[2,4,32,1024]{3,2,1,0:T(8,128)(2,1)S(1)}, bf16[2,4,32,1024]{3,2,1,0:T(8,128)(2,1)S(1)}, u32[]{:S(2)}, u32[]{:S(2)}) collective-permute-start(bf16[2,4,32,1024]{3,2,1,0:T(8,128)(2,1)S(1)} %collective-permute-done.12.refs_5_), channel_id=1, source_target_pairs={{2,0},{4,2},{6,4},{7,6},{5,7},{3,5},{1,3},{0,1},{10,8},{12,10},{14... | collective-permute-start | bytes 1572872 | tf_op jit(solution)/shard_map/ppermute | solution.py:257
  66.1 14.2 %collective-permute-start.6 = (bf16[2,4,32,1024]{3,2,1,0:T(8,128)(2,1)S(1)}, bf16[2,4,32,1024]{3,2,1,0:T(8,128)(2,1)S(1)}, u32[]{:S(2)}, u32[]{:S(2)}) collective-permute-start(bf16[2,4,32,1024]{3,2,1,0:T(8,128)(2,1)S(1)} %collective-permute-done.5.refs_4_), channel_id=1, source_target_pairs={{0,2},{2,4},{4,6},{6,7},{7,5},{5,3},{3,1},{1,0},{8,10},{10,12},{12... | collective-permute-start | bytes 1572872 | tf_op jit(solution)/shard_map/ppermute | solution.py:257
  76.7 7.9 %collective-permute-start.24 = (bf16[3,64,1024]{2,1,0:T(8,128)(2,1)S(1)}, bf16[3,64,1024]{2,1,0:T(8,128)(2,1)S(1)}, u32[]{:S(2)}, u32[]{:S(2)}) collective-permute-start(bf16[3,64,1024]{2,1,0:T(8,128)(2,1)S(1)} %get-tuple-element.52), channel_id=1, source_target_pairs={{0,16},{8,24},{16,0},{24,8},{1,17},{9,25},{17,1},{25,9},{2,18},{10... | collective-permute-start | bytes 1179656 | tf_op jit(solution)/shard_map/ppermute | solution.py:261
  77.7 3.1 %collective-permute-start.25 = (bf16[2,64,1024]{2,1,0:T(8,128)(2,1)S(1)}, bf16[2,64,1024]{2,1,0:T(8,128)(2,1)S(1)}, u32[]{:S(2)}, u32[]{:S(2)}) collective-permute-start(bf16[2,64,1024]{2,1,0:T(8,128)(2,1)S(1)} %get-tuple-element.53), channel_id=1, source_target_pairs={{0,8},{8,0},{16,24},{24,16},{1,9},{9,1},{17,25},{25,17},{2,10},{10... | collective-permute-start | bytes 786440 | tf_op jit(solution)/shard_map/ppermute | solution.py:263
  78.8 13.4 %collective-permute-start.14 = (bf16[2,4,32,1024]{3,2,1,0:T(8,128)(2,1)S(1)}, bf16[2,4,32,1024]{3,2,1,0:T(8,128)(2,1)S(1)}, u32[]{:S(2)}, u32[]{:S(2)}) collective-permute-start(bf16[2,4,32,1024]{3,2,1,0:T(8,128)(2,1)S(1)} %collective-permute-done.13.refs_5_), channel_id=1, source_target_pairs={{2,0},{4,2},{6,4},{7,6},{5,7},{3,5},{1,3},{0,1},{10,8},{12,10},{14... | collective-permute-start | bytes 1572872 | tf_op jit(solution)/shard_map/ppermute | solution.py:257
  80.3 13.4 %collective-permute-start.7 = (bf16[2,4,32,1024]{3,2,1,0:T(8,128)(2,1)S(1)}, bf16[2,4,32,1024]{3,2,1,0:T(8,128)(2,1)S(1)}, u32[]{:S(2)}, u32[]{:S(2)}) collective-permute-start(bf16[2,4,32,1024]{3,2,1,0:T(8,128)(2,1)S(1)} %collective-permute-done.6.refs_4_), channel_id=1, source_target_pairs={{0,2},{2,4},{4,6},{6,7},{7,5},{5,3},{3,1},{1,0},{8,10},{10,12},{12... | collective-permute-start | bytes 1572872 | tf_op jit(solution)/shard_map/ppermute | solution.py:257
  89.3 7.8 %collective-permute-start.26 = (bf16[3,64,1024]{2,1,0:T(8,128)(2,1)S(1)}, bf16[3,64,1024]{2,1,0:T(8,128)(2,1)S(1)}, u32[]{:S(2)}, u32[]{:S(2)}) collective-permute-start(bf16[3,64,1024]{2,1,0:T(8,128)(2,1)S(1)} %get-tuple-element.56), channel_id=1, source_target_pairs={{0,16},{8,24},{16,0},{24,8},{1,17},{9,25},{17,1},{25,9},{2,18},{10... | collective-permute-start | bytes 1179656 | tf_op jit(solution)/shard_map/ppermute | solution.py:261
  90.3 3.9 %collective-permute-start.27 = (bf16[2,64,1024]{2,1,0:T(8,128)(2,1)S(1)}, bf16[2,64,1024]{2,1,0:T(8,128)(2,1)S(1)}, u32[]{:S(2)}, u32[]{:S(2)}) collective-permute-start(bf16[2,64,1024]{2,1,0:T(8,128)(2,1)S(1)} %get-tuple-element.57), channel_id=1, source_target_pairs={{0,8},{8,0},{16,24},{24,16},{1,9},{9,1},{17,25},{25,17},{2,10},{10... | collective-permute-start | bytes 786440 | tf_op jit(solution)/shard_map/ppermute | solution.py:263
  92.2 12.5 %collective-permute-start.15 = (bf16[2,4,32,1024]{3,2,1,0:T(8,128)(2,1)S(1)}, bf16[2,4,32,1024]{3,2,1,0:T(8,128)(2,1)S(1)}, u32[]{:S(2)}, u32[]{:S(2)}) collective-permute-start(bf16[2,4,32,1024]{3,2,1,0:T(8,128)(2,1)S(1)} %collective-permute-done.14.refs_5_), channel_id=1, source_target_pairs={{2,0},{4,2},{6,4},{7,6},{5,7},{3,5},{1,3},{0,1},{10,8},{12,10},{14... | collective-permute-start | bytes 1572872 | tf_op jit(solution)/shard_map/ppermute | solution.py:257
  93.7 12.2 %collective-permute-start.8 = (bf16[2,4,32,1024]{3,2,1,0:T(8,128)(2,1)S(1)}, bf16[2,4,32,1024]{3,2,1,0:T(8,128)(2,1)S(1)}, u32[]{:S(2)}, u32[]{:S(2)}) collective-permute-start(bf16[2,4,32,1024]{3,2,1,0:T(8,128)(2,1)S(1)} %collective-permute-done.7.refs_4_), channel_id=1, source_target_pairs={{0,2},{2,4},{4,6},{6,7},{7,5},{5,3},{3,1},{1,0},{8,10},{10,12},{12... | collective-permute-start | bytes 1572872 | tf_op jit(solution)/shard_map/ppermute | solution.py:257
  101.8 7.8 %collective-permute-start.28 = (bf16[3,64,1024]{2,1,0:T(8,128)(2,1)S(1)}, bf16[3,64,1024]{2,1,0:T(8,128)(2,1)S(1)}, u32[]{:S(2)}, u32[]{:S(2)}) collective-permute-start(bf16[3,64,1024]{2,1,0:T(8,128)(2,1)S(1)} %get-tuple-element.60), channel_id=1, source_target_pairs={{0,16},{8,24},{16,0},{24,8},{1,17},{9,25},{17,1},{25,9},{2,18},{10... | collective-permute-start | bytes 1179656 | tf_op jit(solution)/shard_map/ppermute | solution.py:261
  102.8 3.1 %collective-permute-start.29 = (bf16[2,64,1024]{2,1,0:T(8,128)(2,1)S(1)}, bf16[2,64,1024]{2,1,0:T(8,128)(2,1)S(1)}, u32[]{:S(2)}, u32[]{:S(2)}) collective-permute-start(bf16[2,64,1024]{2,1,0:T(8,128)(2,1)S(1)} %get-tuple-element.61), channel_id=1, source_target_pairs={{0,8},{8,0},{16,24},{24,16},{1,9},{9,1},{17,25},{25,17},{2,10},{10... | collective-permute-start | bytes 786440 | tf_op jit(solution)/shard_map/ppermute | solution.py:263
  114.4 7.8 %collective-permute-start.30 = (bf16[3,64,1024]{2,1,0:T(8,128)(2,1)S(1)}, bf16[3,64,1024]{2,1,0:T(8,128)(2,1)S(1)}, u32[]{:S(2)}, u32[]{:S(2)}) collective-permute-start(bf16[3,64,1024]{2,1,0:T(8,128)(2,1)S(1)} %get-tuple-element.64), channel_id=1, source_target_pairs={{0,16},{8,24},{16,0},{24,8},{1,17},{9,25},{17,1},{25,9},{2,18},{10... | collective-permute-start | bytes 1179656 | tf_op jit(solution)/shard_map/ppermute | solution.py:261
  115.3 1.5 %collective-permute-start.31 = (bf16[2,64,1024]{2,1,0:T(8,128)(2,1)S(1)}, bf16[2,64,1024]{2,1,0:T(8,128)(2,1)S(1)}, u32[]{:S(2)}, u32[]{:S(2)}) collective-permute-start(bf16[2,64,1024]{2,1,0:T(8,128)(2,1)S(1)} %get-tuple-element.65), channel_id=1, source_target_pairs={{0,8},{8,0},{16,24},{24,16},{1,9},{9,1},{17,25},{25,17},{2,10},{10... | collective-permute-start | bytes 786440 | tf_op jit(solution)/shard_map/ppermute | solution.py:263
  123.8 1.6 %collective-permute-start.32 = (bf16[2,64,1024]{2,1,0:T(8,128)(2,1)S(1)}, bf16[2,64,1024]{2,1,0:T(8,128)(2,1)S(1)}, u32[]{:S(2)}, u32[]{:S(2)}) collective-permute-start(bf16[2,64,1024]{2,1,0:T(8,128)(2,1)S(1)} %get-tuple-element.67), channel_id=1, source_target_pairs={{0,8},{8,0},{16,24},{24,16},{1,9},{9,1},{17,25},{25,17},{2,10},{10... | collective-permute-start | bytes 786440 | tf_op jit(solution)/shard_map/ppermute | solution.py:263
  (3 other events, 24.0 us)

commit v2 on v0

v2 whole, which is shorter than its diff:
```python
import functools

import jax
import jax.numpy as jnp
from jax import lax
from jax.experimental import pallas as pl
from jax.experimental.pallas import tpu as pltpu
from jax.sharding import PartitionSpec as P

CAP = 2
KERNEL_COST = 4 * 10**9
FINISH_LAG = 1
PLACE_LAG = 0
LANES = 128
BF16 = jnp.bfloat16
F32 = jnp.float32


def ring_order(n):
    return list(range(0, n, 2)) + list(range(1, n, 2))[::-1]


def plan_of(owners_ref, side):
    n = owners_ref.shape[1]
    own = [owners_ref[0, p] for p in range(n)]
    rank, key = [], []
    for p in range(n):
        r = jnp.int32(0)
        for q in range(p):
            r = r + (own[q] == own[p]).astype(jnp.int32)
        rank.append(r)
        key.append(own[p] * CAP + r)
    place = []
    for p in range(n):
        r = jnp.int32(0)
        for q in range(n):
            if q != p:
                r = r + (key[q] < key[p]).astype(jnp.int32)
        place.append(jnp.where(side == 0, r, n - 1 - r))
    pair_at = []
    for i in range(n):
        r = jnp.int32(0)
        for p in range(n):
            r = r + jnp.where(place[p] == i, p, 0)
        pair_at.append(r)

    def slot_place(sector, slot):
        r = jnp.int32(-1)
        for p in range(n):
            r = jnp.where((own[p] == sector) & (rank[p] == slot), place[p], r)
        return r

    return pair_at, slot_place


def prepare(r, m):
    ids, meta, spread = r["ids"], r["meta"], r["spread"]
    side, core = ids[0], ids[1]
    pair_at, slot_place = plan_of(r["owners"], side)
    for slot in range(CAP):
        meta[0, slot] = slot_place(side * 2 + core, slot)
        meta[0, CAP + slot] = slot_place(side * 2 + 1 - core, slot)
    meta[0, 2 * CAP] = core
    meta[0, 2 * CAP + 1] = ids[2]
    for s in range(2):
        w = r[f"w{s}"]
        nb = w.shape[1]
        for i, pair in enumerate(pair_at):
            for k in range(nb):
                row = (s * len(pair_at) + i) * nb + k
                spread[pl.ds(row, 1), :] = jnp.full((1, LANES), w[pair, k], F32)
        r["res"][pl.ds(s * m, m), :] = r[f"res{s}"][...]


def step_kernel(cfg, *refs):
    r = dict(zip(cfg["names"], refs, strict=True))
    half, n_owner, m, nb = cfg["half"], cfg["n_owner"], cfg["m"], cfg["nb"]
    pairs, sent = cfg["pairs"], cfg["sent"]
    if cfg["first"]:
        prepare(r, m)
    place_of = [r["meta"][0, slot] for slot in range(CAP)]
    other_of = [r["meta"][0, CAP + slot] for slot in range(CAP)]
    core, q = r["meta"][0, 2 * CAP], r["meta"][0, 2 * CAP + 1]
    stores = []

    def store(buf, sem, unit, which):
        base = 0
        for lane, (step, turn, start, rows) in enumerate(unit):
            at = lax.rem(q - turn * step + 2 * n_owner, n_owner)
            owner = jnp.where(at < n_owner // 2, 2 * at, 2 * (n_owner - 1 - at) + 1)
            row = pl.multiple_of(owner * (2 * half) + which * half + start, 8)
            c = pltpu.make_async_copy(
                r[buf].at[:, pl.ds(base, rows), :], r["out"].at[:, pl.ds(row, rows), :], r[sem].at[lane]
            )
            c.start()
            stores.append(c)
            base += rows

    for j, unit in enumerate(cfg["finish"]):
        kept, crossed, fin = r[f"kept{j}"], r[f"crossed{j}"], r[f"fin{j}"]
        for slot in range(CAP):
            i = jnp.maximum(other_of[slot], 0)
            r[f"swap{j}"][slot] = (kept[i] + crossed[sent - 1 - i].astype(F32)).astype(BF16)
        for slot in range(CAP):
            place = place_of[slot]
            i = jnp.maximum(place, 0)
            fin[slot] = jnp.where(place >= 0, kept[i] + crossed[sent - 1 - i].astype(F32), 0.0)
        store(f"fin{j}", f"finsem{j}", unit, core)
    for j, unit in enumerate(cfg["place"]):
        for slot in range(CAP):
            v = r[f"swapped{j}"][slot].astype(F32)
            r[f"put{j}"][slot] = jnp.where(place_of[slot] >= 0, v, 0.0)
        store(f"put{j}", f"putsem{j}", unit, 1 - core)

    if cfg["compute"] is not None:
        unit = cfg["compute"]
        total = sum(block[-1] for block in unit)
        for s in range(2):
            base = 0
            for lane, (*_, rows) in enumerate(unit):
                for c in range(0, m, LANES):
                    cols = pl.ds(c, LANES)
                    x = [r[f"x{lane}"][s, k, :, cols].astype(F32) for k in range(nb)]
                    for i in range(pairs):
                        row = (s * pairs + i) * nb
                        a = r["spread"][pl.ds(row, 1), :] * x[0]
                        for k in range(1, nb):
                            a = a + r["spread"][pl.ds(row + k, 1), :] * x[k]
                        r["abuf"][pl.ds(i * total + base, rows), pl.ds(s * m + c, LANES)] = a.astype(BF16)
                base += rows
        w = m // cfg["tiles"]
        for t in range(cfg["tiles"]):
            cols = pl.ds(t * w, w)
            y = jnp.dot(r["abuf"][...], r["res"][:, cols], preferred_element_type=F32)
            y = y.reshape(pairs, total, w)
            r["send"][:, :, cols] = y[pairs - sent :].astype(BF16)
            r["kept"][:, :, cols] = y[:sent]
    r["token"][...] = jnp.zeros_like(r["token"])
    for c in stores:
        c.wait()


def step_call(static, common, out, compute=None, finish=(), place=(), after=()):
    m, pairs, sent = static["m"], static["pairs"], static["sent"]
    smem = pl.BlockSpec(memory_space=pltpu.SMEM)
    vmem = pl.BlockSpec(memory_space=pltpu.VMEM)
    anym = pl.BlockSpec(memory_space=pl.ANY)
    names, args, specs = [], [], []
    outs, shapes, ospecs = [], [], []
    snames, scratch = [], []

    def take(name, arg, spec):
        names.append(name)
        args.append(arg)
        specs.append(spec)

    def give(name, shape, dtype, spec):
        outs.append(name)
        shapes.append(jax.ShapeDtypeStruct(shape, dtype))
        ospecs.append(spec)

    def hold(name, what):
        snames.append(name)
        scratch.append(what)

    def rows_in(unit):
        return sum(block[-1] for block in unit)

    first = "meta" not in common
    if first:
        for name in ("ids", "owners", "w0", "w1"):
            take(name, common[name], smem)
        for name in ("res0", "res1"):
            take(name, common[name], vmem)
        give("meta", (1, 2 * CAP + 2), jnp.int32, smem)
        give("spread", (2 * pairs * static["nb"], LANES), F32, vmem)
        give("res", (2 * m, m), BF16, vmem)
    else:
        take("meta", common["meta"], smem)
    flops = 0
    if compute is not None:
        unit, xs = compute
        total = rows_in(unit)
        if not first:
            take("res", common["res"], vmem)
        if not first:
            take("spread", common["spread"], vmem)
        for lane, x in enumerate(xs):
            take(f"x{lane}", x, vmem)
        give("send", (sent, total, m), BF16, vmem)
        give("kept", (sent, total, m), F32, vmem)
        hold("abuf", pltpu.VMEM((pairs * total, 2 * m), BF16))
        flops += 2 * pairs * total * 2 * m * m
    for j, (unit, kept, crossed) in enumerate(finish):
        take(f"kept{j}", kept, vmem)
        take(f"crossed{j}", crossed, vmem)
        give(f"swap{j}", (CAP, rows_in(unit), m), BF16, vmem)
        hold(f"fin{j}", pltpu.VMEM((CAP, rows_in(unit), m), F32))
        hold(f"finsem{j}", pltpu.SemaphoreType.DMA((len(unit),)))
    for j, (unit, swapped) in enumerate(place):
        take(f"swapped{j}", swapped, vmem)
        hold(f"put{j}", pltpu.VMEM((CAP, rows_in(unit), m), F32))
        hold(f"putsem{j}", pltpu.SemaphoreType.DMA((len(unit),)))
    for j, x in enumerate(after):
        take(f"after{j}", x, anym)
    give("token", (8, LANES), F32, vmem)
    aliases = {}
    if finish or place:
        give("out", (CAP, m, m), F32, anym)
        if out is not None:
            aliases[len(names)] = outs.index("out")
            take("out_in", out, anym)
    cfg = dict(
        static,
        first=first,
        compute=None if compute is None else compute[0],
        finish=[f[0] for f in finish],
        place=[p[0] for p in place],
        tiles=4,
        names=names + outs + snames,
    )
    got = pl.pallas_call(
        functools.partial(step_kernel, cfg),
        in_specs=specs,
        out_specs=ospecs,
        out_shape=shapes,
        scratch_shapes=scratch,
        input_output_aliases=aliases,
        compiler_params=pltpu.CompilerParams(vmem_limit_bytes=24 * 1024 * 1024),
        cost_estimate=pl.CostEstimate(flops=KERNEL_COST, bytes_accessed=1000, transcendentals=0),
    )(*args)
    return dict(zip(outs, got, strict=True))


def shards(broadcast_ops, resident_ops, integrals, owner_list):
    n_sector = lax.axis_size("sector")
    n_owner = lax.axis_size("owner")
    sector = lax.axis_index("sector")
    owner = lax.axis_index("owner")
    nb, rows, m = broadcast_ops.shape[1:]
    pairs = owner_list.shape[1]
    half = rows // 2
    core = sector % 2
    swap_core = [(i, i ^ 1) for i in range(n_sector)]
    swap_side = [(i, (i + 2) % n_sector) for i in range(n_sector)]
    order = ring_order(n_owner)
    up = [(order[i], order[(i + 1) % n_owner]) for i in range(n_owner)]
    down = [(b, a) for a, b in up]
    if half % 32 == 0:
        lanes = [(1, 0, half // 2), (-1, half // 2, half // 2)]
    else:
        lanes = [(1, 0, half)]
    cuts = 2 if lanes[0][2] % 32 == 0 else 1
    static = dict(m=m, nb=nb, half=half, n_owner=n_owner, pairs=pairs, sent=min(pairs, CAP + 1))

    shared = broadcast_ops[0]
    theirs = lax.dynamic_slice_in_dim(shared, (1 - core) * half, half, 1).astype(BF16)
    arrived = lax.ppermute(theirs, "sector", swap_core)
    mine = lax.dynamic_slice_in_dim(shared, core * half, half, 1).astype(BF16)
    xs = [jnp.stack([mine[:, a : a + n], arrived[:, a : a + n]]) for _, a, n in lanes]
    resident, *xs = lax.optimization_barrier((resident_ops[0, 0], *xs))
    res_own = resident.astype(BF16)
    w_own = integrals[0, 0]
    w_other = lax.ppermute(w_own, "sector", swap_core)
    res_other = lax.ppermute(res_own, "sector", swap_core)
    q = jnp.where(owner % 2 == 0, owner // 2, n_owner - 1 - owner // 2)
    ids = jnp.stack([sector // 2, core, q]).astype(jnp.int32)
    common = {"ids": ids, "owners": owner_list, "w0": w_own, "w1": w_other, "res0": res_own, "res1": res_other}

    def send_on(x, turn):
        return lax.ppermute(x, "owner", up if turn == 1 else down)

    units, kept, crossed, swapped = [], {}, {}, {}
    to_finish, to_place = [], []
    state = {"out": None, "token": None}

    def call(unit, rows, n_finish, n_place):
        finish = [to_finish.pop(0) for _ in range(max(0, n_finish))]
        place = [to_place.pop(0) for _ in range(max(0, n_place))]
        got = step_call(
            static,
            common,
            state["out"],
            None if unit is None else (unit, rows),
            [(units[f], kept[f], crossed[f]) for f in finish],
            [(units[p], swapped[p]) for p in place],
            [] if state["token"] is None else [state["token"]],
        )
        common.update({name: got[name] for name in ("meta", "spread", "res") if name in got})
        state["out"], state["token"] = got.get("out", state["out"]), got["token"]
        if unit is not None:
            i = len(units)
            units.append(unit)
            kept[i] = got["kept"]
            crossed[i] = lax.ppermute(got["send"], "sector", swap_side)
            to_finish.append(i)
        for j, f in enumerate(finish):
            swapped[f] = lax.ppermute(got[f"swap{j}"], "sector", swap_core)
            to_place.append(f)

    last = n_owner - 1
    for step in range(last):
        unit = [(step, *lane) for lane in lanes]
        if state["token"] is not None:
            for i in range(len(xs) - 1, -1, -1):
                xs[i], state["token"] = lax.optimization_barrier((xs[i], state["token"]))
        if step < last - 1:
            then = [send_on(x, lane[0]) for x, lane in zip(xs, lanes, strict=True)]
        else:
            then = [[send_on(jnp.split(x, cuts, 2)[c], lane[0]) for x, lane in zip(xs, lanes, strict=True)] for c in range(cuts)]
        call(unit, xs, len(to_finish) - FINISH_LAG, len(to_place) - PLACE_LAG)
        xs = then
    for c in range(cuts):
        unit = [(last, turn, start + c * (rows // cuts), rows // cuts) for turn, start, rows in lanes]
        if c < cuts - 1:
            call(unit, xs[c], len(to_finish) - 1, len(to_place))
        else:
            call(unit, xs[c], 0, 0)
    call(None, None, len(to_finish), len(to_place))
    call(None, None, 0, len(to_place))
    return state["out"][None, None]


def solution(mesh):
    in_specs = (
        P("sector", None, "owner", None),
        P("sector", "owner", None, None),
        P("sector", "owner", None, None),
        P("owner", None),
    )
    out_specs = P("sector", "owner", None, None, None)
    return jax.shard_map(shards, mesh=mesh, in_specs=in_specs, out_specs=out_specs, check_vma=False)
```

time: 369 us -> 117 us (0.32)
  waiting for transfers between devices: 251 us -> 52.6 us
  matrix products: 73.6 us -> 0 us
  Pallas kernels: 0 us -> 31.5 us
  starting transfers between devices: 0.04 us -> 29.8 us
  local copies, waits for them, and re-layouts: 20.7 us -> 2 us
  between operations: 13.4 us -> 0.37 us
  other arithmetic: 10.2 us -> 0.49 us
    all_gather x1 -> x0, waiting for transfers between devices: 126 us -> none  [shards(): lax.all_gather(shared.astype(jnp.bfloat16), 'owner', axis=1, tiled=True)]
    reduce_scatter x1 -> x0, waiting for transfers between devices: 124 us -> none  [shards(): lax.psum_scatter(jnp.einsum('jk,kmn->jmn', chosen, products, precision=hi...]
    dot_general x3 -> x0, matrix products: 73.6 us -> none  [the longest x1 41.2 us: shards(): jnp.einsum('jk,kmn->jmn', chosen, products, precision=highest)]
    ppermute x0 -> x37, waiting for transfers between devices: none -> 52.6 us  [the longest x16 39.7 us: send_on(): return lax.ppermute(x, 'owner', up if turn == 1 else down)]
    pallas_call x0 -> x11, Pallas kernels: none -> 31.5 us  [step_call(): pl.pallas_call(functools.partial(step_kernel, cfg), in_specs=specs, out_s...]
    ppermute x0 -> x37, starting transfers between devices: none -> 29.8 us  [the longest x16 17.2 us: send_on(): return lax.ppermute(x, 'owner', up if turn == 1 else down)]
    convert_element_type x1, local copies, waits for them, and re-layouts: 20.6 us -> 1.84 us  [shards(): mine = lax.dynamic_slice_in_dim(shared, core * half, half, 1).astype(BF16)]
    broadcast_in_dim x1 -> x0, other arithmetic: 6.63 us -> none  [shards(): return result[None, None]]
  transfers between devices with their start and end apart: 2 -> 37, of which waited for: 2 -> 17; matrix products, arithmetic and copies ran while one was open for 0% -> 0% of each run, Pallas kernels for 0% -> 24%
where the time goes in v2:
time: 117 us
  waiting for transfers between devices  52.6 us (45%)
  Pallas kernels  31.5 us (27%)
  starting transfers between devices  29.8 us (25%)
  local copies, waits for them, and re-layouts  2 us (2%)
    ppermute x16, waiting for transfers between devices, send_on(): return lax.ppermute(x, 'owner', up if turn == 1 else down)  39.7 us
    pallas_call x11, Pallas kernels, step_call(): pl.pallas_call(functools.partial(step_kernel, cfg), in_specs=specs, out_s...  31.5 us
    ppermute x16, starting transfers between devices, send_on(): return lax.ppermute(x, 'owner', up if turn == 1 else down)  17.2 us
    ppermute x9, starting transfers between devices, call(): crossed[i] = lax.ppermute(got['send'], 'sector', swap_side)  10.5 us
    ppermute x9, waiting for transfers between devices, call(): crossed[i] = lax.ppermute(got['send'], 'sector', swap_side)  9.1 us
  transfers between devices with their start and end apart: 37, of which 17 were waited for; matrix products, arithmetic and copies ran while one was open for 0% of the time, Pallas kernels for 24%

profile of v2, /device:TPU:0, one launch (start us, length us, event | category | flops | bytes accessed | tf_op | source)
XLA Modules:
  0.0 116.8 jit_solution(16807155631854008131)
XLA Ops:
  0.0 1.8 %fusion = (bf16[4,64,1024]{2,1,0:T(8,128)(2,1)S(1)}, bf16[4,64,1024]{2,1,0:T(8,128)(2,1)S(1)}) fusion(f32[1,4,128,1024]{3,2,1,0:T(8,128)} %param.4, s32[]{:T(128)S(6)} %select_n.33, s32[]{:T(128)S(6)} %select_n.34), kind=kLoop, calls=%fused_computation.2 | loop fusion | bytes 2097160 | tf_op jit(solution)/shard_map/convert_element_type | solution.py:259
  2.4 1.5 %collective-permute-done.1 = bf16[4,64,1024]{2,1,0:T(8,128)(2,1)S(1)} collective-permute-done((bf16[4,64,1024]{2,1,0:T(8,128)(2,1)S(1)}, bf16[4,64,1024]{2,1,0:T(8,128)(2,1)S(1)}, u32[]{:S(2)}, u32[]{:S(2)}) %collective-permute-start.1) | collective-permute-done | bytes 524320 | tf_op jit(solution)/shard_map/ppermute | solution.py:258
  4.8 2.6 %collective-permute-start.4 = (bf16[2,4,32,1024]{3,2,1,0:T(8,128)(2,1)S(1)}, bf16[2,4,32,1024]{3,2,1,0:T(8,128)(2,1)}, u32[]{:S(2)}, u32[]{:S(2)}) collective-permute-start(bf16[2,4,32,1024]{3,2,1,0:T(8,128)(2,1)S(1)} %get-tuple-element.82.refs_7_), channel_id=1, source_target_pairs={{2,0},{4,2},{6,4},{7,6},{5,7},{3,5},{1,3},{0,1},{10,8},{12,10},{14... | collective-permute-start | bytes 1572872 | tf_op jit(solution)/shard_map/ppermute | solution.py:271
  8.8 3.7 %shard_map.46 = (s32[1,6]{1,0:T(1,128)S(1)}, f32[32,128]{1,0:T(8,128)S(1)}, bf16[2048,1024]{1,0:T(8,128)(2,1)S(1)}, bf16[3,64,1024]{2,1,0:T(8,128)(2,1)S(1)}, f3...) custom-call(s32[3]{0:T(128)S(1)} %pad_add_fusion.refs_0_, s32[1,4]{1,0:T(1,128)S(1)} %copy-done.1, f32[4,4]{1,0:T(4,128)S(1)} %bitcast.19, ...), custom_call_target="tpu_custom_call" | custom-call | flops 4000000000 | bytes 1000 | tf_op jit(solution)/shard_map/pallas_call | solution.py:222
  12.5 7.6 %collective-permute-done.4.refs_4_ = bf16[2,4,32,1024]{3,2,1,0:T(8,128)(2,1)} collective-permute-done((bf16[2,4,32,1024]{3,2,1,0:T(8,128)(2,1)S(1)}, bf16[2,4,32,1024]{3,2,1,0:T(8,128)(2,1)}, u32[]{:S(2)}, u32[]{:S(2)}) %collective-permute-start.4) | collective-permute-done | bytes 524320 | tf_op jit(solution)/shard_map/ppermute | solution.py:271
  20.1 1.7 %collective-permute-start.6 = (bf16[2,4,32,1024]{3,2,1,0:T(8,128)(2,1)}, bf16[2,4,32,1024]{3,2,1,0:T(8,128)(2,1)S(1)}, u32[]{:S(2)}, u32[]{:S(2)}) collective-permute-start(bf16[2,4,32,1024]{3,2,1,0:T(8,128)(2,1)} %collective-permute-done.4.refs_4_), channel_id=1, source_target_pairs={{2,0},{4,2},{6,4},{7,6},{5,7},{3,5},{1,3},{0,1},{10,8},{12,10},{14... | collective-permute-start | bytes 1572872 | tf_op jit(solution)/shard_map/ppermute | solution.py:271
  22.1 1.7 %collective-permute-start.9 = (bf16[3,64,1024]{2,1,0:T(8,128)(2,1)S(1)}, bf16[3,64,1024]{2,1,0:T(8,128)(2,1)S(1)}, u32[]{:S(2)}, u32[]{:S(2)}) collective-permute-start(bf16[3,64,1024]{2,1,0:T(8,128)(2,1)S(1)} %get-tuple-element.96), channel_id=1, source_target_pairs={{0,16},{8,24},{16,0},{24,8},{1,17},{9,25},{17,1},{25,9},{2,18},{10... | collective-permute-start | bytes 1179656 | tf_op jit(solution)/shard_map/ppermute | solution.py:295
  23.8 2.9 %shard_map.47 = (bf16[3,64,1024]{2,1,0:T(8,128)(2,1)S(1)}, f32[3,64,1024]{2,1,0:T(8,128)S(1)}, f32[8,128]{1,0:T(8,128)S(1)}) custom-call(s32[1,6]{1,0:T(1,128)S(1)} %get-tuple-element.83.refs_0_, bf16[2048,1024]{1,0:T(8,128)(2,1)S(1)} %get-tuple-element.84.refs_1_, f32[32,128]{1,0:T(8,128)S(1)} %get-tuple-element.85.refs_2_, ...), custom_call_target="tpu_custom_call" | custom-call | flops 4000000000 | bytes 1000 | tf_op jit(solution)/shard_map/pallas_call | solution.py:222
  27.2 6.8 %collective-permute-done.6.refs_4_ = bf16[2,4,32,1024]{3,2,1,0:T(8,128)(2,1)S(1)} collective-permute-done((bf16[2,4,32,1024]{3,2,1,0:T(8,128)(2,1)}, bf16[2,4,32,1024]{3,2,1,0:T(8,128)(2,1)S(1)}, u32[]{:S(2)}, u32[]{:S(2)}) %collective-permute-start.6) | collective-permute-done | bytes 524320 | tf_op jit(solution)/shard_map/ppermute | solution.py:271
  35.7 1.4 %collective-permute-start.8 = (bf16[2,4,32,1024]{3,2,1,0:T(8,128)(2,1)S(1)}, bf16[2,4,32,1024]{3,2,1,0:T(8,128)(2,1)S(1)}, u32[]{:S(2)}, u32[]{:S(2)}) collective-permute-start(bf16[2,4,32,1024]{3,2,1,0:T(8,128)(2,1)S(1)} %collective-permute-done.6.refs_4_), channel_id=1, source_target_pairs={{2,0},{4,2},{6,4},{7,6},{5,7},{3,5},{1,3},{0,1},{10,8},{12,10},{14... | collective-permute-start | bytes 1572872 | tf_op jit(solution)/shard_map/ppermute | solution.py:271
  37.1 3.2 %shard_map.48 = (bf16[3,64,1024]{2,1,0:T(8,128)(2,1)S(1)}, f32[3,64,1024]{2,1,0:T(8,128)S(1)}, bf16[2,64,1024]{2,1,0:T(8,128)(2,1)S(1)}, f32[8,128]{1,0:T(8,128)S(1)}, f32[2,1024,1024]{2,1,0:T(8,128)}) custom-call(s32[1,6]{1,0:T(1,128)S(1)} %get-tuple-element.83.refs_0_, bf16[2048,1024]{1,0:T(8,128)(2,1)S(1)} %get-tuple-element.84.refs_1_, ...), custom_call_target="tpu_custom_call" | custom-call | flops 4000000000 | bytes 1000 | tf_op jit(solution)/shard_map/pallas_call | solution.py:222
  40.4 1.6 %collective-permute-start.16 = (bf16[3,64,1024]{2,1,0:T(8,128)(2,1)S(1)}, bf16[3,64,1024]{2,1,0:T(8,128)(2,1)S(1)}, u32[]{:S(2)}, u32[]{:S(2)}) collective-permute-start(bf16[3,64,1024]{2,1,0:T(8,128)(2,1)S(1)} %get-tuple-element.112), channel_id=1, source_target_pairs={{0,16},{8,24},{16,0},{24,8},{1,17},{9,25},{17,1},{25,9},{2,18},{10... | collective-permute-start | bytes 1179656 | tf_op jit(solution)/shard_map/ppermute | solution.py:295
  42.0 5.9 %collective-permute-done.8.refs_4_ = bf16[2,4,32,1024]{3,2,1,0:T(8,128)(2,1)S(1)} collective-permute-done((bf16[2,4,32,1024]{3,2,1,0:T(8,128)(2,1)S(1)}, bf16[2,4,32,1024]{3,2,1,0:T(8,128)(2,1)S(1)}, u32[]{:S(2)}, u32[]{:S(2)}) %collective-permute-start.8) | collective-permute-done | bytes 524320 | tf_op jit(solution)/shard_map/ppermute | solution.py:271
  49.9 3.4 %shard_map.49 = (bf16[3,64,1024]{2,1,0:T(8,128)(2,1)S(1)}, f32[3,64,1024]{2,1,0:T(8,128)S(1)}, bf16[2,64,1024]{2,1,0:T(8,128)(2,1)S(1)}, f32[8,128]{1,0:T(8,128)S(1)}, f32[2,1024,1024]{2,1,0:T(8,128)}) custom-call(s32[1,6]{1,0:T(1,128)S(1)} %get-tuple-element.83.refs_0_, ...), custom_call_target="tpu_custom_call", output_to_operand_aliasing={{4}: (9, {})} | custom-call | flops 4000000000 | bytes 1000 | tf_op jit(solution)/shard_map/pallas_call | solution.py:222
  53.3 8.0 %collective-permute-done.11.refs_4_ = bf16[2,4,32,1024]{3,2,1,0:T(8,128)(2,1)S(1)} collective-permute-done((bf16[2,4,32,1024]{3,2,1,0:T(8,128)(2,1)S(1)}, bf16[2,4,32,1024]{3,2,1,0:T(8,128)(2,1)S(1)}, u32[]{:S(2)}, u32[]{:S(2)}) %collective-permute-start.11) | collective-permute-done | bytes 524320 | tf_op jit(solution)/shard_map/ppermute | solution.py:271
  63.4 1.5 %collective-permute-start.20 = (bf16[3,64,1024]{2,1,0:T(8,128)(2,1)S(1)}, bf16[3,64,1024]{2,1,0:T(8,128)(2,1)S(1)}, u32[]{:S(2)}, u32[]{:S(2)}) collective-permute-start(bf16[3,64,1024]{2,1,0:T(8,128)(2,1)S(1)} %get-tuple-element.121), channel_id=1, source_target_pairs={{0,16},{8,24},{16,0},{24,8},{1,17},{9,25},{17,1},{25,9},{2,18},{10... | collective-permute-start | bytes 1179656 | tf_op jit(solution)/shard_map/ppermute | solution.py:295
  64.9 3.4 %shard_map.50 = (bf16[3,64,1024]{2,1,0:T(8,128)(2,1)S(1)}, f32[3,64,1024]{2,1,0:T(8,128)S(1)}, bf16[2,64,1024]{2,1,0:T(8,128)(2,1)S(1)}, f32[8,128]{1,0:T(8,128)S(1)}, f32[2,1024,1024]{2,1,0:T(8,128)}) custom-call(s32[1,6]{1,0:T(1,128)S(1)} %get-tuple-element.83.refs_0_, ...), custom_call_target="tpu_custom_call", output_to_operand_aliasing={{4}: (9, {})} | custom-call | flops 4000000000 | bytes 1000 | tf_op jit(solution)/shard_map/pallas_call | solution.py:222
  68.3 3.0 %collective-permute-done.15.refs_4_ = bf16[2,4,32,1024]{3,2,1,0:T(8,128)(2,1)S(1)} collective-permute-done((bf16[2,4,32,1024]{3,2,1,0:T(8,128)(2,1)S(1)}, bf16[2,4,32,1024]{3,2,1,0:T(8,128)(2,1)S(1)}, u32[]{:S(2)}, u32[]{:S(2)}) %collective-permute-start.15) | collective-permute-done | bytes 524320 | tf_op jit(solution)/shard_map/ppermute | solution.py:271
  73.3 2.3 %collective-permute-start.22 = (bf16[3,64,1024]{2,1,0:T(8,128)(2,1)S(1)}, bf16[3,64,1024]{2,1,0:T(8,128)(2,1)S(1)}, u32[]{:S(2)}, u32[]{:S(2)}) collective-permute-start(bf16[3,64,1024]{2,1,0:T(8,128)(2,1)S(1)} %get-tuple-element.130), channel_id=1, source_target_pairs={{0,16},{8,24},{16,0},{24,8},{1,17},{9,25},{17,1},{25,9},{2,18},{10... | collective-permute-start | bytes 1179656 | tf_op jit(solution)/shard_map/ppermute | solution.py:295
  75.7 3.4 %shard_map.51 = (bf16[3,64,1024]{2,1,0:T(8,128)(2,1)S(1)}, f32[3,64,1024]{2,1,0:T(8,128)S(1)}, bf16[2,64,1024]{2,1,0:T(8,128)(2,1)S(1)}, f32[8,128]{1,0:T(8,128)S(1)}, f32[2,1024,1024]{2,1,0:T(8,128)}) custom-call(s32[1,6]{1,0:T(1,128)S(1)} %get-tuple-element.83.refs_0_, ...), custom_call_target="tpu_custom_call", output_to_operand_aliasing={{4}: (9, {})} | custom-call | flops 4000000000 | bytes 1000 | tf_op jit(solution)/shard_map/pallas_call | solution.py:222
  79.2 3.5 %collective-permute-done.19.refs_4_ = bf16[2,4,32,1024]{3,2,1,0:T(8,128)(2,1)S(1)} collective-permute-done((bf16[2,4,32,1024]{3,2,1,0:T(8,128)(2,1)S(1)}, bf16[2,4,32,1024]{3,2,1,0:T(8,128)(2,1)S(1)}, u32[]{:S(2)}, u32[]{:S(2)}) %collective-permute-start.19) | collective-permute-done | bytes 524320 | tf_op jit(solution)/shard_map/ppermute | solution.py:271
  83.3 1.6 %collective-permute-start.25 = (bf16[2,4,16,1024]{3,2,1,0:T(8,128)(2,1)S(1)}, bf16[2,4,16,1024]{3,2,1,0:T(8,128)(2,1)S(1)}, u32[]{:S(2)}, u32[]{:S(2)}) collective-permute-start(bf16[2,4,16,1024]{3,2,1,0:T(8,128)(2,1)S(1)} %get-tuple-element.160), channel_id=1, source_target_pairs={{0,2},{2,4},{4,6},{6,7},{7,5},{5,3},{3,1},{1,0},{8,10},{10,12},{12... | collective-permute-start | bytes 786440 | tf_op jit(solution)/shard_map/ppermute | solution.py:271
  85.7 3.4 %shard_map.52 = (bf16[3,64,1024]{2,1,0:T(8,128)(2,1)S(1)}, f32[3,64,1024]{2,1,0:T(8,128)S(1)}, bf16[2,64,1024]{2,1,0:T(8,128)(2,1)S(1)}, f32[8,128]{1,0:T(8,128)S(1)}, f32[2,1024,1024]{2,1,0:T(8,128)}) custom-call(s32[1,6]{1,0:T(1,128)S(1)} %get-tuple-element.83.refs_0_, ...), custom_call_target="tpu_custom_call", output_to_operand_aliasing={{4}: (9, {})} | custom-call | flops 4000000000 | bytes 1000 | tf_op jit(solution)/shard_map/pallas_call | solution.py:222
  89.2 1.6 %collective-permute-start.30 = (bf16[2,4,16,1024]{3,2,1,0:T(8,128)(2,1)S(1)}, bf16[2,4,16,1024]{3,2,1,0:T(8,128)(2,1)S(1)}, u32[]{:S(2)}, u32[]{:S(2)}) collective-permute-start(bf16[2,4,16,1024]{3,2,1,0:T(8,128)(2,1)S(1)} %get-tuple-element.159), channel_id=1, source_target_pairs={{0,2},{2,4},{4,6},{6,7},{7,5},{5,3},{3,1},{1,0},{8,10},{10,12},{12... | collective-permute-start | bytes 786440 | tf_op jit(solution)/shard_map/ppermute | solution.py:271
  92.1 2.7 %shard_map.53 = (bf16[3,32,1024]{2,1,0:T(8,128)(2,1)S(1)}, f32[3,32,1024]{2,1,0:T(8,128)S(1)}, bf16[2,64,1024]{2,1,0:T(8,128)(2,1)S(1)}, f32[8,128]{1,0:T(8,128)S(1)}, f32[2,1024,1024]{2,1,0:T(8,128)}) custom-call(s32[1,6]{1,0:T(1,128)S(1)} %get-tuple-element.83.refs_0_, ...), custom_call_target="tpu_custom_call", output_to_operand_aliasing={{4}: (9, {})} | custom-call | flops 4000000000 | bytes 1000 | tf_op jit(solution)/shard_map/pallas_call | solution.py:222
  96.0 1.9 %collective-permute-done.30.refs_3_ = bf16[2,4,16,1024]{3,2,1,0:T(8,128)(2,1)S(1)} collective-permute-done((bf16[2,4,16,1024]{3,2,1,0:T(8,128)(2,1)S(1)}, bf16[2,4,16,1024]{3,2,1,0:T(8,128)(2,1)S(1)}, u32[]{:S(2)}, u32[]{:S(2)}) %collective-permute-start.30) | collective-permute-done | bytes 262176 | tf_op jit(solution)/shard_map/ppermute | solution.py:271
  99.3 1.6 %shard_map.54 = (bf16[3,32,1024]{2,1,0:T(8,128)(2,1)S(1)}, f32[3,32,1024]{2,1,0:T(8,128)S(1)}, f32[8,128]{1,0:T(8,128)S(1)}) custom-call(s32[1,6]{1,0:T(1,128)S(1)} %get-tuple-element.83.refs_0_, bf16[2048,1024]{1,0:T(8,128)(2,1)S(1)} %get-tuple-element.84.refs_1_, f32[32,128]{1,0:T(8,128)S(1)} %get-tuple-element.85.refs_2_, ...), custom_call_target="tpu_custom_call" | custom-call | flops 4000000000 | bytes 1000 | tf_op jit(solution)/shard_map/pallas_call | solution.py:222
  101.6 1.7 %collective-permute-done.24.refs_2_ = bf16[3,64,1024]{2,1,0:T(8,128)(2,1)S(1)} collective-permute-done((bf16[3,64,1024]{2,1,0:T(8,128)(2,1)S(1)}, bf16[3,64,1024]{2,1,0:T(8,128)(2,1)S(1)}, u32[]{:S(2)}, u32[]{:S(2)}) %collective-permute-start.24) | collective-permute-done | bytes 393248 | tf_op jit(solution)/shard_map/ppermute | solution.py:295
  103.2 4.2 %collective-permute-done.29.refs_4_ = bf16[3,32,1024]{2,1,0:T(8,128)(2,1)S(1)} collective-permute-done((bf16[3,32,1024]{2,1,0:T(8,128)(2,1)S(1)}, bf16[3,32,1024]{2,1,0:T(8,128)(2,1)S(1)}, u32[]{:S(2)}, u32[]{:S(2)}) %collective-permute-start.29) | collective-permute-done | bytes 196640 | tf_op jit(solution)/shard_map/ppermute | solution.py:295
  107.4 3.2 %collective-permute-done.32.refs_6_ = bf16[3,32,1024]{2,1,0:T(8,128)(2,1)S(1)} collective-permute-done((bf16[3,32,1024]{2,1,0:T(8,128)(2,1)S(1)}, bf16[3,32,1024]{2,1,0:T(8,128)(2,1)S(1)}, u32[]{:S(2)}, u32[]{:S(2)}) %collective-permute-start.32) | collective-permute-done | bytes 196640 | tf_op jit(solution)/shard_map/ppermute | solution.py:295
  110.7 1.8 %shard_map.55 = (bf16[2,64,1024]{2,1,0:T(8,128)(2,1)S(1)}, bf16[2,32,1024]{2,1,0:T(8,128)(2,1)S(1)}, bf16[2,32,1024]{2,1,0:T(8,128)(2,1)S(1)}, f32[8,128]{1,0:T(8,128)S(1)}, f32[2,1024,1024]{2,1,0:T(8,128)}) custom-call(s32[1,6]{1,0:T(1,128)S(1)} %get-tuple-element.83.refs_0_, ...), custom_call_target="tpu_custom_call", output_to_operand_aliasing={{4}: (9, {})} | custom-call | flops 4000000000 | bytes 1000 | tf_op jit(solution)/shard_map/pallas_call | solution.py:222
  114.5 2.2 %shard_map.56 = (f32[8,128]{1,0:T(8,128)}, f32[2,1024,1024]{2,1,0:T(8,128)}) custom-call(s32[1,6]{1,0:T(1,128)S(1)} %get-tuple-element.83.refs_0_, bf16[2,64,1024]{2,1,0:T(8,128)(2,1)S(1)} %collective-permute-done.34.refs_1_, bf16[2,32,1024]{2,1,0:T(8,128)(2,1)S(1)} %collective-permute-done.35.refs_2_, ...), custom_call_target="tpu_custom_call", output_to_operand_aliasing={{1}: (5, {})} | custom-call | flops 4000000000 | bytes 1000 | tf_op jit(solution)/shard_map/pallas_call | solution.py:222
  (67 shorter events, 19.8 us)
Async XLA Ops:
  4.4 4.4 %collective-permute-start.2 = (bf16[1024,1024]{1,0:T(8,128)(2,1)S(1)}, bf16[1024,1024]{1,0:T(8,128)(2,1)}, u32[]{:S(2)}, u32[]{:S(2)}) collective-permute-start(bf16[1024,1024]{1,0:T(8,128)(2,1)S(1)} %convert_element_type.19.refs_4_), channel_id=1, source_target_pairs={{0,8},{8,0},{16,24},{24,16},{1,9},{9,1},{17,25},{25,17},{2,10},{10... | collective-permute-start | bytes 6291464 | tf_op jit(solution)/shard_map/ppermute | solution.py:265
  4.8 15.3 %collective-permute-start.4 = (bf16[2,4,32,1024]{3,2,1,0:T(8,128)(2,1)S(1)}, bf16[2,4,32,1024]{3,2,1,0:T(8,128)(2,1)}, u32[]{:S(2)}, u32[]{:S(2)}) collective-permute-start(bf16[2,4,32,1024]{3,2,1,0:T(8,128)(2,1)S(1)} %get-tuple-element.82.refs_7_), channel_id=1, source_target_pairs={{2,0},{4,2},{6,4},{7,6},{5,7},{3,5},{1,3},{0,1},{10,8},{12,10},{14... | collective-permute-start | bytes 1572872 | tf_op jit(solution)/shard_map/ppermute | solution.py:271
  7.5 14.3 %collective-permute-start.3 = (bf16[2,4,32,1024]{3,2,1,0:T(8,128)(2,1)S(1)}, bf16[2,4,32,1024]{3,2,1,0:T(8,128)(2,1)}, u32[]{:S(2)}, u32[]{:S(2)}) collective-permute-start(bf16[2,4,32,1024]{3,2,1,0:T(8,128)(2,1)S(1)} %get-tuple-element.81.refs_6_), channel_id=1, source_target_pairs={{0,2},{2,4},{4,6},{6,7},{7,5},{5,3},{3,1},{1,0},{8,10},{10,12},{12... | collective-permute-start | bytes 1572872 | tf_op jit(solution)/shard_map/ppermute | solution.py:271
  20.1 13.8 %collective-permute-start.6 = (bf16[2,4,32,1024]{3,2,1,0:T(8,128)(2,1)}, bf16[2,4,32,1024]{3,2,1,0:T(8,128)(2,1)S(1)}, u32[]{:S(2)}, u32[]{:S(2)}) collective-permute-start(bf16[2,4,32,1024]{3,2,1,0:T(8,128)(2,1)} %collective-permute-done.4.refs_4_), channel_id=1, source_target_pairs={{2,0},{4,2},{6,4},{7,6},{5,7},{3,5},{1,3},{0,1},{10,8},{12,10},{14... | collective-permute-start | bytes 1572872 | tf_op jit(solution)/shard_map/ppermute | solution.py:271
  21.8 13.3 %collective-permute-start.5 = (bf16[2,4,32,1024]{3,2,1,0:T(8,128)(2,1)}, bf16[2,4,32,1024]{3,2,1,0:T(8,128)(2,1)S(1)}, u32[]{:S(2)}, u32[]{:S(2)}) collective-permute-start(bf16[2,4,32,1024]{3,2,1,0:T(8,128)(2,1)} %collective-permute-done.3.refs_3_), channel_id=1, source_target_pairs={{0,2},{2,4},{4,6},{6,7},{7,5},{5,3},{3,1},{1,0},{8,10},{10,12},{12... | collective-permute-start | bytes 1572872 | tf_op jit(solution)/shard_map/ppermute | solution.py:271
  22.1 15.0 %collective-permute-start.9 = (bf16[3,64,1024]{2,1,0:T(8,128)(2,1)S(1)}, bf16[3,64,1024]{2,1,0:T(8,128)(2,1)S(1)}, u32[]{:S(2)}, u32[]{:S(2)}) collective-permute-start(bf16[3,64,1024]{2,1,0:T(8,128)(2,1)S(1)} %get-tuple-element.96), channel_id=1, source_target_pairs={{0,16},{8,24},{16,0},{24,8},{1,17},{9,25},{17,1},{25,9},{2,18},{10... | collective-permute-start | bytes 1179656 | tf_op jit(solution)/shard_map/ppermute | solution.py:295
  26.8 23.1 %collective-permute-start.12 = (bf16[3,64,1024]{2,1,0:T(8,128)(2,1)S(1)}, bf16[3,64,1024]{2,1,0:T(8,128)(2,1)S(1)}, u32[]{:S(2)}, u32[]{:S(2)}) collective-permute-start(bf16[3,64,1024]{2,1,0:T(8,128)(2,1)S(1)} %get-tuple-element.103), channel_id=1, source_target_pairs={{0,16},{8,24},{16,0},{24,8},{1,17},{9,25},{17,1},{25,9},{2,18},{10... | collective-permute-start | bytes 1179656 | tf_op jit(solution)/shard_map/ppermute | solution.py:295
  35.1 12.8 %collective-permute-start.7 = (bf16[2,4,32,1024]{3,2,1,0:T(8,128)(2,1)S(1)}, bf16[2,4,32,1024]{3,2,1,0:T(8,128)(2,1)S(1)}, u32[]{:S(2)}, u32[]{:S(2)}) collective-permute-start(bf16[2,4,32,1024]{3,2,1,0:T(8,128)(2,1)S(1)} %collective-permute-done.5.refs_3_), channel_id=1, source_target_pairs={{0,2},{2,4},{4,6},{6,7},{7,5},{5,3},{3,1},{1,0},{8,10},{10,12},{12... | collective-permute-start | bytes 1572872 | tf_op jit(solution)/shard_map/ppermute | solution.py:271
  35.7 12.2 %collective-permute-start.8 = (bf16[2,4,32,1024]{3,2,1,0:T(8,128)(2,1)S(1)}, bf16[2,4,32,1024]{3,2,1,0:T(8,128)(2,1)S(1)}, u32[]{:S(2)}, u32[]{:S(2)}) collective-permute-start(bf16[2,4,32,1024]{3,2,1,0:T(8,128)(2,1)S(1)} %collective-permute-done.6.refs_4_), channel_id=1, source_target_pairs={{2,0},{4,2},{6,4},{7,6},{5,7},{3,5},{1,3},{0,1},{10,8},{12,10},{14... | collective-permute-start | bytes 1572872 | tf_op jit(solution)/shard_map/ppermute | solution.py:271
  40.3 9.6 %collective-permute-start.13 = (bf16[2,64,1024]{2,1,0:T(8,128)(2,1)S(1)}, bf16[2,64,1024]{2,1,0:T(8,128)(2,1)S(1)}, u32[]{:S(2)}, u32[]{:S(2)}) collective-permute-start(bf16[2,64,1024]{2,1,0:T(8,128)(2,1)S(1)} %get-tuple-element.104), channel_id=1, source_target_pairs={{0,8},{8,0},{16,24},{24,16},{1,9},{9,1},{17,25},{25,17},{2,10},{10... | collective-permute-start | bytes 786440 | tf_op jit(solution)/shard_map/ppermute | solution.py:298
  40.4 24.5 %collective-permute-start.16 = (bf16[3,64,1024]{2,1,0:T(8,128)(2,1)S(1)}, bf16[3,64,1024]{2,1,0:T(8,128)(2,1)S(1)}, u32[]{:S(2)}, u32[]{:S(2)}) collective-permute-start(bf16[3,64,1024]{2,1,0:T(8,128)(2,1)S(1)} %get-tuple-element.112), channel_id=1, source_target_pairs={{0,16},{8,24},{16,0},{24,8},{1,17},{9,25},{17,1},{25,9},{2,18},{10... | collective-permute-start | bytes 1179656 | tf_op jit(solution)/shard_map/ppermute | solution.py:295
  47.9 14.1 %collective-permute-start.10 = (bf16[2,4,32,1024]{3,2,1,0:T(8,128)(2,1)S(1)}, bf16[2,4,32,1024]{3,2,1,0:T(8,128)(2,1)S(1)}, u32[]{:S(2)}, u32[]{:S(2)}) collective-permute-start(bf16[2,4,32,1024]{3,2,1,0:T(8,128)(2,1)S(1)} %collective-permute-done.7.refs_3_), channel_id=1, source_target_pairs={{0,2},{2,4},{4,6},{6,7},{7,5},{5,3},{3,1},{1,0},{8,10},{10,12},{12... | collective-permute-start | bytes 1572872 | tf_op jit(solution)/shard_map/ppermute | solution.py:271
  49.2 12.1 %collective-permute-start.11 = (bf16[2,4,32,1024]{3,2,1,0:T(8,128)(2,1)S(1)}, bf16[2,4,32,1024]{3,2,1,0:T(8,128)(2,1)S(1)}, u32[]{:S(2)}, u32[]{:S(2)}) collective-permute-start(bf16[2,4,32,1024]{3,2,1,0:T(8,128)(2,1)S(1)} %collective-permute-done.8.refs_4_), channel_id=1, source_target_pairs={{2,0},{4,2},{6,4},{7,6},{5,7},{3,5},{1,3},{0,1},{10,8},{12,10},{14... | collective-permute-start | bytes 1572872 | tf_op jit(solution)/shard_map/ppermute | solution.py:271
  53.3 11.6 %collective-permute-start.17 = (bf16[2,64,1024]{2,1,0:T(8,128)(2,1)S(1)}, bf16[2,64,1024]{2,1,0:T(8,128)(2,1)S(1)}, u32[]{:S(2)}, u32[]{:S(2)}) collective-permute-start(bf16[2,64,1024]{2,1,0:T(8,128)(2,1)S(1)} %get-tuple-element.113), channel_id=1, source_target_pairs={{0,8},{8,0},{16,24},{24,16},{1,9},{9,1},{17,25},{25,17},{2,10},{10... | collective-permute-start | bytes 786440 | tf_op jit(solution)/shard_map/ppermute | solution.py:298
  61.3 10.0 %collective-permute-start.15 = (bf16[2,4,32,1024]{3,2,1,0:T(8,128)(2,1)S(1)}, bf16[2,4,32,1024]{3,2,1,0:T(8,128)(2,1)S(1)}, u32[]{:S(2)}, u32[]{:S(2)}) collective-permute-start(bf16[2,4,32,1024]{3,2,1,0:T(8,128)(2,1)S(1)} %collective-permute-done.11.refs_4_), channel_id=1, source_target_pairs={{2,0},{4,2},{6,4},{7,6},{5,7},{3,5},{1,3},{0,1},{10,8},{12,10},{14... | collective-permute-start | bytes 1572872 | tf_op jit(solution)/shard_map/ppermute | solution.py:271
  62.0 10.2 %collective-permute-start.14 = (bf16[2,4,32,1024]{3,2,1,0:T(8,128)(2,1)S(1)}, bf16[2,4,32,1024]{3,2,1,0:T(8,128)(2,1)S(1)}, u32[]{:S(2)}, u32[]{:S(2)}) collective-permute-start(bf16[2,4,32,1024]{3,2,1,0:T(8,128)(2,1)S(1)} %collective-permute-done.10.refs_3_), channel_id=1, source_target_pairs={{0,2},{2,4},{4,6},{6,7},{7,5},{5,3},{3,1},{1,0},{8,10},{10,12},{12... | collective-permute-start | bytes 1572872 | tf_op jit(solution)/shard_map/ppermute | solution.py:271
  63.4 12.3 %collective-permute-start.20 = (bf16[3,64,1024]{2,1,0:T(8,128)(2,1)S(1)}, bf16[3,64,1024]{2,1,0:T(8,128)(2,1)S(1)}, u32[]{:S(2)}, u32[]{:S(2)}) collective-permute-start(bf16[3,64,1024]{2,1,0:T(8,128)(2,1)S(1)} %get-tuple-element.121), channel_id=1, source_target_pairs={{0,16},{8,24},{16,0},{24,8},{1,17},{9,25},{17,1},{25,9},{2,18},{10... | collective-permute-start | bytes 1179656 | tf_op jit(solution)/shard_map/ppermute | solution.py:295
  68.2 7.4 %collective-permute-start.21 = (bf16[2,64,1024]{2,1,0:T(8,128)(2,1)S(1)}, bf16[2,64,1024]{2,1,0:T(8,128)(2,1)S(1)}, u32[]{:S(2)}, u32[]{:S(2)}) collective-permute-start(bf16[2,64,1024]{2,1,0:T(8,128)(2,1)S(1)} %get-tuple-element.122), channel_id=1, source_target_pairs={{0,8},{8,0},{16,24},{24,16},{1,9},{9,1},{17,25},{25,17},{2,10},{10... | collective-permute-start | bytes 786440 | tf_op jit(solution)/shard_map/ppermute | solution.py:298
  71.3 11.4 %collective-permute-start.19 = (bf16[2,4,32,1024]{3,2,1,0:T(8,128)(2,1)S(1)}, bf16[2,4,32,1024]{3,2,1,0:T(8,128)(2,1)S(1)}, u32[]{:S(2)}, u32[]{:S(2)}) collective-permute-start(bf16[2,4,32,1024]{3,2,1,0:T(8,128)(2,1)S(1)} %collective-permute-done.15.refs_4_), channel_id=1, source_target_pairs={{2,0},{4,2},{6,4},{7,6},{5,7},{3,5},{1,3},{0,1},{10,8},{12,10},{14... | collective-permute-start | bytes 1572872 | tf_op jit(solution)/shard_map/ppermute | solution.py:271
  72.2 11.1 %collective-permute-start.18 = (bf16[2,4,32,1024]{3,2,1,0:T(8,128)(2,1)S(1)}, bf16[2,4,32,1024]{3,2,1,0:T(8,128)(2,1)S(1)}, u32[]{:S(2)}, u32[]{:S(2)}) collective-permute-start(bf16[2,4,32,1024]{3,2,1,0:T(8,128)(2,1)S(1)} %collective-permute-done.14.refs_3_), channel_id=1, source_target_pairs={{0,2},{2,4},{4,6},{6,7},{7,5},{5,3},{3,1},{1,0},{8,10},{10,12},{12... | collective-permute-start | bytes 1572872 | tf_op jit(solution)/shard_map/ppermute | solution.py:271
  73.3 12.3 %collective-permute-start.22 = (bf16[3,64,1024]{2,1,0:T(8,128)(2,1)S(1)}, bf16[3,64,1024]{2,1,0:T(8,128)(2,1)S(1)}, u32[]{:S(2)}, u32[]{:S(2)}) collective-permute-start(bf16[3,64,1024]{2,1,0:T(8,128)(2,1)S(1)} %get-tuple-element.130), channel_id=1, source_target_pairs={{0,16},{8,24},{16,0},{24,8},{1,17},{9,25},{17,1},{25,9},{2,18},{10... | collective-permute-start | bytes 1179656 | tf_op jit(solution)/shard_map/ppermute | solution.py:295
  79.0 6.6 %collective-permute-start.23 = (bf16[2,64,1024]{2,1,0:T(8,128)(2,1)S(1)}, bf16[2,64,1024]{2,1,0:T(8,128)(2,1)S(1)}, u32[]{:S(2)}, u32[]{:S(2)}) collective-permute-start(bf16[2,64,1024]{2,1,0:T(8,128)(2,1)S(1)} %get-tuple-element.131), channel_id=1, source_target_pairs={{0,8},{8,0},{16,24},{24,16},{1,9},{9,1},{17,25},{25,17},{2,10},{10... | collective-permute-start | bytes 786440 | tf_op jit(solution)/shard_map/ppermute | solution.py:298
  79.1 11.7 %collective-permute-start.27 = (bf16[3,64,1024]{2,1,0:T(8,128)(2,1)S(1)}, bf16[3,64,1024]{2,1,0:T(8,128)(2,1)S(1)}, u32[]{:S(2)}, u32[]{:S(2)}) collective-permute-start(bf16[3,64,1024]{2,1,0:T(8,128)(2,1)S(1)} %get-tuple-element.137), channel_id=1, source_target_pairs={{0,16},{8,24},{16,0},{24,8},{1,17},{9,25},{17,1},{25,9},{2,18},{10... | collective-permute-start | bytes 1179656 | tf_op jit(solution)/shard_map/ppermute | solution.py:295
  83.3 7.9 %collective-permute-start.25 = (bf16[2,4,16,1024]{3,2,1,0:T(8,128)(2,1)S(1)}, bf16[2,4,16,1024]{3,2,1,0:T(8,128)(2,1)S(1)}, u32[]{:S(2)}, u32[]{:S(2)}) collective-permute-start(bf16[2,4,16,1024]{3,2,1,0:T(8,128)(2,1)S(1)} %get-tuple-element.160), channel_id=1, source_target_pairs={{0,2},{2,4},{4,6},{6,7},{7,5},{5,3},{3,1},{1,0},{8,10},{10,12},{12... | collective-permute-start | bytes 786440 | tf_op jit(solution)/shard_map/ppermute | solution.py:271
  85.0 7.1 %collective-permute-start.26 = (bf16[2,4,16,1024]{3,2,1,0:T(8,128)(2,1)S(1)}, bf16[2,4,16,1024]{3,2,1,0:T(8,128)(2,1)S(1)}, u32[]{:S(2)}, u32[]{:S(2)}) collective-permute-start(bf16[2,4,16,1024]{3,2,1,0:T(8,128)(2,1)S(1)} %get-tuple-element.158), channel_id=1, source_target_pairs={{2,0},{4,2},{6,4},{7,6},{5,7},{3,5},{1,3},{0,1},{10,8},{12,10},{14... | collective-permute-start | bytes 786440 | tf_op jit(solution)/shard_map/ppermute | solution.py:271
  89.1 3.1 %collective-permute-start.28 = (bf16[2,64,1024]{2,1,0:T(8,128)(2,1)S(1)}, bf16[2,64,1024]{2,1,0:T(8,128)(2,1)S(1)}, u32[]{:S(2)}, u32[]{:S(2)}) collective-permute-start(bf16[2,64,1024]{2,1,0:T(8,128)(2,1)S(1)} %get-tuple-element.138), channel_id=1, source_target_pairs={{0,8},{8,0},{16,24},{24,16},{1,9},{9,1},{17,25},{25,17},{2,10},{10... | collective-permute-start | bytes 786440 | tf_op jit(solution)/shard_map/ppermute | solution.py:298
  89.2 8.8 %collective-permute-start.30 = (bf16[2,4,16,1024]{3,2,1,0:T(8,128)(2,1)S(1)}, bf16[2,4,16,1024]{3,2,1,0:T(8,128)(2,1)S(1)}, u32[]{:S(2)}, u32[]{:S(2)}) collective-permute-start(bf16[2,4,16,1024]{3,2,1,0:T(8,128)(2,1)S(1)} %get-tuple-element.159), channel_id=1, source_target_pairs={{0,2},{2,4},{4,6},{6,7},{7,5},{5,3},{3,1},{1,0},{8,10},{10,12},{12... | collective-permute-start | bytes 786440 | tf_op jit(solution)/shard_map/ppermute | solution.py:271
  90.8 8.5 %collective-permute-start.31 = (bf16[2,4,16,1024]{3,2,1,0:T(8,128)(2,1)S(1)}, bf16[2,4,16,1024]{3,2,1,0:T(8,128)(2,1)S(1)}, u32[]{:S(2)}, u32[]{:S(2)}) collective-permute-start(bf16[2,4,16,1024]{3,2,1,0:T(8,128)(2,1)S(1)} %get-tuple-element.157), channel_id=1, source_target_pairs={{2,0},{4,2},{6,4},{7,6},{5,7},{3,5},{1,3},{0,1},{10,8},{12,10},{14... | collective-permute-start | bytes 786440 | tf_op jit(solution)/shard_map/ppermute | solution.py:271
  91.2 12.0 %collective-permute-start.24 = (bf16[3,64,1024]{2,1,0:T(8,128)(2,1)S(1)}, bf16[3,64,1024]{2,1,0:T(8,128)(2,1)S(1)}, u32[]{:S(2)}, u32[]{:S(2)}) collective-permute-start(bf16[3,64,1024]{2,1,0:T(8,128)(2,1)S(1)} %get-tuple-element.135), channel_id=1, source_target_pairs={{0,16},{8,24},{16,0},{24,8},{1,17},{9,25},{17,1},{25,9},{2,18},{10... | collective-permute-start | bytes 1179656 | tf_op jit(solution)/shard_map/ppermute | solution.py:295
  94.8 12.7 %collective-permute-start.29 = (bf16[3,32,1024]{2,1,0:T(8,128)(2,1)S(1)}, bf16[3,32,1024]{2,1,0:T(8,128)(2,1)S(1)}, u32[]{:S(2)}, u32[]{:S(2)}) collective-permute-start(bf16[3,32,1024]{2,1,0:T(8,128)(2,1)S(1)} %get-tuple-element.142), channel_id=1, source_target_pairs={{0,16},{8,24},{16,0},{24,8},{1,17},{9,25},{17,1},{25,9},{2,18},{10... | collective-permute-start | bytes 589832 | tf_op jit(solution)/shard_map/ppermute | solution.py:295
  96.0 14.6 %collective-permute-start.33 = (bf16[2,64,1024]{2,1,0:T(8,128)(2,1)S(1)}, bf16[2,64,1024]{2,1,0:T(8,128)(2,1)S(1)}, u32[]{:S(2)}, u32[]{:S(2)}) collective-permute-start(bf16[2,64,1024]{2,1,0:T(8,128)(2,1)S(1)} %get-tuple-element.146), channel_id=1, source_target_pairs={{0,8},{8,0},{16,24},{24,16},{1,9},{9,1},{17,25},{25,17},{2,10},{10... | collective-permute-start | bytes 786440 | tf_op jit(solution)/shard_map/ppermute | solution.py:298
  100.8 9.8 %collective-permute-start.32 = (bf16[3,32,1024]{2,1,0:T(8,128)(2,1)S(1)}, bf16[3,32,1024]{2,1,0:T(8,128)(2,1)S(1)}, u32[]{:S(2)}, u32[]{:S(2)}) collective-permute-start(bf16[3,32,1024]{2,1,0:T(8,128)(2,1)S(1)} %get-tuple-element.145), channel_id=1, source_target_pairs={{0,16},{8,24},{16,0},{24,8},{1,17},{9,25},{17,1},{25,9},{2,18},{10... | collective-permute-start | bytes 589832 | tf_op jit(solution)/shard_map/ppermute | solution.py:295
  (8 other events, 28.7 us)

commit v3 on v2

--- a/solution.py
+++ b/solution.py
@@ -8,7 +8,7 @@
 from jax.sharding import PartitionSpec as P
 
 CAP = 2
-KERNEL_COST = 4 * 10**9
+KERNEL_COST = 3 * 10**9
 FINISH_LAG = 1
 PLACE_LAG = 0
 LANES = 128
@@ -307,16 +307,26 @@
         if step < last - 1:
             then = [send_on(x, lane[0]) for x, lane in zip(xs, lanes, strict=True)]
         else:
-            then = [[send_on(jnp.split(x, cuts, 2)[c], lane[0]) for x, lane in zip(xs, lanes, strict=True)] for c in range(cuts)]
-        call(unit, xs, len(to_finish) - FINISH_LAG, len(to_place) - PLACE_LAG)
-        xs = then
+            cut = [jnp.split(x, cuts, 2) for x in xs]
+            then = [[send_on(x[0], lane[0]) for x, lane in zip(cut, lanes, strict=True)]]
+        if step < last - 1:
+            call(unit, xs, len(to_finish) - FINISH_LAG, len(to_place) - PLACE_LAG)
+            xs = then
+        else:
+            call(unit, xs, 0, 0)
+            for c in range(1, cuts):
+                for x in cut:
+                    x[c], state["token"] = lax.optimization_barrier((x[c], state["token"]))
+                then.append([send_on(x[c], lane[0]) for x, lane in zip(cut, lanes, strict=True)])
+            xs = then
     for c in range(cuts):
         unit = [(last, turn, start + c * (rows // cuts), rows // cuts) for turn, start, rows in lanes]
         if c < cuts - 1:
             call(unit, xs[c], len(to_finish) - 1, len(to_place))
         else:
-            call(unit, xs[c], 0, 0)
-    call(None, None, len(to_finish), len(to_place))
+            call(unit, xs[c], len(to_finish) - 1, 0)
+    call(None, None, len(to_finish) - 1, len(to_place) - 1)
+    call(None, None, 1, 1)
     call(None, None, 0, len(to_place))
     return state["out"][None, None]
 

time: 117 us -> 112 us (0.957)
  waiting for transfers between devices: 52.6 us -> 43.7 us
  starting transfers between devices: 29.8 us -> 32.8 us
  Pallas kernels: 31.5 us -> 32.7 us
    ppermute x9, waiting for transfers between devices: 9.1 us -> 3.27 us  [call(): crossed[i] = lax.ppermute(got['send'], 'sector', swap_side)]
    ppermute x16, waiting for transfers between devices: 39.7 us -> 36.6 us  [send_on(): return lax.ppermute(x, 'owner', up if turn == 1 else down)]
    ppermute x9, starting transfers between devices: 10.5 us -> 12.4 us  [call(): crossed[i] = lax.ppermute(got['send'], 'sector', swap_side)]
    pallas_call x11 -> x12, Pallas kernels: 31.5 us -> 32.7 us  [step_call(): pl.pallas_call(functools.partial(step_kernel, cfg), in_specs=specs, out_s...]
  transfers between devices with their start and end apart: 37 -> 37, of which waited for: 17 -> 14; matrix products, arithmetic and copies ran while one was open for 0% -> 0% of each run, Pallas kernels for 24% -> 27%
where the time goes in v3:
time: 112 us
  waiting for transfers between devices  43.7 us (39%)
  starting transfers between devices  32.8 us (29%)
  Pallas kernels  32.7 us (29%)
  local copies, waits for them, and re-layouts  2.01 us (2%)
    ppermute x16, waiting for transfers between devices, send_on(): return lax.ppermute(x, 'owner', up if turn == 1 else down)  36.6 us
    pallas_call x12, Pallas kernels, step_call(): pl.pallas_call(functools.partial(step_kernel, cfg), in_specs=specs, out_s...  32.7 us
    ppermute x16, starting transfers between devices, send_on(): return lax.ppermute(x, 'owner', up if turn == 1 else down)  17.9 us
    ppermute x9, starting transfers between devices, call(): crossed[i] = lax.ppermute(got['send'], 'sector', swap_side)  12.4 us
    ppermute x9, waiting for transfers between devices, call(): crossed[i] = lax.ppermute(got['send'], 'sector', swap_side)  3.27 us
  transfers between devices with their start and end apart: 37, of which 14 were waited for; matrix products, arithmetic and copies ran while one was open for 0% of the time, Pallas kernels for 27%

profile of v3, /device:TPU:0, one launch (start us, length us, event | category | flops | bytes accessed | tf_op | source)
XLA Modules:
  0.0 112.1 jit_solution(7941690378249287783)
XLA Ops:
  0.0 1.8 %fusion = (bf16[4,64,1024]{2,1,0:T(8,128)(2,1)S(1)}, bf16[4,64,1024]{2,1,0:T(8,128)(2,1)S(1)}) fusion(f32[1,4,128,1024]{3,2,1,0:T(8,128)} %param.4, s32[]{:T(128)S(6)} %select_n.33, s32[]{:T(128)S(6)} %select_n.34), kind=kLoop, calls=%fused_computation.2 | loop fusion | bytes 2097160 | tf_op jit(solution)/shard_map/convert_element_type | solution.py:259
  2.4 1.5 %collective-permute-done.1 = bf16[4,64,1024]{2,1,0:T(8,128)(2,1)S(1)} collective-permute-done((bf16[4,64,1024]{2,1,0:T(8,128)(2,1)S(1)}, bf16[4,64,1024]{2,1,0:T(8,128)(2,1)S(1)}, u32[]{:S(2)}, u32[]{:S(2)}) %collective-permute-start.1) | collective-permute-done | bytes 524320 | tf_op jit(solution)/shard_map/ppermute | solution.py:258
  4.8 2.6 %collective-permute-start.4 = (bf16[2,4,32,1024]{3,2,1,0:T(8,128)(2,1)S(1)}, bf16[2,4,32,1024]{3,2,1,0:T(8,128)(2,1)}, u32[]{:S(2)}, u32[]{:S(2)}) collective-permute-start(bf16[2,4,32,1024]{3,2,1,0:T(8,128)(2,1)S(1)} %get-tuple-element.88.refs_7_), channel_id=1, source_target_pairs={{2,0},{4,2},{6,4},{7,6},{5,7},{3,5},{1,3},{0,1},{10,8},{12,10},{14... | collective-permute-start | bytes 1572872 | tf_op jit(solution)/shard_map/ppermute | solution.py:271
  8.8 3.7 %shard_map.46 = (s32[1,6]{1,0:T(1,128)S(1)}, f32[32,128]{1,0:T(8,128)S(1)}, bf16[2048,1024]{1,0:T(8,128)(2,1)S(1)}, bf16[3,64,1024]{2,1,0:T(8,128)(2,1)S(1)}, f3...) custom-call(s32[3]{0:T(128)S(1)} %pad_add_fusion.refs_0_, s32[1,4]{1,0:T(1,128)S(1)} %copy-done.1, f32[4,4]{1,0:T(4,128)S(1)} %bitcast.19, ...), custom_call_target="tpu_custom_call" | custom-call | flops 3000000000 | bytes 1000 | tf_op jit(solution)/shard_map/pallas_call | solution.py:222
  12.5 7.6 %collective-permute-done.4.refs_4_ = bf16[2,4,32,1024]{3,2,1,0:T(8,128)(2,1)} collective-permute-done((bf16[2,4,32,1024]{3,2,1,0:T(8,128)(2,1)S(1)}, bf16[2,4,32,1024]{3,2,1,0:T(8,128)(2,1)}, u32[]{:S(2)}, u32[]{:S(2)}) %collective-permute-start.4) | collective-permute-done | bytes 524320 | tf_op jit(solution)/shard_map/ppermute | solution.py:271
  20.1 1.7 %collective-permute-start.6 = (bf16[2,4,32,1024]{3,2,1,0:T(8,128)(2,1)}, bf16[2,4,32,1024]{3,2,1,0:T(8,128)(2,1)S(1)}, u32[]{:S(2)}, u32[]{:S(2)}) collective-permute-start(bf16[2,4,32,1024]{3,2,1,0:T(8,128)(2,1)} %collective-permute-done.4.refs_4_), channel_id=1, source_target_pairs={{2,0},{4,2},{6,4},{7,6},{5,7},{3,5},{1,3},{0,1},{10,8},{12,10},{14... | collective-permute-start | bytes 1572872 | tf_op jit(solution)/shard_map/ppermute | solution.py:271
  22.1 1.7 %collective-permute-start.9 = (bf16[3,64,1024]{2,1,0:T(8,128)(2,1)S(1)}, bf16[3,64,1024]{2,1,0:T(8,128)(2,1)S(1)}, u32[]{:S(2)}, u32[]{:S(2)}) collective-permute-start(bf16[3,64,1024]{2,1,0:T(8,128)(2,1)S(1)} %get-tuple-element.102), channel_id=1, source_target_pairs={{0,16},{8,24},{16,0},{24,8},{1,17},{9,25},{17,1},{25,9},{2,18},{10... | collective-permute-start | bytes 1179656 | tf_op jit(solution)/shard_map/ppermute | solution.py:295
  23.8 2.9 %shard_map.47 = (bf16[3,64,1024]{2,1,0:T(8,128)(2,1)S(1)}, f32[3,64,1024]{2,1,0:T(8,128)S(1)}, f32[8,128]{1,0:T(8,128)S(1)}) custom-call(s32[1,6]{1,0:T(1,128)S(1)} %get-tuple-element.89.refs_0_, bf16[2048,1024]{1,0:T(8,128)(2,1)S(1)} %get-tuple-element.90.refs_1_, f32[32,128]{1,0:T(8,128)S(1)} %get-tuple-element.91.refs_2_, ...), custom_call_target="tpu_custom_call" | custom-call | flops 3000000000 | bytes 1000 | tf_op jit(solution)/shard_map/pallas_call | solution.py:222
  26.8 7.2 %collective-permute-done.6.refs_4_ = bf16[2,4,32,1024]{3,2,1,0:T(8,128)(2,1)S(1)} collective-permute-done((bf16[2,4,32,1024]{3,2,1,0:T(8,128)(2,1)}, bf16[2,4,32,1024]{3,2,1,0:T(8,128)(2,1)S(1)}, u32[]{:S(2)}, u32[]{:S(2)}) %collective-permute-start.6) | collective-permute-done | bytes 524320 | tf_op jit(solution)/shard_map/ppermute | solution.py:271
  34.0 1.4 %collective-permute-start.8 = (bf16[2,4,32,1024]{3,2,1,0:T(8,128)(2,1)S(1)}, bf16[2,4,32,1024]{3,2,1,0:T(8,128)(2,1)S(1)}, u32[]{:S(2)}, u32[]{:S(2)}) collective-permute-start(bf16[2,4,32,1024]{3,2,1,0:T(8,128)(2,1)S(1)} %collective-permute-done.6.refs_4_), channel_id=1, source_target_pairs={{2,0},{4,2},{6,4},{7,6},{5,7},{3,5},{1,3},{0,1},{10,8},{12,10},{14... | collective-permute-start | bytes 1572872 | tf_op jit(solution)/shard_map/ppermute | solution.py:271
  36.0 1.4 %collective-permute-start.12 = (bf16[3,64,1024]{2,1,0:T(8,128)(2,1)S(1)}, bf16[3,64,1024]{2,1,0:T(8,128)(2,1)S(1)}, u32[]{:S(2)}, u32[]{:S(2)}) collective-permute-start(bf16[3,64,1024]{2,1,0:T(8,128)(2,1)S(1)} %get-tuple-element.109), channel_id=1, source_target_pairs={{0,16},{8,24},{16,0},{24,8},{1,17},{9,25},{17,1},{25,9},{2,18},{10... | collective-permute-start | bytes 1179656 | tf_op jit(solution)/shard_map/ppermute | solution.py:295
  37.4 3.2 %shard_map.48 = (bf16[3,64,1024]{2,1,0:T(8,128)(2,1)S(1)}, f32[3,64,1024]{2,1,0:T(8,128)S(1)}, bf16[2,64,1024]{2,1,0:T(8,128)(2,1)S(1)}, f32[8,128]{1,0:T(8,128)S(1)}, f32[2,1024,1024]{2,1,0:T(8,128)}) custom-call(s32[1,6]{1,0:T(1,128)S(1)} %get-tuple-element.89.refs_0_, bf16[2048,1024]{1,0:T(8,128)(2,1)S(1)} %get-tuple-element.90.refs_1_, ...), custom_call_target="tpu_custom_call" | custom-call | flops 3000000000 | bytes 1000 | tf_op jit(solution)/shard_map/pallas_call | solution.py:222
  40.7 6.0 %collective-permute-done.8.refs_4_ = bf16[2,4,32,1024]{3,2,1,0:T(8,128)(2,1)S(1)} collective-permute-done((bf16[2,4,32,1024]{3,2,1,0:T(8,128)(2,1)S(1)}, bf16[2,4,32,1024]{3,2,1,0:T(8,128)(2,1)S(1)}, u32[]{:S(2)}, u32[]{:S(2)}) %collective-permute-start.8) | collective-permute-done | bytes 524320 | tf_op jit(solution)/shard_map/ppermute | solution.py:271
  49.9 3.4 %shard_map.49 = (bf16[3,64,1024]{2,1,0:T(8,128)(2,1)S(1)}, f32[3,64,1024]{2,1,0:T(8,128)S(1)}, bf16[2,64,1024]{2,1,0:T(8,128)(2,1)S(1)}, f32[8,128]{1,0:T(8,128)S(1)}, f32[2,1024,1024]{2,1,0:T(8,128)}) custom-call(s32[1,6]{1,0:T(1,128)S(1)} %get-tuple-element.89.refs_0_, ...), custom_call_target="tpu_custom_call", output_to_operand_aliasing={{4}: (9, {})} | custom-call | flops 3000000000 | bytes 1000 | tf_op jit(solution)/shard_map/pallas_call | solution.py:222
  53.4 5.4 %collective-permute-done.11.refs_4_ = bf16[2,4,32,1024]{3,2,1,0:T(8,128)(2,1)S(1)} collective-permute-done((bf16[2,4,32,1024]{3,2,1,0:T(8,128)(2,1)S(1)}, bf16[2,4,32,1024]{3,2,1,0:T(8,128)(2,1)S(1)}, u32[]{:S(2)}, u32[]{:S(2)}) %collective-permute-start.11) | collective-permute-done | bytes 524320 | tf_op jit(solution)/shard_map/ppermute | solution.py:271
  62.0 3.4 %shard_map.50 = (bf16[3,64,1024]{2,1,0:T(8,128)(2,1)S(1)}, f32[3,64,1024]{2,1,0:T(8,128)S(1)}, bf16[2,64,1024]{2,1,0:T(8,128)(2,1)S(1)}, f32[8,128]{1,0:T(8,128)S(1)}, f32[2,1024,1024]{2,1,0:T(8,128)}) custom-call(s32[1,6]{1,0:T(1,128)S(1)} %get-tuple-element.89.refs_0_, ...), custom_call_target="tpu_custom_call", output_to_operand_aliasing={{4}: (9, {})} | custom-call | flops 3000000000 | bytes 1000 | tf_op jit(solution)/shard_map/pallas_call | solution.py:222
  65.4 5.4 %collective-permute-done.15.refs_4_ = bf16[2,4,32,1024]{3,2,1,0:T(8,128)(2,1)S(1)} collective-permute-done((bf16[2,4,32,1024]{3,2,1,0:T(8,128)(2,1)S(1)}, bf16[2,4,32,1024]{3,2,1,0:T(8,128)(2,1)S(1)}, u32[]{:S(2)}, u32[]{:S(2)}) %collective-permute-start.15) | collective-permute-done | bytes 524320 | tf_op jit(solution)/shard_map/ppermute | solution.py:271
  71.2 1.7 %collective-permute-start.18 = (bf16[2,4,32,1024]{3,2,1,0:T(8,128)(2,1)S(1)}, bf16[2,4,32,1024]{3,2,1,0:T(8,128)(2,1)S(1)}, u32[]{:S(2)}, u32[]{:S(2)}) collective-permute-start(bf16[2,4,32,1024]{3,2,1,0:T(8,128)(2,1)S(1)} %collective-permute-done.14.refs_3_), channel_id=1, source_target_pairs={{0,2},{2,4},{4,6},{6,7},{7,5},{5,3},{3,1},{1,0},{8,10},{10,12},{12... | collective-permute-start | bytes 1572872 | tf_op jit(solution)/shard_map/ppermute | solution.py:271
  73.9 3.4 %shard_map.51 = (bf16[3,64,1024]{2,1,0:T(8,128)(2,1)S(1)}, f32[3,64,1024]{2,1,0:T(8,128)S(1)}, bf16[2,64,1024]{2,1,0:T(8,128)(2,1)S(1)}, f32[8,128]{1,0:T(8,128)S(1)}, f32[2,1024,1024]{2,1,0:T(8,128)}) custom-call(s32[1,6]{1,0:T(1,128)S(1)} %get-tuple-element.89.refs_0_, ...), custom_call_target="tpu_custom_call", output_to_operand_aliasing={{4}: (9, {})} | custom-call | flops 3000000000 | bytes 1000 | tf_op jit(solution)/shard_map/pallas_call | solution.py:222
  78.5 2.5 %collective-permute-done.19.refs_4_ = bf16[2,4,32,1024]{3,2,1,0:T(8,128)(2,1)S(1)} collective-permute-done((bf16[2,4,32,1024]{3,2,1,0:T(8,128)(2,1)S(1)}, bf16[2,4,32,1024]{3,2,1,0:T(8,128)(2,1)S(1)}, u32[]{:S(2)}, u32[]{:S(2)}) %collective-permute-start.19) | collective-permute-done | bytes 524320 | tf_op jit(solution)/shard_map/ppermute | solution.py:271
  81.8 1.4 %collective-permute-start.22 = (bf16[2,4,16,1024]{3,2,1,0:T(8,128)(2,1)S(1)}, bf16[2,4,16,1024]{3,2,1,0:T(8,128)(2,1)S(1)}, u32[]{:S(2)}, u32[]{:S(2)}) collective-permute-start(bf16[2,4,16,1024]{3,2,1,0:T(8,128)(2,1)S(1)} %get-tuple-element.170), channel_id=1, source_target_pairs={{0,2},{2,4},{4,6},{6,7},{7,5},{5,3},{3,1},{1,0},{8,10},{10,12},{12... | collective-permute-start | bytes 786440 | tf_op jit(solution)/shard_map/ppermute | solution.py:271
  84.4 2.3 %shard_map.52 = (bf16[3,64,1024]{2,1,0:T(8,128)(2,1)S(1)}, f32[3,64,1024]{2,1,0:T(8,128)S(1)}, f32[8,128]{1,0:T(8,128)S(1)}) custom-call(s32[1,6]{1,0:T(1,128)S(1)} %get-tuple-element.89.refs_0_, bf16[2048,1024]{1,0:T(8,128)(2,1)S(1)} %get-tuple-element.90.refs_1_, f32[32,128]{1,0:T(8,128)S(1)} %get-tuple-element.91.refs_2_, ...), custom_call_target="tpu_custom_call" | custom-call | flops 3000000000 | bytes 1000 | tf_op jit(solution)/shard_map/pallas_call | solution.py:222
  86.7 1.9 %collective-permute-start.32 = (bf16[3,64,1024]{2,1,0:T(8,128)(2,1)S(1)}, bf16[3,64,1024]{2,1,0:T(8,128)(2,1)S(1)}, u32[]{:S(2)}, u32[]{:S(2)}) collective-permute-start(bf16[3,64,1024]{2,1,0:T(8,128)(2,1)S(1)} %get-tuple-element.152), channel_id=1, source_target_pairs={{0,16},{8,24},{16,0},{24,8},{1,17},{9,25},{17,1},{25,9},{2,18},{10... | collective-permute-start | bytes 1179656 | tf_op jit(solution)/shard_map/ppermute | solution.py:295
  88.6 1.5 %collective-permute-start.31 = (bf16[2,4,16,1024]{3,2,1,0:T(8,128)(2,1)S(1)}, bf16[2,4,16,1024]{3,2,1,0:T(8,128)(2,1)S(1)}, u32[]{:S(2)}, u32[]{:S(2)}) collective-permute-start(bf16[2,4,16,1024]{3,2,1,0:T(8,128)(2,1)S(1)} %get-tuple-element.150), channel_id=1, source_target_pairs={{2,0},{4,2},{6,4},{7,6},{5,7},{3,5},{1,3},{0,1},{10,8},{12,10},{14... | collective-permute-start | bytes 786440 | tf_op jit(solution)/shard_map/ppermute | solution.py:271
  91.8 2.8 %shard_map.53 = (bf16[3,32,1024]{2,1,0:T(8,128)(2,1)S(1)}, f32[3,32,1024]{2,1,0:T(8,128)S(1)}, bf16[2,64,1024]{2,1,0:T(8,128)(2,1)S(1)}, bf16[2,64,1024]{2,1,0:T...) custom-call(s32[1,6]{1,0:T(1,128)S(1)} %get-tuple-element.89.refs_0_, ...), custom_call_target="tpu_custom_call", output_to_operand_aliasing={{5}: (11, {})} | custom-call | flops 3000000000 | bytes 1000 | tf_op jit(solution)/shard_map/pallas_call | solution.py:222
  97.2 1.7 %collective-permute-done.32.refs_6_ = bf16[3,64,1024]{2,1,0:T(8,128)(2,1)S(1)} collective-permute-done((bf16[3,64,1024]{2,1,0:T(8,128)(2,1)S(1)}, bf16[3,64,1024]{2,1,0:T(8,128)(2,1)S(1)}, u32[]{:S(2)}, u32[]{:S(2)}) %collective-permute-start.32) | collective-permute-done | bytes 393248 | tf_op jit(solution)/shard_map/ppermute | solution.py:295
  98.8 2.5 %shard_map.54 = (bf16[3,32,1024]{2,1,0:T(8,128)(2,1)S(1)}, f32[3,32,1024]{2,1,0:T(8,128)S(1)}, bf16[2,64,1024]{2,1,0:T(8,128)(2,1)S(1)}, f32[8,128]{1,0:T(8,128)S(1)}, f32[2,1024,1024]{2,1,0:T(8,128)}) custom-call(s32[1,6]{1,0:T(1,128)S(1)} %get-tuple-element.89.refs_0_, ...), custom_call_target="tpu_custom_call", output_to_operand_aliasing={{4}: (8, {})} | custom-call | flops 3000000000 | bytes 1000 | tf_op jit(solution)/shard_map/pallas_call | solution.py:222
  101.3 1.9 %collective-permute-start.34 = (bf16[3,32,1024]{2,1,0:T(8,128)(2,1)S(1)}, bf16[3,32,1024]{2,1,0:T(8,128)(2,1)S(1)}, u32[]{:S(2)}, u32[]{:S(2)}) collective-permute-start(bf16[3,32,1024]{2,1,0:T(8,128)(2,1)S(1)} %get-tuple-element.159), channel_id=1, source_target_pairs={{0,16},{8,24},{16,0},{24,8},{1,17},{9,25},{17,1},{25,9},{2,18},{10... | collective-permute-start | bytes 589832 | tf_op jit(solution)/shard_map/ppermute | solution.py:295
  103.2 1.7 %shard_map.55 = (bf16[2,32,1024]{2,1,0:T(8,128)(2,1)S(1)}, f32[8,128]{1,0:T(8,128)S(1)}, f32[2,1024,1024]{2,1,0:T(8,128)}) custom-call(s32[1,6]{1,0:T(1,128)S(1)} %get-tuple-element.89.refs_0_, f32[3,32,1024]{2,1,0:T(8,128)S(1)} %get-tuple-element.145.refs_1_, ...), custom_call_target="tpu_custom_call", output_to_operand_aliasing={{2}: (6, {})} | custom-call | flops 3000000000 | bytes 1000 | tf_op jit(solution)/shard_map/pallas_call | solution.py:222
  105.5 1.6 %collective-permute-done.34.refs_2_ = bf16[3,32,1024]{2,1,0:T(8,128)(2,1)S(1)} collective-permute-done((bf16[3,32,1024]{2,1,0:T(8,128)(2,1)S(1)}, bf16[3,32,1024]{2,1,0:T(8,128)(2,1)S(1)}, u32[]{:S(2)}, u32[]{:S(2)}) %collective-permute-start.34) | collective-permute-done | bytes 196640 | tf_op jit(solution)/shard_map/ppermute | solution.py:295
  107.0 1.5 %shard_map.56 = (bf16[2,32,1024]{2,1,0:T(8,128)(2,1)S(1)}, f32[8,128]{1,0:T(8,128)S(1)}, f32[2,1024,1024]{2,1,0:T(8,128)}) custom-call(s32[1,6]{1,0:T(1,128)S(1)} %get-tuple-element.89.refs_0_, f32[3,32,1024]{2,1,0:T(8,128)S(1)} %get-tuple-element.158.refs_1_, ...), custom_call_target="tpu_custom_call", output_to_operand_aliasing={{2}: (5, {})} | custom-call | flops 3000000000 | bytes 1000 | tf_op jit(solution)/shard_map/pallas_call | solution.py:222
  109.9 2.0 %shard_map.57 = (f32[8,128]{1,0:T(8,128)}, f32[2,1024,1024]{2,1,0:T(8,128)}) custom-call(s32[1,6]{1,0:T(1,128)S(1)} %get-tuple-element.89.refs_0_, bf16[2,32,1024]{2,1,0:T(8,128)(2,1)S(1)} %collective-permute-done.33.refs_1_, bf16[2,32,1024]{2,1,0:T(8,128)(2,1)S(1)} %collective-permute-done.36.refs_2_, ...), custom_call_target="tpu_custom_call", output_to_operand_aliasing={{1}: (4, {})} | custom-call | flops 3000000000 | bytes 1000 | tf_op jit(solution)/shard_map/pallas_call | solution.py:222
  (68 shorter events, 21.1 us)
Async XLA Ops:
  4.4 4.4 %collective-permute-start.2 = (bf16[1024,1024]{1,0:T(8,128)(2,1)S(1)}, bf16[1024,1024]{1,0:T(8,128)(2,1)}, u32[]{:S(2)}, u32[]{:S(2)}) collective-permute-start(bf16[1024,1024]{1,0:T(8,128)(2,1)S(1)} %convert_element_type.19.refs_4_), channel_id=1, source_target_pairs={{0,8},{8,0},{16,24},{24,16},{1,9},{9,1},{17,25},{25,17},{2,10},{10... | collective-permute-start | bytes 6291464 | tf_op jit(solution)/shard_map/ppermute | solution.py:265
  4.8 15.3 %collective-permute-start.4 = (bf16[2,4,32,1024]{3,2,1,0:T(8,128)(2,1)S(1)}, bf16[2,4,32,1024]{3,2,1,0:T(8,128)(2,1)}, u32[]{:S(2)}, u32[]{:S(2)}) collective-permute-start(bf16[2,4,32,1024]{3,2,1,0:T(8,128)(2,1)S(1)} %get-tuple-element.88.refs_7_), channel_id=1, source_target_pairs={{2,0},{4,2},{6,4},{7,6},{5,7},{3,5},{1,3},{0,1},{10,8},{12,10},{14... | collective-permute-start | bytes 1572872 | tf_op jit(solution)/shard_map/ppermute | solution.py:271
  7.5 14.3 %collective-permute-start.3 = (bf16[2,4,32,1024]{3,2,1,0:T(8,128)(2,1)S(1)}, bf16[2,4,32,1024]{3,2,1,0:T(8,128)(2,1)}, u32[]{:S(2)}, u32[]{:S(2)}) collective-permute-start(bf16[2,4,32,1024]{3,2,1,0:T(8,128)(2,1)S(1)} %get-tuple-element.87.refs_6_), channel_id=1, source_target_pairs={{0,2},{2,4},{4,6},{6,7},{7,5},{5,3},{3,1},{1,0},{8,10},{10,12},{12... | collective-permute-start | bytes 1572872 | tf_op jit(solution)/shard_map/ppermute | solution.py:271
  20.1 13.8 %collective-permute-start.6 = (bf16[2,4,32,1024]{3,2,1,0:T(8,128)(2,1)}, bf16[2,4,32,1024]{3,2,1,0:T(8,128)(2,1)S(1)}, u32[]{:S(2)}, u32[]{:S(2)}) collective-permute-start(bf16[2,4,32,1024]{3,2,1,0:T(8,128)(2,1)} %collective-permute-done.4.refs_4_), channel_id=1, source_target_pairs={{2,0},{4,2},{6,4},{7,6},{5,7},{3,5},{1,3},{0,1},{10,8},{12,10},{14... | collective-permute-start | bytes 1572872 | tf_op jit(solution)/shard_map/ppermute | solution.py:271
  21.8 13.6 %collective-permute-start.5 = (bf16[2,4,32,1024]{3,2,1,0:T(8,128)(2,1)}, bf16[2,4,32,1024]{3,2,1,0:T(8,128)(2,1)S(1)}, u32[]{:S(2)}, u32[]{:S(2)}) collective-permute-start(bf16[2,4,32,1024]{3,2,1,0:T(8,128)(2,1)} %collective-permute-done.3.refs_3_), channel_id=1, source_target_pairs={{0,2},{2,4},{4,6},{6,7},{7,5},{5,3},{3,1},{1,0},{8,10},{10,12},{12... | collective-permute-start | bytes 1572872 | tf_op jit(solution)/shard_map/ppermute | solution.py:271
  22.1 15.3 %collective-permute-start.9 = (bf16[3,64,1024]{2,1,0:T(8,128)(2,1)S(1)}, bf16[3,64,1024]{2,1,0:T(8,128)(2,1)S(1)}, u32[]{:S(2)}, u32[]{:S(2)}) collective-permute-start(bf16[3,64,1024]{2,1,0:T(8,128)(2,1)S(1)} %get-tuple-element.102), channel_id=1, source_target_pairs={{0,16},{8,24},{16,0},{24,8},{1,17},{9,25},{17,1},{25,9},{2,18},{10... | collective-permute-start | bytes 1179656 | tf_op jit(solution)/shard_map/ppermute | solution.py:295
  34.0 12.7 %collective-permute-start.8 = (bf16[2,4,32,1024]{3,2,1,0:T(8,128)(2,1)S(1)}, bf16[2,4,32,1024]{3,2,1,0:T(8,128)(2,1)S(1)}, u32[]{:S(2)}, u32[]{:S(2)}) collective-permute-start(bf16[2,4,32,1024]{3,2,1,0:T(8,128)(2,1)S(1)} %collective-permute-done.6.refs_4_), channel_id=1, source_target_pairs={{2,0},{4,2},{6,4},{7,6},{5,7},{3,5},{1,3},{0,1},{10,8},{12,10},{14... | collective-permute-start | bytes 1572872 | tf_op jit(solution)/shard_map/ppermute | solution.py:271
  35.4 12.5 %collective-permute-start.7 = (bf16[2,4,32,1024]{3,2,1,0:T(8,128)(2,1)S(1)}, bf16[2,4,32,1024]{3,2,1,0:T(8,128)(2,1)S(1)}, u32[]{:S(2)}, u32[]{:S(2)}) collective-permute-start(bf16[2,4,32,1024]{3,2,1,0:T(8,128)(2,1)S(1)} %collective-permute-done.5.refs_3_), channel_id=1, source_target_pairs={{0,2},{2,4},{4,6},{6,7},{7,5},{5,3},{3,1},{1,0},{8,10},{10,12},{12... | collective-permute-start | bytes 1572872 | tf_op jit(solution)/shard_map/ppermute | solution.py:271
  36.0 13.9 %collective-permute-start.12 = (bf16[3,64,1024]{2,1,0:T(8,128)(2,1)S(1)}, bf16[3,64,1024]{2,1,0:T(8,128)(2,1)S(1)}, u32[]{:S(2)}, u32[]{:S(2)}) collective-permute-start(bf16[3,64,1024]{2,1,0:T(8,128)(2,1)S(1)} %get-tuple-element.109), channel_id=1, source_target_pairs={{0,16},{8,24},{16,0},{24,8},{1,17},{9,25},{17,1},{25,9},{2,18},{10... | collective-permute-start | bytes 1179656 | tf_op jit(solution)/shard_map/ppermute | solution.py:295
  40.7 9.3 %collective-permute-start.13 = (bf16[2,64,1024]{2,1,0:T(8,128)(2,1)S(1)}, bf16[2,64,1024]{2,1,0:T(8,128)(2,1)S(1)}, u32[]{:S(2)}, u32[]{:S(2)}) collective-permute-start(bf16[2,64,1024]{2,1,0:T(8,128)(2,1)S(1)} %get-tuple-element.110), channel_id=1, source_target_pairs={{0,8},{8,0},{16,24},{24,16},{1,9},{9,1},{17,25},{25,17},{2,10},{10... | collective-permute-start | bytes 786440 | tf_op jit(solution)/shard_map/ppermute | solution.py:298
  46.7 12.1 %collective-permute-start.11 = (bf16[2,4,32,1024]{3,2,1,0:T(8,128)(2,1)S(1)}, bf16[2,4,32,1024]{3,2,1,0:T(8,128)(2,1)S(1)}, u32[]{:S(2)}, u32[]{:S(2)}) collective-permute-start(bf16[2,4,32,1024]{3,2,1,0:T(8,128)(2,1)S(1)} %collective-permute-done.8.refs_4_), channel_id=1, source_target_pairs={{2,0},{4,2},{6,4},{7,6},{5,7},{3,5},{1,3},{0,1},{10,8},{12,10},{14... | collective-permute-start | bytes 1572872 | tf_op jit(solution)/shard_map/ppermute | solution.py:271
  47.9 12.1 %collective-permute-start.10 = (bf16[2,4,32,1024]{3,2,1,0:T(8,128)(2,1)S(1)}, bf16[2,4,32,1024]{3,2,1,0:T(8,128)(2,1)S(1)}, u32[]{:S(2)}, u32[]{:S(2)}) collective-permute-start(bf16[2,4,32,1024]{3,2,1,0:T(8,128)(2,1)S(1)} %collective-permute-done.7.refs_3_), channel_id=1, source_target_pairs={{0,2},{2,4},{4,6},{6,7},{7,5},{5,3},{3,1},{1,0},{8,10},{10,12},{12... | collective-permute-start | bytes 1572872 | tf_op jit(solution)/shard_map/ppermute | solution.py:271
  48.7 13.3 %collective-permute-start.16 = (bf16[3,64,1024]{2,1,0:T(8,128)(2,1)S(1)}, bf16[3,64,1024]{2,1,0:T(8,128)(2,1)S(1)}, u32[]{:S(2)}, u32[]{:S(2)}) collective-permute-start(bf16[3,64,1024]{2,1,0:T(8,128)(2,1)S(1)} %get-tuple-element.118), channel_id=1, source_target_pairs={{0,16},{8,24},{16,0},{24,8},{1,17},{9,25},{17,1},{25,9},{2,18},{10... | collective-permute-start | bytes 1179656 | tf_op jit(solution)/shard_map/ppermute | solution.py:295
  53.3 8.7 %collective-permute-start.17 = (bf16[2,64,1024]{2,1,0:T(8,128)(2,1)S(1)}, bf16[2,64,1024]{2,1,0:T(8,128)(2,1)S(1)}, u32[]{:S(2)}, u32[]{:S(2)}) collective-permute-start(bf16[2,64,1024]{2,1,0:T(8,128)(2,1)S(1)} %get-tuple-element.119), channel_id=1, source_target_pairs={{0,8},{8,0},{16,24},{24,16},{1,9},{9,1},{17,25},{25,17},{2,10},{10... | collective-permute-start | bytes 786440 | tf_op jit(solution)/shard_map/ppermute | solution.py:298
  58.8 12.1 %collective-permute-start.15 = (bf16[2,4,32,1024]{3,2,1,0:T(8,128)(2,1)S(1)}, bf16[2,4,32,1024]{3,2,1,0:T(8,128)(2,1)S(1)}, u32[]{:S(2)}, u32[]{:S(2)}) collective-permute-start(bf16[2,4,32,1024]{3,2,1,0:T(8,128)(2,1)S(1)} %collective-permute-done.11.refs_4_), channel_id=1, source_target_pairs={{2,0},{4,2},{6,4},{7,6},{5,7},{3,5},{1,3},{0,1},{10,8},{12,10},{14... | collective-permute-start | bytes 1572872 | tf_op jit(solution)/shard_map/ppermute | solution.py:271
  59.9 11.2 %collective-permute-start.14 = (bf16[2,4,32,1024]{3,2,1,0:T(8,128)(2,1)S(1)}, bf16[2,4,32,1024]{3,2,1,0:T(8,128)(2,1)S(1)}, u32[]{:S(2)}, u32[]{:S(2)}) collective-permute-start(bf16[2,4,32,1024]{3,2,1,0:T(8,128)(2,1)S(1)} %collective-permute-done.10.refs_3_), channel_id=1, source_target_pairs={{0,2},{2,4},{4,6},{6,7},{7,5},{5,3},{3,1},{1,0},{8,10},{10,12},{12... | collective-permute-start | bytes 1572872 | tf_op jit(solution)/shard_map/ppermute | solution.py:271
  60.8 13.1 %collective-permute-start.20 = (bf16[3,64,1024]{2,1,0:T(8,128)(2,1)S(1)}, bf16[3,64,1024]{2,1,0:T(8,128)(2,1)S(1)}, u32[]{:S(2)}, u32[]{:S(2)}) collective-permute-start(bf16[3,64,1024]{2,1,0:T(8,128)(2,1)S(1)} %get-tuple-element.127), channel_id=1, source_target_pairs={{0,16},{8,24},{16,0},{24,8},{1,17},{9,25},{17,1},{25,9},{2,18},{10... | collective-permute-start | bytes 1179656 | tf_op jit(solution)/shard_map/ppermute | solution.py:295
  65.4 8.5 %collective-permute-start.21 = (bf16[2,64,1024]{2,1,0:T(8,128)(2,1)S(1)}, bf16[2,64,1024]{2,1,0:T(8,128)(2,1)S(1)}, u32[]{:S(2)}, u32[]{:S(2)}) collective-permute-start(bf16[2,64,1024]{2,1,0:T(8,128)(2,1)S(1)} %get-tuple-element.128), channel_id=1, source_target_pairs={{0,8},{8,0},{16,24},{24,16},{1,9},{9,1},{17,25},{25,17},{2,10},{10... | collective-permute-start | bytes 786440 | tf_op jit(solution)/shard_map/ppermute | solution.py:298
  70.9 10.1 %collective-permute-start.19 = (bf16[2,4,32,1024]{3,2,1,0:T(8,128)(2,1)S(1)}, bf16[2,4,32,1024]{3,2,1,0:T(8,128)(2,1)S(1)}, u32[]{:S(2)}, u32[]{:S(2)}) collective-permute-start(bf16[2,4,32,1024]{3,2,1,0:T(8,128)(2,1)S(1)} %collective-permute-done.15.refs_4_), channel_id=1, source_target_pairs={{2,0},{4,2},{6,4},{7,6},{5,7},{3,5},{1,3},{0,1},{10,8},{12,10},{14... | collective-permute-start | bytes 1572872 | tf_op jit(solution)/shard_map/ppermute | solution.py:271
  71.2 10.6 %collective-permute-start.18 = (bf16[2,4,32,1024]{3,2,1,0:T(8,128)(2,1)S(1)}, bf16[2,4,32,1024]{3,2,1,0:T(8,128)(2,1)S(1)}, u32[]{:S(2)}, u32[]{:S(2)}) collective-permute-start(bf16[2,4,32,1024]{3,2,1,0:T(8,128)(2,1)S(1)} %collective-permute-done.14.refs_3_), channel_id=1, source_target_pairs={{0,2},{2,4},{4,6},{6,7},{7,5},{5,3},{3,1},{1,0},{8,10},{10,12},{12... | collective-permute-start | bytes 1572872 | tf_op jit(solution)/shard_map/ppermute | solution.py:271
  72.9 13.8 %collective-permute-start.24 = (bf16[3,64,1024]{2,1,0:T(8,128)(2,1)S(1)}, bf16[3,64,1024]{2,1,0:T(8,128)(2,1)S(1)}, u32[]{:S(2)}, u32[]{:S(2)}) collective-permute-start(bf16[3,64,1024]{2,1,0:T(8,128)(2,1)S(1)} %get-tuple-element.136), channel_id=1, source_target_pairs={{0,16},{8,24},{16,0},{24,8},{1,17},{9,25},{17,1},{25,9},{2,18},{10... | collective-permute-start | bytes 1179656 | tf_op jit(solution)/shard_map/ppermute | solution.py:295
  77.3 11.3 %collective-permute-start.26 = (bf16[2,64,1024]{2,1,0:T(8,128)(2,1)S(1)}, bf16[2,64,1024]{2,1,0:T(8,128)(2,1)S(1)}, u32[]{:S(2)}, u32[]{:S(2)}) collective-permute-start(bf16[2,64,1024]{2,1,0:T(8,128)(2,1)S(1)} %get-tuple-element.139), channel_id=1, source_target_pairs={{0,8},{8,0},{16,24},{24,16},{1,9},{9,1},{17,25},{25,17},{2,10},{10... | collective-permute-start | bytes 786440 | tf_op jit(solution)/shard_map/ppermute | solution.py:298
  77.3 12.7 %collective-permute-start.25 = (bf16[3,64,1024]{2,1,0:T(8,128)(2,1)S(1)}, bf16[3,64,1024]{2,1,0:T(8,128)(2,1)S(1)}, u32[]{:S(2)}, u32[]{:S(2)}) collective-permute-start(bf16[3,64,1024]{2,1,0:T(8,128)(2,1)S(1)} %get-tuple-element.138), channel_id=1, source_target_pairs={{0,16},{8,24},{16,0},{24,8},{1,17},{9,25},{17,1},{25,9},{2,18},{10... | collective-permute-start | bytes 1179656 | tf_op jit(solution)/shard_map/ppermute | solution.py:295
  81.8 9.3 %collective-permute-start.22 = (bf16[2,4,16,1024]{3,2,1,0:T(8,128)(2,1)S(1)}, bf16[2,4,16,1024]{3,2,1,0:T(8,128)(2,1)S(1)}, u32[]{:S(2)}, u32[]{:S(2)}) collective-permute-start(bf16[2,4,16,1024]{3,2,1,0:T(8,128)(2,1)S(1)} %get-tuple-element.170), channel_id=1, source_target_pairs={{0,2},{2,4},{4,6},{6,7},{7,5},{5,3},{3,1},{1,0},{8,10},{10,12},{12... | collective-permute-start | bytes 786440 | tf_op jit(solution)/shard_map/ppermute | solution.py:271
  83.3 8.5 %collective-permute-start.23 = (bf16[2,4,16,1024]{3,2,1,0:T(8,128)(2,1)S(1)}, bf16[2,4,16,1024]{3,2,1,0:T(8,128)(2,1)S(1)}, u32[]{:S(2)}, u32[]{:S(2)}) collective-permute-start(bf16[2,4,16,1024]{3,2,1,0:T(8,128)(2,1)S(1)} %get-tuple-element.172), channel_id=1, source_target_pairs={{2,0},{4,2},{6,4},{7,6},{5,7},{3,5},{1,3},{0,1},{10,8},{12,10},{14... | collective-permute-start | bytes 786440 | tf_op jit(solution)/shard_map/ppermute | solution.py:271
  86.7 12.1 %collective-permute-start.32 = (bf16[3,64,1024]{2,1,0:T(8,128)(2,1)S(1)}, bf16[3,64,1024]{2,1,0:T(8,128)(2,1)S(1)}, u32[]{:S(2)}, u32[]{:S(2)}) collective-permute-start(bf16[3,64,1024]{2,1,0:T(8,128)(2,1)S(1)} %get-tuple-element.152), channel_id=1, source_target_pairs={{0,16},{8,24},{16,0},{24,8},{1,17},{9,25},{17,1},{25,9},{2,18},{10... | collective-permute-start | bytes 1179656 | tf_op jit(solution)/shard_map/ppermute | solution.py:295
  88.6 7.1 %collective-permute-start.31 = (bf16[2,4,16,1024]{3,2,1,0:T(8,128)(2,1)S(1)}, bf16[2,4,16,1024]{3,2,1,0:T(8,128)(2,1)S(1)}, u32[]{:S(2)}, u32[]{:S(2)}) collective-permute-start(bf16[2,4,16,1024]{3,2,1,0:T(8,128)(2,1)S(1)} %get-tuple-element.150), channel_id=1, source_target_pairs={{2,0},{4,2},{6,4},{7,6},{5,7},{3,5},{1,3},{0,1},{10,8},{12,10},{14... | collective-permute-start | bytes 786440 | tf_op jit(solution)/shard_map/ppermute | solution.py:271
  90.1 7.1 %collective-permute-start.30 = (bf16[2,4,16,1024]{3,2,1,0:T(8,128)(2,1)S(1)}, bf16[2,4,16,1024]{3,2,1,0:T(8,128)(2,1)S(1)}, u32[]{:S(2)}, u32[]{:S(2)}) collective-permute-start(bf16[2,4,16,1024]{3,2,1,0:T(8,128)(2,1)S(1)} %get-tuple-element.149), channel_id=1, source_target_pairs={{0,2},{2,4},{4,6},{6,7},{7,5},{5,3},{3,1},{1,0},{8,10},{10,12},{12... | collective-permute-start | bytes 786440 | tf_op jit(solution)/shard_map/ppermute | solution.py:271
  94.6 8.5 %collective-permute-start.27 = (bf16[3,32,1024]{2,1,0:T(8,128)(2,1)S(1)}, bf16[3,32,1024]{2,1,0:T(8,128)(2,1)S(1)}, u32[]{:S(2)}, u32[]{:S(2)}) collective-permute-start(bf16[3,32,1024]{2,1,0:T(8,128)(2,1)S(1)} %get-tuple-element.146), channel_id=1, source_target_pairs={{0,16},{8,24},{16,0},{24,8},{1,17},{9,25},{17,1},{25,9},{2,18},{10... | collective-permute-start | bytes 589832 | tf_op jit(solution)/shard_map/ppermute | solution.py:295
  95.7 7.5 %collective-permute-start.28 = (bf16[2,64,1024]{2,1,0:T(8,128)(2,1)S(1)}, bf16[2,64,1024]{2,1,0:T(8,128)(2,1)S(1)}, u32[]{:S(2)}, u32[]{:S(2)}) collective-permute-start(bf16[2,64,1024]{2,1,0:T(8,128)(2,1)S(1)} %get-tuple-element.147), channel_id=1, source_target_pairs={{0,8},{8,0},{16,24},{24,16},{1,9},{9,1},{17,25},{25,17},{2,10},{10... | collective-permute-start | bytes 786440 | tf_op jit(solution)/shard_map/ppermute | solution.py:298
  95.7 7.5 %collective-permute-start.29 = (bf16[2,64,1024]{2,1,0:T(8,128)(2,1)S(1)}, bf16[2,64,1024]{2,1,0:T(8,128)(2,1)S(1)}, u32[]{:S(2)}, u32[]{:S(2)}) collective-permute-start(bf16[2,64,1024]{2,1,0:T(8,128)(2,1)S(1)} %get-tuple-element.148), channel_id=1, source_target_pairs={{0,8},{8,0},{16,24},{24,16},{1,9},{9,1},{17,25},{25,17},{2,10},{10... | collective-permute-start | bytes 786440 | tf_op jit(solution)/shard_map/ppermute | solution.py:298
  101.3 5.7 %collective-permute-start.34 = (bf16[3,32,1024]{2,1,0:T(8,128)(2,1)S(1)}, bf16[3,32,1024]{2,1,0:T(8,128)(2,1)S(1)}, u32[]{:S(2)}, u32[]{:S(2)}) collective-permute-start(bf16[3,32,1024]{2,1,0:T(8,128)(2,1)S(1)} %get-tuple-element.159), channel_id=1, source_target_pairs={{0,16},{8,24},{16,0},{24,8},{1,17},{9,25},{17,1},{25,9},{2,18},{10... | collective-permute-start | bytes 589832 | tf_op jit(solution)/shard_map/ppermute | solution.py:295
  (8 other events, 32.6 us)

commit v4 on v3

--- a/solution.py
+++ b/solution.py
@@ -274,7 +274,7 @@
     to_finish, to_place = [], []
     state = {"out": None, "token": None}
 
-    def call(unit, rows, n_finish, n_place):
+    def call(unit, rows, n_finish, n_place, after=()):
         finish = [to_finish.pop(0) for _ in range(max(0, n_finish))]
         place = [to_place.pop(0) for _ in range(max(0, n_place))]
         got = step_call(
@@ -284,7 +284,7 @@
             None if unit is None else (unit, rows),
             [(units[f], kept[f], crossed[f]) for f in finish],
             [(units[p], swapped[p]) for p in place],
-            [] if state["token"] is None else [state["token"]],
+            [*after] if state["token"] is None else [state["token"], *after],
         )
         common.update({name: got[name] for name in ("meta", "spread", "res") if name in got})
         state["out"], state["token"] = got.get("out", state["out"]), got["token"]
@@ -324,10 +324,11 @@
         if c < cuts - 1:
             call(unit, xs[c], len(to_finish) - 1, len(to_place))
         else:
-            call(unit, xs[c], len(to_finish) - 1, 0)
-    call(None, None, len(to_finish) - 1, len(to_place) - 1)
-    call(None, None, 1, 1)
-    call(None, None, 0, len(to_place))
+            call(unit, xs[c], 0, 0, [crossed[i] for i in to_finish[:-1]])
+    call(None, None, len(to_finish) - 1, len(to_place))
+    call(None, None, 1, 0)
+    call(None, None, 0, len(to_place) - 1)
+    call(None, None, 0, 1)
     return state["out"][None, None]
 
 

time: 112 us -> 111 us (level)
  waiting for transfers between devices: 43.7 us -> 42.2 us
    ppermute x9, waiting for transfers between devices: 1.35 us -> 0.02 us  [call(): swapped[f] = lax.ppermute(got[f'swap{j}'], 'sector', swap_core)]
    pallas_call x12 -> x13, Pallas kernels: 32.7 us -> 33.2 us  [step_call(): pl.pallas_call(functools.partial(step_kernel, cfg), in_specs=specs, out_s...]
  transfers between devices with their start and end apart: 37 -> 37, of which waited for: 14 -> 14; matrix products, arithmetic and copies ran while one was open for 0% -> 0% of each run, Pallas kernels for 27% -> 28%
where the time goes in v4:
time: 111 us
  waiting for transfers between devices  42.2 us (38%)
  Pallas kernels  33.2 us (30%)
  starting transfers between devices  32.8 us (30%)
  local copies, waits for them, and re-layouts  2.01 us (2%)
    ppermute x16, waiting for transfers between devices, send_on(): return lax.ppermute(x, 'owner', up if turn == 1 else down)  36.6 us
    pallas_call x13, Pallas kernels, step_call(): pl.pallas_call(functools.partial(step_kernel, cfg), in_specs=specs, out_s...  33.2 us
    ppermute x16, starting transfers between devices, send_on(): return lax.ppermute(x, 'owner', up if turn == 1 else down)  17.9 us
    ppermute x9, starting transfers between devices, call(): crossed[i] = lax.ppermute(got['send'], 'sector', swap_side)  12.4 us
    ppermute x9, waiting for transfers between devices, call(): crossed[i] = lax.ppermute(got['send'], 'sector', swap_side)  3.07 us
  transfers between devices with their start and end apart: 37, of which 14 were waited for; matrix products, arithmetic and copies ran while one was open for 0% of the time, Pallas kernels for 28%

profile of v4, /device:TPU:0, one launch (start us, length us, event | category | flops | bytes accessed | tf_op | source)
XLA Modules:
  0.0 111.1 jit_solution(14311237591460374214)
XLA Ops:
  0.0 1.8 %fusion = (bf16[4,64,1024]{2,1,0:T(8,128)(2,1)S(1)}, bf16[4,64,1024]{2,1,0:T(8,128)(2,1)S(1)}) fusion(f32[1,4,128,1024]{3,2,1,0:T(8,128)} %param.4, s32[]{:T(128)S(6)} %select_n.33, s32[]{:T(128)S(6)} %select_n.34), kind=kLoop, calls=%fused_computation.2 | loop fusion | bytes 2097160 | tf_op jit(solution)/shard_map/convert_element_type | solution.py:259
  2.4 1.5 %collective-permute-done.1 = bf16[4,64,1024]{2,1,0:T(8,128)(2,1)S(1)} collective-permute-done((bf16[4,64,1024]{2,1,0:T(8,128)(2,1)S(1)}, bf16[4,64,1024]{2,1,0:T(8,128)(2,1)S(1)}, u32[]{:S(2)}, u32[]{:S(2)}) %collective-permute-start.1) | collective-permute-done | bytes 524320 | tf_op jit(solution)/shard_map/ppermute | solution.py:258
  4.8 2.6 %collective-permute-start.4 = (bf16[2,4,32,1024]{3,2,1,0:T(8,128)(2,1)S(1)}, bf16[2,4,32,1024]{3,2,1,0:T(8,128)(2,1)}, u32[]{:S(2)}, u32[]{:S(2)}) collective-permute-start(bf16[2,4,32,1024]{3,2,1,0:T(8,128)(2,1)S(1)} %get-tuple-element.89.refs_7_), channel_id=1, source_target_pairs={{2,0},{4,2},{6,4},{7,6},{5,7},{3,5},{1,3},{0,1},{10,8},{12,10},{14... | collective-permute-start | bytes 1572872 | tf_op jit(solution)/shard_map/ppermute | solution.py:271
  8.8 3.7 %shard_map.46 = (s32[1,6]{1,0:T(1,128)S(1)}, f32[32,128]{1,0:T(8,128)S(1)}, bf16[2048,1024]{1,0:T(8,128)(2,1)S(1)}, bf16[3,64,1024]{2,1,0:T(8,128)(2,1)S(1)}, f3...) custom-call(s32[3]{0:T(128)S(1)} %pad_add_fusion.refs_0_, s32[1,4]{1,0:T(1,128)S(1)} %copy-done.1, f32[4,4]{1,0:T(4,128)S(1)} %bitcast.19, ...), custom_call_target="tpu_custom_call" | custom-call | flops 3000000000 | bytes 1000 | tf_op jit(solution)/shard_map/pallas_call | solution.py:222
  12.5 7.6 %collective-permute-done.4.refs_4_ = bf16[2,4,32,1024]{3,2,1,0:T(8,128)(2,1)} collective-permute-done((bf16[2,4,32,1024]{3,2,1,0:T(8,128)(2,1)S(1)}, bf16[2,4,32,1024]{3,2,1,0:T(8,128)(2,1)}, u32[]{:S(2)}, u32[]{:S(2)}) %collective-permute-start.4) | collective-permute-done | bytes 524320 | tf_op jit(solution)/shard_map/ppermute | solution.py:271
  20.1 1.7 %collective-permute-start.6 = (bf16[2,4,32,1024]{3,2,1,0:T(8,128)(2,1)}, bf16[2,4,32,1024]{3,2,1,0:T(8,128)(2,1)S(1)}, u32[]{:S(2)}, u32[]{:S(2)}) collective-permute-start(bf16[2,4,32,1024]{3,2,1,0:T(8,128)(2,1)} %collective-permute-done.4.refs_4_), channel_id=1, source_target_pairs={{2,0},{4,2},{6,4},{7,6},{5,7},{3,5},{1,3},{0,1},{10,8},{12,10},{14... | collective-permute-start | bytes 1572872 | tf_op jit(solution)/shard_map/ppermute | solution.py:271
  22.1 1.7 %collective-permute-start.9 = (bf16[3,64,1024]{2,1,0:T(8,128)(2,1)S(1)}, bf16[3,64,1024]{2,1,0:T(8,128)(2,1)S(1)}, u32[]{:S(2)}, u32[]{:S(2)}) collective-permute-start(bf16[3,64,1024]{2,1,0:T(8,128)(2,1)S(1)} %get-tuple-element.103), channel_id=1, source_target_pairs={{0,16},{8,24},{16,0},{24,8},{1,17},{9,25},{17,1},{25,9},{2,18},{10... | collective-permute-start | bytes 1179656 | tf_op jit(solution)/shard_map/ppermute | solution.py:295
  23.8 2.9 %shard_map.47 = (bf16[3,64,1024]{2,1,0:T(8,128)(2,1)S(1)}, f32[3,64,1024]{2,1,0:T(8,128)S(1)}, f32[8,128]{1,0:T(8,128)S(1)}) custom-call(s32[1,6]{1,0:T(1,128)S(1)} %get-tuple-element.90.refs_0_, bf16[2048,1024]{1,0:T(8,128)(2,1)S(1)} %get-tuple-element.91.refs_1_, f32[32,128]{1,0:T(8,128)S(1)} %get-tuple-element.92.refs_2_, ...), custom_call_target="tpu_custom_call" | custom-call | flops 3000000000 | bytes 1000 | tf_op jit(solution)/shard_map/pallas_call | solution.py:222
  26.8 7.2 %collective-permute-done.6.refs_4_ = bf16[2,4,32,1024]{3,2,1,0:T(8,128)(2,1)S(1)} collective-permute-done((bf16[2,4,32,1024]{3,2,1,0:T(8,128)(2,1)}, bf16[2,4,32,1024]{3,2,1,0:T(8,128)(2,1)S(1)}, u32[]{:S(2)}, u32[]{:S(2)}) %collective-permute-start.6) | collective-permute-done | bytes 524320 | tf_op jit(solution)/shard_map/ppermute | solution.py:271
  34.0 1.4 %collective-permute-start.8 = (bf16[2,4,32,1024]{3,2,1,0:T(8,128)(2,1)S(1)}, bf16[2,4,32,1024]{3,2,1,0:T(8,128)(2,1)S(1)}, u32[]{:S(2)}, u32[]{:S(2)}) collective-permute-start(bf16[2,4,32,1024]{3,2,1,0:T(8,128)(2,1)S(1)} %collective-permute-done.6.refs_4_), channel_id=1, source_target_pairs={{2,0},{4,2},{6,4},{7,6},{5,7},{3,5},{1,3},{0,1},{10,8},{12,10},{14... | collective-permute-start | bytes 1572872 | tf_op jit(solution)/shard_map/ppermute | solution.py:271
  36.0 1.4 %collective-permute-start.12 = (bf16[3,64,1024]{2,1,0:T(8,128)(2,1)S(1)}, bf16[3,64,1024]{2,1,0:T(8,128)(2,1)S(1)}, u32[]{:S(2)}, u32[]{:S(2)}) collective-permute-start(bf16[3,64,1024]{2,1,0:T(8,128)(2,1)S(1)} %get-tuple-element.110), channel_id=1, source_target_pairs={{0,16},{8,24},{16,0},{24,8},{1,17},{9,25},{17,1},{25,9},{2,18},{10... | collective-permute-start | bytes 1179656 | tf_op jit(solution)/shard_map/ppermute | solution.py:295
  37.4 3.2 %shard_map.48 = (bf16[3,64,1024]{2,1,0:T(8,128)(2,1)S(1)}, f32[3,64,1024]{2,1,0:T(8,128)S(1)}, bf16[2,64,1024]{2,1,0:T(8,128)(2,1)S(1)}, f32[8,128]{1,0:T(8,128)S(1)}, f32[2,1024,1024]{2,1,0:T(8,128)}) custom-call(s32[1,6]{1,0:T(1,128)S(1)} %get-tuple-element.90.refs_0_, bf16[2048,1024]{1,0:T(8,128)(2,1)S(1)} %get-tuple-element.91.refs_1_, ...), custom_call_target="tpu_custom_call" | custom-call | flops 3000000000 | bytes 1000 | tf_op jit(solution)/shard_map/pallas_call | solution.py:222
  40.7 6.0 %collective-permute-done.8.refs_4_ = bf16[2,4,32,1024]{3,2,1,0:T(8,128)(2,1)S(1)} collective-permute-done((bf16[2,4,32,1024]{3,2,1,0:T(8,128)(2,1)S(1)}, bf16[2,4,32,1024]{3,2,1,0:T(8,128)(2,1)S(1)}, u32[]{:S(2)}, u32[]{:S(2)}) %collective-permute-start.8) | collective-permute-done | bytes 524320 | tf_op jit(solution)/shard_map/ppermute | solution.py:271
  49.9 3.4 %shard_map.49 = (bf16[3,64,1024]{2,1,0:T(8,128)(2,1)S(1)}, f32[3,64,1024]{2,1,0:T(8,128)S(1)}, bf16[2,64,1024]{2,1,0:T(8,128)(2,1)S(1)}, f32[8,128]{1,0:T(8,128)S(1)}, f32[2,1024,1024]{2,1,0:T(8,128)}) custom-call(s32[1,6]{1,0:T(1,128)S(1)} %get-tuple-element.90.refs_0_, ...), custom_call_target="tpu_custom_call", output_to_operand_aliasing={{4}: (9, {})} | custom-call | flops 3000000000 | bytes 1000 | tf_op jit(solution)/shard_map/pallas_call | solution.py:222
  53.4 5.4 %collective-permute-done.11.refs_4_ = bf16[2,4,32,1024]{3,2,1,0:T(8,128)(2,1)S(1)} collective-permute-done((bf16[2,4,32,1024]{3,2,1,0:T(8,128)(2,1)S(1)}, bf16[2,4,32,1024]{3,2,1,0:T(8,128)(2,1)S(1)}, u32[]{:S(2)}, u32[]{:S(2)}) %collective-permute-start.11) | collective-permute-done | bytes 524320 | tf_op jit(solution)/shard_map/ppermute | solution.py:271
  62.0 3.4 %shard_map.50 = (bf16[3,64,1024]{2,1,0:T(8,128)(2,1)S(1)}, f32[3,64,1024]{2,1,0:T(8,128)S(1)}, bf16[2,64,1024]{2,1,0:T(8,128)(2,1)S(1)}, f32[8,128]{1,0:T(8,128)S(1)}, f32[2,1024,1024]{2,1,0:T(8,128)}) custom-call(s32[1,6]{1,0:T(1,128)S(1)} %get-tuple-element.90.refs_0_, ...), custom_call_target="tpu_custom_call", output_to_operand_aliasing={{4}: (9, {})} | custom-call | flops 3000000000 | bytes 1000 | tf_op jit(solution)/shard_map/pallas_call | solution.py:222
  65.4 5.4 %collective-permute-done.15.refs_4_ = bf16[2,4,32,1024]{3,2,1,0:T(8,128)(2,1)S(1)} collective-permute-done((bf16[2,4,32,1024]{3,2,1,0:T(8,128)(2,1)S(1)}, bf16[2,4,32,1024]{3,2,1,0:T(8,128)(2,1)S(1)}, u32[]{:S(2)}, u32[]{:S(2)}) %collective-permute-start.15) | collective-permute-done | bytes 524320 | tf_op jit(solution)/shard_map/ppermute | solution.py:271
  71.2 1.7 %collective-permute-start.18 = (bf16[2,4,32,1024]{3,2,1,0:T(8,128)(2,1)S(1)}, bf16[2,4,32,1024]{3,2,1,0:T(8,128)(2,1)S(1)}, u32[]{:S(2)}, u32[]{:S(2)}) collective-permute-start(bf16[2,4,32,1024]{3,2,1,0:T(8,128)(2,1)S(1)} %collective-permute-done.14.refs_3_), channel_id=1, source_target_pairs={{0,2},{2,4},{4,6},{6,7},{7,5},{5,3},{3,1},{1,0},{8,10},{10,12},{12... | collective-permute-start | bytes 1572872 | tf_op jit(solution)/shard_map/ppermute | solution.py:271
  73.9 3.4 %shard_map.51 = (bf16[3,64,1024]{2,1,0:T(8,128)(2,1)S(1)}, f32[3,64,1024]{2,1,0:T(8,128)S(1)}, bf16[2,64,1024]{2,1,0:T(8,128)(2,1)S(1)}, f32[8,128]{1,0:T(8,128)S(1)}, f32[2,1024,1024]{2,1,0:T(8,128)}) custom-call(s32[1,6]{1,0:T(1,128)S(1)} %get-tuple-element.90.refs_0_, ...), custom_call_target="tpu_custom_call", output_to_operand_aliasing={{4}: (9, {})} | custom-call | flops 3000000000 | bytes 1000 | tf_op jit(solution)/shard_map/pallas_call | solution.py:222
  78.5 2.5 %collective-permute-done.19.refs_4_ = bf16[2,4,32,1024]{3,2,1,0:T(8,128)(2,1)S(1)} collective-permute-done((bf16[2,4,32,1024]{3,2,1,0:T(8,128)(2,1)S(1)}, bf16[2,4,32,1024]{3,2,1,0:T(8,128)(2,1)S(1)}, u32[]{:S(2)}, u32[]{:S(2)}) %collective-permute-start.19) | collective-permute-done | bytes 524320 | tf_op jit(solution)/shard_map/ppermute | solution.py:271
  81.8 1.4 %collective-permute-start.24 = (bf16[2,4,16,1024]{3,2,1,0:T(8,128)(2,1)S(1)}, bf16[2,4,16,1024]{3,2,1,0:T(8,128)(2,1)S(1)}, u32[]{:S(2)}, u32[]{:S(2)}) collective-permute-start(bf16[2,4,16,1024]{3,2,1,0:T(8,128)(2,1)S(1)} %get-tuple-element.173), channel_id=1, source_target_pairs={{0,2},{2,4},{4,6},{6,7},{7,5},{5,3},{3,1},{1,0},{8,10},{10,12},{12... | collective-permute-start | bytes 786440 | tf_op jit(solution)/shard_map/ppermute | solution.py:271
  84.4 2.3 %shard_map.52 = (bf16[3,64,1024]{2,1,0:T(8,128)(2,1)S(1)}, f32[3,64,1024]{2,1,0:T(8,128)S(1)}, f32[8,128]{1,0:T(8,128)S(1)}) custom-call(s32[1,6]{1,0:T(1,128)S(1)} %get-tuple-element.90.refs_0_, bf16[2048,1024]{1,0:T(8,128)(2,1)S(1)} %get-tuple-element.91.refs_1_, f32[32,128]{1,0:T(8,128)S(1)} %get-tuple-element.92.refs_2_, ...), custom_call_target="tpu_custom_call" | custom-call | flops 3000000000 | bytes 1000 | tf_op jit(solution)/shard_map/pallas_call | solution.py:222
  86.7 1.9 %collective-permute-start.29 = (bf16[3,64,1024]{2,1,0:T(8,128)(2,1)S(1)}, bf16[3,64,1024]{2,1,0:T(8,128)(2,1)S(1)}, u32[]{:S(2)}, u32[]{:S(2)}) collective-permute-start(bf16[3,64,1024]{2,1,0:T(8,128)(2,1)S(1)} %get-tuple-element.149), channel_id=1, source_target_pairs={{0,16},{8,24},{16,0},{24,8},{1,17},{9,25},{17,1},{25,9},{2,18},{10... | collective-permute-start | bytes 1179656 | tf_op jit(solution)/shard_map/ppermute | solution.py:295
  88.6 1.5 %collective-permute-start.23 = (bf16[2,4,16,1024]{3,2,1,0:T(8,128)(2,1)S(1)}, bf16[2,4,16,1024]{3,2,1,0:T(8,128)(2,1)S(1)}, u32[]{:S(2)}, u32[]{:S(2)}) collective-permute-start(bf16[2,4,16,1024]{3,2,1,0:T(8,128)(2,1)S(1)} %get-tuple-element.140), channel_id=1, source_target_pairs={{2,0},{4,2},{6,4},{7,6},{5,7},{3,5},{1,3},{0,1},{10,8},{12,10},{14... | collective-permute-start | bytes 786440 | tf_op jit(solution)/shard_map/ppermute | solution.py:271
  91.8 2.8 %shard_map.53 = (bf16[3,32,1024]{2,1,0:T(8,128)(2,1)S(1)}, f32[3,32,1024]{2,1,0:T(8,128)S(1)}, bf16[2,64,1024]{2,1,0:T(8,128)(2,1)S(1)}, bf16[2,64,1024]{2,1,0:T...) custom-call(s32[1,6]{1,0:T(1,128)S(1)} %get-tuple-element.90.refs_0_, ...), custom_call_target="tpu_custom_call", output_to_operand_aliasing={{5}: (11, {})} | custom-call | flops 3000000000 | bytes 1000 | tf_op jit(solution)/shard_map/pallas_call | solution.py:222
  97.2 1.7 %collective-permute-done.29.refs_6_.refs_2_ = bf16[3,64,1024]{2,1,0:T(8,128)(2,1)S(1)} collective-permute-done((bf16[3,64,1024]{2,1,0:T(8,128)(2,1)S(1)}, bf16[3,64,1024]{2,1,0:T(8,128)(2,1)S(1)}, u32[]{:S(2)}, u32[]{:S(2)}) %collective-permute-start.29) | collective-permute-done | bytes 393248 | tf_op jit(solution)/shard_map/ppermute | solution.py:295
  98.8 1.6 %shard_map.54 = (bf16[3,32,1024]{2,1,0:T(8,128)(2,1)S(1)}, f32[3,32,1024]{2,1,0:T(8,128)S(1)}, f32[8,128]{1,0:T(8,128)S(1)}) custom-call(s32[1,6]{1,0:T(1,128)S(1)} %get-tuple-element.90.refs_0_, bf16[2048,1024]{1,0:T(8,128)(2,1)S(1)} %get-tuple-element.91.refs_1_, f32[32,128]{1,0:T(8,128)S(1)} %get-tuple-element.92.refs_2_, ...), custom_call_target="tpu_custom_call" | custom-call | flops 3000000000 | bytes 1000 | tf_op jit(solution)/shard_map/pallas_call | solution.py:222
  100.4 1.9 %collective-permute-start.30 = (bf16[3,32,1024]{2,1,0:T(8,128)(2,1)S(1)}, bf16[3,32,1024]{2,1,0:T(8,128)(2,1)S(1)}, u32[]{:S(2)}, u32[]{:S(2)}) collective-permute-start(bf16[3,32,1024]{2,1,0:T(8,128)(2,1)S(1)} %get-tuple-element.151), channel_id=1, source_target_pairs={{0,16},{8,24},{16,0},{24,8},{1,17},{9,25},{17,1},{25,9},{2,18},{10... | collective-permute-start | bytes 589832 | tf_op jit(solution)/shard_map/ppermute | solution.py:295
  102.8 1.9 %shard_map.55 = (bf16[2,64,1024]{2,1,0:T(8,128)(2,1)S(1)}, bf16[2,32,1024]{2,1,0:T(8,128)(2,1)S(1)}, f32[8,128]{1,0:T(8,128)S(1)}, f32[2,1024,1024]{2,1,0:T(8,128)}) custom-call(s32[1,6]{1,0:T(1,128)S(1)} %get-tuple-element.90.refs_0_, f32[3,64,1024]{2,1,0:T(8,128)S(1)} %get-tuple-element.152.refs_1_, ...), custom_call_target="tpu_custom_call", output_to_operand_aliasing={{3}: (8, {})} | custom-call | flops 3000000000 | bytes 1000 | tf_op jit(solution)/shard_map/pallas_call | solution.py:222
  106.1 1.3 %shard_map.56 = (bf16[2,32,1024]{2,1,0:T(8,128)(2,1)S(1)}, f32[8,128]{1,0:T(8,128)S(1)}, f32[2,1024,1024]{2,1,0:T(8,128)}) custom-call(s32[1,6]{1,0:T(1,128)S(1)} %get-tuple-element.90.refs_0_, f32[3,32,1024]{2,1,0:T(8,128)S(1)} %get-tuple-element.150.refs_1_, ...), custom_call_target="tpu_custom_call", output_to_operand_aliasing={{2}: (4, {})} | custom-call | flops 3000000000 | bytes 1000 | tf_op jit(solution)/shard_map/pallas_call | solution.py:222
  107.5 1.5 %shard_map.57 = (f32[8,128]{1,0:T(8,128)S(1)}, f32[2,1024,1024]{2,1,0:T(8,128)}) custom-call(s32[1,6]{1,0:T(1,128)S(1)} %get-tuple-element.90.refs_0_, bf16[2,64,1024]{2,1,0:T(8,128)(2,1)S(1)} %collective-permute-done.35.refs_1_, bf16[2,32,1024]{2,1,0:T(8,128)(2,1)S(1)} %collective-permute-done.36.refs_2_, ...), custom_call_target="tpu_custom_call", output_to_operand_aliasing={{1}: (4, {})} | custom-call | flops 3000000000 | bytes 1000 | tf_op jit(solution)/shard_map/pallas_call | solution.py:222
  109.0 1.9 %shard_map.58 = (f32[8,128]{1,0:T(8,128)}, f32[2,1024,1024]{2,1,0:T(8,128)}) custom-call(s32[1,6]{1,0:T(1,128)S(1)} %get-tuple-element.90.refs_0_, bf16[2,32,1024]{2,1,0:T(8,128)(2,1)S(1)} %collective-permute-done.34.refs_1_, f32[8,128]{1,0:T(8,128)S(1)} %get-tuple-element.166.refs_2_, ...), custom_call_target="tpu_custom_call", output_to_operand_aliasing={{1}: (3, {})} | custom-call | flops 3000000000 | bytes 1000 | tf_op jit(solution)/shard_map/pallas_call | solution.py:222
  (69 shorter events, 21.1 us)
Async XLA Ops:
  4.4 4.4 %collective-permute-start.2 = (bf16[1024,1024]{1,0:T(8,128)(2,1)S(1)}, bf16[1024,1024]{1,0:T(8,128)(2,1)}, u32[]{:S(2)}, u32[]{:S(2)}) collective-permute-start(bf16[1024,1024]{1,0:T(8,128)(2,1)S(1)} %convert_element_type.19.refs_4_), channel_id=1, source_target_pairs={{0,8},{8,0},{16,24},{24,16},{1,9},{9,1},{17,25},{25,17},{2,10},{10... | collective-permute-start | bytes 6291464 | tf_op jit(solution)/shard_map/ppermute | solution.py:265
  4.8 15.3 %collective-permute-start.4 = (bf16[2,4,32,1024]{3,2,1,0:T(8,128)(2,1)S(1)}, bf16[2,4,32,1024]{3,2,1,0:T(8,128)(2,1)}, u32[]{:S(2)}, u32[]{:S(2)}) collective-permute-start(bf16[2,4,32,1024]{3,2,1,0:T(8,128)(2,1)S(1)} %get-tuple-element.89.refs_7_), channel_id=1, source_target_pairs={{2,0},{4,2},{6,4},{7,6},{5,7},{3,5},{1,3},{0,1},{10,8},{12,10},{14... | collective-permute-start | bytes 1572872 | tf_op jit(solution)/shard_map/ppermute | solution.py:271
  7.5 14.3 %collective-permute-start.3 = (bf16[2,4,32,1024]{3,2,1,0:T(8,128)(2,1)S(1)}, bf16[2,4,32,1024]{3,2,1,0:T(8,128)(2,1)}, u32[]{:S(2)}, u32[]{:S(2)}) collective-permute-start(bf16[2,4,32,1024]{3,2,1,0:T(8,128)(2,1)S(1)} %get-tuple-element.88.refs_6_), channel_id=1, source_target_pairs={{0,2},{2,4},{4,6},{6,7},{7,5},{5,3},{3,1},{1,0},{8,10},{10,12},{12... | collective-permute-start | bytes 1572872 | tf_op jit(solution)/shard_map/ppermute | solution.py:271
  20.1 13.8 %collective-permute-start.6 = (bf16[2,4,32,1024]{3,2,1,0:T(8,128)(2,1)}, bf16[2,4,32,1024]{3,2,1,0:T(8,128)(2,1)S(1)}, u32[]{:S(2)}, u32[]{:S(2)}) collective-permute-start(bf16[2,4,32,1024]{3,2,1,0:T(8,128)(2,1)} %collective-permute-done.4.refs_4_), channel_id=1, source_target_pairs={{2,0},{4,2},{6,4},{7,6},{5,7},{3,5},{1,3},{0,1},{10,8},{12,10},{14... | collective-permute-start | bytes 1572872 | tf_op jit(solution)/shard_map/ppermute | solution.py:271
  21.8 13.6 %collective-permute-start.5 = (bf16[2,4,32,1024]{3,2,1,0:T(8,128)(2,1)}, bf16[2,4,32,1024]{3,2,1,0:T(8,128)(2,1)S(1)}, u32[]{:S(2)}, u32[]{:S(2)}) collective-permute-start(bf16[2,4,32,1024]{3,2,1,0:T(8,128)(2,1)} %collective-permute-done.3.refs_3_), channel_id=1, source_target_pairs={{0,2},{2,4},{4,6},{6,7},{7,5},{5,3},{3,1},{1,0},{8,10},{10,12},{12... | collective-permute-start | bytes 1572872 | tf_op jit(solution)/shard_map/ppermute | solution.py:271
  22.1 15.3 %collective-permute-start.9 = (bf16[3,64,1024]{2,1,0:T(8,128)(2,1)S(1)}, bf16[3,64,1024]{2,1,0:T(8,128)(2,1)S(1)}, u32[]{:S(2)}, u32[]{:S(2)}) collective-permute-start(bf16[3,64,1024]{2,1,0:T(8,128)(2,1)S(1)} %get-tuple-element.103), channel_id=1, source_target_pairs={{0,16},{8,24},{16,0},{24,8},{1,17},{9,25},{17,1},{25,9},{2,18},{10... | collective-permute-start | bytes 1179656 | tf_op jit(solution)/shard_map/ppermute | solution.py:295
  34.0 12.7 %collective-permute-start.8 = (bf16[2,4,32,1024]{3,2,1,0:T(8,128)(2,1)S(1)}, bf16[2,4,32,1024]{3,2,1,0:T(8,128)(2,1)S(1)}, u32[]{:S(2)}, u32[]{:S(2)}) collective-permute-start(bf16[2,4,32,1024]{3,2,1,0:T(8,128)(2,1)S(1)} %collective-permute-done.6.refs_4_), channel_id=1, source_target_pairs={{2,0},{4,2},{6,4},{7,6},{5,7},{3,5},{1,3},{0,1},{10,8},{12,10},{14... | collective-permute-start | bytes 1572872 | tf_op jit(solution)/shard_map/ppermute | solution.py:271
  35.4 12.5 %collective-permute-start.7 = (bf16[2,4,32,1024]{3,2,1,0:T(8,128)(2,1)S(1)}, bf16[2,4,32,1024]{3,2,1,0:T(8,128)(2,1)S(1)}, u32[]{:S(2)}, u32[]{:S(2)}) collective-permute-start(bf16[2,4,32,1024]{3,2,1,0:T(8,128)(2,1)S(1)} %collective-permute-done.5.refs_3_), channel_id=1, source_target_pairs={{0,2},{2,4},{4,6},{6,7},{7,5},{5,3},{3,1},{1,0},{8,10},{10,12},{12... | collective-permute-start | bytes 1572872 | tf_op jit(solution)/shard_map/ppermute | solution.py:271
  36.0 13.9 %collective-permute-start.12 = (bf16[3,64,1024]{2,1,0:T(8,128)(2,1)S(1)}, bf16[3,64,1024]{2,1,0:T(8,128)(2,1)S(1)}, u32[]{:S(2)}, u32[]{:S(2)}) collective-permute-start(bf16[3,64,1024]{2,1,0:T(8,128)(2,1)S(1)} %get-tuple-element.110), channel_id=1, source_target_pairs={{0,16},{8,24},{16,0},{24,8},{1,17},{9,25},{17,1},{25,9},{2,18},{10... | collective-permute-start | bytes 1179656 | tf_op jit(solution)/shard_map/ppermute | solution.py:295
  40.6 9.3 %collective-permute-start.13 = (bf16[2,64,1024]{2,1,0:T(8,128)(2,1)S(1)}, bf16[2,64,1024]{2,1,0:T(8,128)(2,1)S(1)}, u32[]{:S(2)}, u32[]{:S(2)}) collective-permute-start(bf16[2,64,1024]{2,1,0:T(8,128)(2,1)S(1)} %get-tuple-element.111), channel_id=1, source_target_pairs={{0,8},{8,0},{16,24},{24,16},{1,9},{9,1},{17,25},{25,17},{2,10},{10... | collective-permute-start | bytes 786440 | tf_op jit(solution)/shard_map/ppermute | solution.py:298
  46.7 12.1 %collective-permute-start.11 = (bf16[2,4,32,1024]{3,2,1,0:T(8,128)(2,1)S(1)}, bf16[2,4,32,1024]{3,2,1,0:T(8,128)(2,1)S(1)}, u32[]{:S(2)}, u32[]{:S(2)}) collective-permute-start(bf16[2,4,32,1024]{3,2,1,0:T(8,128)(2,1)S(1)} %collective-permute-done.8.refs_4_), channel_id=1, source_target_pairs={{2,0},{4,2},{6,4},{7,6},{5,7},{3,5},{1,3},{0,1},{10,8},{12,10},{14... | collective-permute-start | bytes 1572872 | tf_op jit(solution)/shard_map/ppermute | solution.py:271
  47.9 12.1 %collective-permute-start.10 = (bf16[2,4,32,1024]{3,2,1,0:T(8,128)(2,1)S(1)}, bf16[2,4,32,1024]{3,2,1,0:T(8,128)(2,1)S(1)}, u32[]{:S(2)}, u32[]{:S(2)}) collective-permute-start(bf16[2,4,32,1024]{3,2,1,0:T(8,128)(2,1)S(1)} %collective-permute-done.7.refs_3_), channel_id=1, source_target_pairs={{0,2},{2,4},{4,6},{6,7},{7,5},{5,3},{3,1},{1,0},{8,10},{10,12},{12... | collective-permute-start | bytes 1572872 | tf_op jit(solution)/shard_map/ppermute | solution.py:271
  48.7 13.3 %collective-permute-start.16 = (bf16[3,64,1024]{2,1,0:T(8,128)(2,1)S(1)}, bf16[3,64,1024]{2,1,0:T(8,128)(2,1)S(1)}, u32[]{:S(2)}, u32[]{:S(2)}) collective-permute-start(bf16[3,64,1024]{2,1,0:T(8,128)(2,1)S(1)} %get-tuple-element.119), channel_id=1, source_target_pairs={{0,16},{8,24},{16,0},{24,8},{1,17},{9,25},{17,1},{25,9},{2,18},{10... | collective-permute-start | bytes 1179656 | tf_op jit(solution)/shard_map/ppermute | solution.py:295
  53.3 8.7 %collective-permute-start.17 = (bf16[2,64,1024]{2,1,0:T(8,128)(2,1)S(1)}, bf16[2,64,1024]{2,1,0:T(8,128)(2,1)S(1)}, u32[]{:S(2)}, u32[]{:S(2)}) collective-permute-start(bf16[2,64,1024]{2,1,0:T(8,128)(2,1)S(1)} %get-tuple-element.120), channel_id=1, source_target_pairs={{0,8},{8,0},{16,24},{24,16},{1,9},{9,1},{17,25},{25,17},{2,10},{10... | collective-permute-start | bytes 786440 | tf_op jit(solution)/shard_map/ppermute | solution.py:298
  58.8 12.1 %collective-permute-start.15 = (bf16[2,4,32,1024]{3,2,1,0:T(8,128)(2,1)S(1)}, bf16[2,4,32,1024]{3,2,1,0:T(8,128)(2,1)S(1)}, u32[]{:S(2)}, u32[]{:S(2)}) collective-permute-start(bf16[2,4,32,1024]{3,2,1,0:T(8,128)(2,1)S(1)} %collective-permute-done.11.refs_4_), channel_id=1, source_target_pairs={{2,0},{4,2},{6,4},{7,6},{5,7},{3,5},{1,3},{0,1},{10,8},{12,10},{14... | collective-permute-start | bytes 1572872 | tf_op jit(solution)/shard_map/ppermute | solution.py:271
  59.9 11.2 %collective-permute-start.14 = (bf16[2,4,32,1024]{3,2,1,0:T(8,128)(2,1)S(1)}, bf16[2,4,32,1024]{3,2,1,0:T(8,128)(2,1)S(1)}, u32[]{:S(2)}, u32[]{:S(2)}) collective-permute-start(bf16[2,4,32,1024]{3,2,1,0:T(8,128)(2,1)S(1)} %collective-permute-done.10.refs_3_), channel_id=1, source_target_pairs={{0,2},{2,4},{4,6},{6,7},{7,5},{5,3},{3,1},{1,0},{8,10},{10,12},{12... | collective-permute-start | bytes 1572872 | tf_op jit(solution)/shard_map/ppermute | solution.py:271
  60.8 13.1 %collective-permute-start.20 = (bf16[3,64,1024]{2,1,0:T(8,128)(2,1)S(1)}, bf16[3,64,1024]{2,1,0:T(8,128)(2,1)S(1)}, u32[]{:S(2)}, u32[]{:S(2)}) collective-permute-start(bf16[3,64,1024]{2,1,0:T(8,128)(2,1)S(1)} %get-tuple-element.128), channel_id=1, source_target_pairs={{0,16},{8,24},{16,0},{24,8},{1,17},{9,25},{17,1},{25,9},{2,18},{10... | collective-permute-start | bytes 1179656 | tf_op jit(solution)/shard_map/ppermute | solution.py:295
  65.4 8.5 %collective-permute-start.21 = (bf16[2,64,1024]{2,1,0:T(8,128)(2,1)S(1)}, bf16[2,64,1024]{2,1,0:T(8,128)(2,1)S(1)}, u32[]{:S(2)}, u32[]{:S(2)}) collective-permute-start(bf16[2,64,1024]{2,1,0:T(8,128)(2,1)S(1)} %get-tuple-element.129), channel_id=1, source_target_pairs={{0,8},{8,0},{16,24},{24,16},{1,9},{9,1},{17,25},{25,17},{2,10},{10... | collective-permute-start | bytes 786440 | tf_op jit(solution)/shard_map/ppermute | solution.py:298
  70.9 10.1 %collective-permute-start.19 = (bf16[2,4,32,1024]{3,2,1,0:T(8,128)(2,1)S(1)}, bf16[2,4,32,1024]{3,2,1,0:T(8,128)(2,1)S(1)}, u32[]{:S(2)}, u32[]{:S(2)}) collective-permute-start(bf16[2,4,32,1024]{3,2,1,0:T(8,128)(2,1)S(1)} %collective-permute-done.15.refs_4_), channel_id=1, source_target_pairs={{2,0},{4,2},{6,4},{7,6},{5,7},{3,5},{1,3},{0,1},{10,8},{12,10},{14... | collective-permute-start | bytes 1572872 | tf_op jit(solution)/shard_map/ppermute | solution.py:271
  71.2 10.6 %collective-permute-start.18 = (bf16[2,4,32,1024]{3,2,1,0:T(8,128)(2,1)S(1)}, bf16[2,4,32,1024]{3,2,1,0:T(8,128)(2,1)S(1)}, u32[]{:S(2)}, u32[]{:S(2)}) collective-permute-start(bf16[2,4,32,1024]{3,2,1,0:T(8,128)(2,1)S(1)} %collective-permute-done.14.refs_3_), channel_id=1, source_target_pairs={{0,2},{2,4},{4,6},{6,7},{7,5},{5,3},{3,1},{1,0},{8,10},{10,12},{12... | collective-permute-start | bytes 1572872 | tf_op jit(solution)/shard_map/ppermute | solution.py:271
  72.9 13.8 %collective-permute-start.26 = (bf16[3,64,1024]{2,1,0:T(8,128)(2,1)S(1)}, bf16[3,64,1024]{2,1,0:T(8,128)(2,1)S(1)}, u32[]{:S(2)}, u32[]{:S(2)}) collective-permute-start(bf16[3,64,1024]{2,1,0:T(8,128)(2,1)S(1)} %get-tuple-element.142), channel_id=1, source_target_pairs={{0,16},{8,24},{16,0},{24,8},{1,17},{9,25},{17,1},{25,9},{2,18},{10... | collective-permute-start | bytes 1179656 | tf_op jit(solution)/shard_map/ppermute | solution.py:295
  77.3 11.3 %collective-permute-start.28 = (bf16[2,64,1024]{2,1,0:T(8,128)(2,1)S(1)}, bf16[2,64,1024]{2,1,0:T(8,128)(2,1)S(1)}, u32[]{:S(2)}, u32[]{:S(2)}) collective-permute-start(bf16[2,64,1024]{2,1,0:T(8,128)(2,1)S(1)} %get-tuple-element.145), channel_id=1, source_target_pairs={{0,8},{8,0},{16,24},{24,16},{1,9},{9,1},{17,25},{25,17},{2,10},{10... | collective-permute-start | bytes 786440 | tf_op jit(solution)/shard_map/ppermute | solution.py:298
  77.4 12.7 %collective-permute-start.27 = (bf16[3,64,1024]{2,1,0:T(8,128)(2,1)S(1)}, bf16[3,64,1024]{2,1,0:T(8,128)(2,1)S(1)}, u32[]{:S(2)}, u32[]{:S(2)}) collective-permute-start(bf16[3,64,1024]{2,1,0:T(8,128)(2,1)S(1)} %get-tuple-element.144), channel_id=1, source_target_pairs={{0,16},{8,24},{16,0},{24,8},{1,17},{9,25},{17,1},{25,9},{2,18},{10... | collective-permute-start | bytes 1179656 | tf_op jit(solution)/shard_map/ppermute | solution.py:295
  81.8 9.3 %collective-permute-start.24 = (bf16[2,4,16,1024]{3,2,1,0:T(8,128)(2,1)S(1)}, bf16[2,4,16,1024]{3,2,1,0:T(8,128)(2,1)S(1)}, u32[]{:S(2)}, u32[]{:S(2)}) collective-permute-start(bf16[2,4,16,1024]{3,2,1,0:T(8,128)(2,1)S(1)} %get-tuple-element.173), channel_id=1, source_target_pairs={{0,2},{2,4},{4,6},{6,7},{7,5},{5,3},{3,1},{1,0},{8,10},{10,12},{12... | collective-permute-start | bytes 786440 | tf_op jit(solution)/shard_map/ppermute | solution.py:271
  83.3 8.5 %collective-permute-start.25 = (bf16[2,4,16,1024]{3,2,1,0:T(8,128)(2,1)S(1)}, bf16[2,4,16,1024]{3,2,1,0:T(8,128)(2,1)S(1)}, u32[]{:S(2)}, u32[]{:S(2)}) collective-permute-start(bf16[2,4,16,1024]{3,2,1,0:T(8,128)(2,1)S(1)} %get-tuple-element.171), channel_id=1, source_target_pairs={{2,0},{4,2},{6,4},{7,6},{5,7},{3,5},{1,3},{0,1},{10,8},{12,10},{14... | collective-permute-start | bytes 786440 | tf_op jit(solution)/shard_map/ppermute | solution.py:271
  86.7 12.1 %collective-permute-start.29 = (bf16[3,64,1024]{2,1,0:T(8,128)(2,1)S(1)}, bf16[3,64,1024]{2,1,0:T(8,128)(2,1)S(1)}, u32[]{:S(2)}, u32[]{:S(2)}) collective-permute-start(bf16[3,64,1024]{2,1,0:T(8,128)(2,1)S(1)} %get-tuple-element.149), channel_id=1, source_target_pairs={{0,16},{8,24},{16,0},{24,8},{1,17},{9,25},{17,1},{25,9},{2,18},{10... | collective-permute-start | bytes 1179656 | tf_op jit(solution)/shard_map/ppermute | solution.py:295
  88.6 7.1 %collective-permute-start.23 = (bf16[2,4,16,1024]{3,2,1,0:T(8,128)(2,1)S(1)}, bf16[2,4,16,1024]{3,2,1,0:T(8,128)(2,1)S(1)}, u32[]{:S(2)}, u32[]{:S(2)}) collective-permute-start(bf16[2,4,16,1024]{3,2,1,0:T(8,128)(2,1)S(1)} %get-tuple-element.140), channel_id=1, source_target_pairs={{2,0},{4,2},{6,4},{7,6},{5,7},{3,5},{1,3},{0,1},{10,8},{12,10},{14... | collective-permute-start | bytes 786440 | tf_op jit(solution)/shard_map/ppermute | solution.py:271
  90.1 7.1 %collective-permute-start.22 = (bf16[2,4,16,1024]{3,2,1,0:T(8,128)(2,1)S(1)}, bf16[2,4,16,1024]{3,2,1,0:T(8,128)(2,1)S(1)}, u32[]{:S(2)}, u32[]{:S(2)}) collective-permute-start(bf16[2,4,16,1024]{3,2,1,0:T(8,128)(2,1)S(1)} %get-tuple-element.138), channel_id=1, source_target_pairs={{0,2},{2,4},{4,6},{6,7},{7,5},{5,3},{3,1},{1,0},{8,10},{10,12},{12... | collective-permute-start | bytes 786440 | tf_op jit(solution)/shard_map/ppermute | solution.py:271
  94.6 8.2 %collective-permute-start.31 = (bf16[3,32,1024]{2,1,0:T(8,128)(2,1)S(1)}, bf16[3,32,1024]{2,1,0:T(8,128)(2,1)S(1)}, u32[]{:S(2)}, u32[]{:S(2)}) collective-permute-start(bf16[3,32,1024]{2,1,0:T(8,128)(2,1)S(1)} %get-tuple-element.154), channel_id=1, source_target_pairs={{0,16},{8,24},{16,0},{24,8},{1,17},{9,25},{17,1},{25,9},{2,18},{10... | collective-permute-start | bytes 589832 | tf_op jit(solution)/shard_map/ppermute | solution.py:295
  95.7 7.1 %collective-permute-start.32 = (bf16[2,64,1024]{2,1,0:T(8,128)(2,1)S(1)}, bf16[2,64,1024]{2,1,0:T(8,128)(2,1)S(1)}, u32[]{:S(2)}, u32[]{:S(2)}) collective-permute-start(bf16[2,64,1024]{2,1,0:T(8,128)(2,1)S(1)} %get-tuple-element.155), channel_id=1, source_target_pairs={{0,8},{8,0},{16,24},{24,16},{1,9},{9,1},{17,25},{25,17},{2,10},{10... | collective-permute-start | bytes 786440 | tf_op jit(solution)/shard_map/ppermute | solution.py:298
  95.7 7.1 %collective-permute-start.33 = (bf16[2,64,1024]{2,1,0:T(8,128)(2,1)S(1)}, bf16[2,64,1024]{2,1,0:T(8,128)(2,1)S(1)}, u32[]{:S(2)}, u32[]{:S(2)}) collective-permute-start(bf16[2,64,1024]{2,1,0:T(8,128)(2,1)S(1)} %get-tuple-element.156), channel_id=1, source_target_pairs={{0,8},{8,0},{16,24},{24,16},{1,9},{9,1},{17,25},{25,17},{2,10},{10... | collective-permute-start | bytes 786440 | tf_op jit(solution)/shard_map/ppermute | solution.py:298
  100.4 5.7 %collective-permute-start.30 = (bf16[3,32,1024]{2,1,0:T(8,128)(2,1)S(1)}, bf16[3,32,1024]{2,1,0:T(8,128)(2,1)S(1)}, u32[]{:S(2)}, u32[]{:S(2)}) collective-permute-start(bf16[3,32,1024]{2,1,0:T(8,128)(2,1)S(1)} %get-tuple-element.151), channel_id=1, source_target_pairs={{0,16},{8,24},{16,0},{24,8},{1,17},{9,25},{17,1},{25,9},{2,18},{10... | collective-permute-start | bytes 589832 | tf_op jit(solution)/shard_map/ppermute | solution.py:295
  (8 other events, 30.7 us)

commit v5 on v4

--- a/solution.py
+++ b/solution.py
@@ -135,7 +135,8 @@
             y = y.reshape(pairs, total, w)
             r["send"][:, :, cols] = y[pairs - sent :].astype(BF16)
             r["kept"][:, :, cols] = y[:sent]
-    r["token"][...] = jnp.zeros_like(r["token"])
+    if cfg["compute"] is not None:
+        r["token"][...] = jnp.zeros_like(r["token"])
     for c in stores:
         c.wait()
 
@@ -203,7 +204,8 @@
         hold(f"putsem{j}", pltpu.SemaphoreType.DMA((len(unit),)))
     for j, x in enumerate(after):
         take(f"after{j}", x, anym)
-    give("token", (8, LANES), F32, vmem)
+    if compute is not None:
+        give("token", (8, LANES), F32, vmem)
     aliases = {}
     if finish or place:
         give("out", (CAP, m, m), F32, anym)
@@ -287,7 +289,7 @@
             [*after] if state["token"] is None else [state["token"], *after],
         )
         common.update({name: got[name] for name in ("meta", "spread", "res") if name in got})
-        state["out"], state["token"] = got.get("out", state["out"]), got["token"]
+        state["out"], state["token"] = got.get("out", state["out"]), got.get("token")
         if unit is not None:
             i = len(units)
             units.append(unit)

time: 111 us -> 111 us (level)
  no operation moved by 1% of the time
where the time goes in v5:
time: 111 us; the launch traced here: 110 us
  waiting for transfers between devices  42.2 us (38%)
  starting transfers between devices  32.8 us (30%)
  Pallas kernels  32.6 us (29%)
  local copies, waits for them, and re-layouts  2.01 us (2%)
    ppermute x16, waiting for transfers between devices, send_on(): return lax.ppermute(x, 'owner', up if turn == 1 else down)  36.6 us
    pallas_call x13, Pallas kernels, step_call(): pl.pallas_call(functools.partial(step_kernel, cfg), in_specs=specs, out_s...  32.6 us
    ppermute x16, starting transfers between devices, send_on(): return lax.ppermute(x, 'owner', up if turn == 1 else down)  17.9 us
    ppermute x9, starting transfers between devices, call(): crossed[i] = lax.ppermute(got['send'], 'sector', swap_side)  12.4 us
    ppermute x9, waiting for transfers between devices, call(): crossed[i] = lax.ppermute(got['send'], 'sector', swap_side)  3.07 us
  transfers between devices with their start and end apart: 37, of which 14 were waited for; matrix products, arithmetic and copies ran while one was open for 0% of the time, Pallas kernels for 28%

profile of v5, /device:TPU:0, one launch (start us, length us, event | category | flops | bytes accessed | tf_op | source)
XLA Modules:
  0.0 110.5 jit_solution(6830340651489861497)
XLA Ops:
  0.0 1.8 %fusion = (bf16[4,64,1024]{2,1,0:T(8,128)(2,1)S(1)}, bf16[4,64,1024]{2,1,0:T(8,128)(2,1)S(1)}) fusion(f32[1,4,128,1024]{3,2,1,0:T(8,128)} %param.4, s32[]{:T(128)S(6)} %select_n.33, s32[]{:T(128)S(6)} %select_n.34), kind=kLoop, calls=%fused_computation.2 | loop fusion | bytes 2097160 | tf_op jit(solution)/shard_map/convert_element_type | solution.py:261
  2.4 1.5 %collective-permute-done.1 = bf16[4,64,1024]{2,1,0:T(8,128)(2,1)S(1)} collective-permute-done((bf16[4,64,1024]{2,1,0:T(8,128)(2,1)S(1)}, bf16[4,64,1024]{2,1,0:T(8,128)(2,1)S(1)}, u32[]{:S(2)}, u32[]{:S(2)}) %collective-permute-start.1) | collective-permute-done | bytes 524320 | tf_op jit(solution)/shard_map/ppermute | solution.py:260
  4.8 2.6 %collective-permute-start.4 = (bf16[2,4,32,1024]{3,2,1,0:T(8,128)(2,1)S(1)}, bf16[2,4,32,1024]{3,2,1,0:T(8,128)(2,1)}, u32[]{:S(2)}, u32[]{:S(2)}) collective-permute-start(bf16[2,4,32,1024]{3,2,1,0:T(8,128)(2,1)S(1)} %get-tuple-element.84.refs_7_), channel_id=1, source_target_pairs={{2,0},{4,2},{6,4},{7,6},{5,7},{3,5},{1,3},{0,1},{10,8},{12,10},{14... | collective-permute-start | bytes 1572872 | tf_op jit(solution)/shard_map/ppermute | solution.py:273
  8.8 3.7 %shard_map.46 = (s32[1,6]{1,0:T(1,128)S(1)}, f32[32,128]{1,0:T(8,128)S(1)}, bf16[2048,1024]{1,0:T(8,128)(2,1)S(1)}, bf16[3,64,1024]{2,1,0:T(8,128)(2,1)S(1)}, f3...) custom-call(s32[3]{0:T(128)S(1)} %pad_add_fusion.refs_0_, s32[1,4]{1,0:T(1,128)S(1)} %copy-done.1, f32[4,4]{1,0:T(4,128)S(1)} %bitcast.19, ...), custom_call_target="tpu_custom_call" | custom-call | flops 3000000000 | bytes 1000 | tf_op jit(solution)/shard_map/pallas_call | solution.py:224
  12.5 7.6 %collective-permute-done.4.refs_4_ = bf16[2,4,32,1024]{3,2,1,0:T(8,128)(2,1)} collective-permute-done((bf16[2,4,32,1024]{3,2,1,0:T(8,128)(2,1)S(1)}, bf16[2,4,32,1024]{3,2,1,0:T(8,128)(2,1)}, u32[]{:S(2)}, u32[]{:S(2)}) %collective-permute-start.4) | collective-permute-done | bytes 524320 | tf_op jit(solution)/shard_map/ppermute | solution.py:273
  20.1 1.7 %collective-permute-start.6 = (bf16[2,4,32,1024]{3,2,1,0:T(8,128)(2,1)}, bf16[2,4,32,1024]{3,2,1,0:T(8,128)(2,1)S(1)}, u32[]{:S(2)}, u32[]{:S(2)}) collective-permute-start(bf16[2,4,32,1024]{3,2,1,0:T(8,128)(2,1)} %collective-permute-done.4.refs_4_), channel_id=1, source_target_pairs={{2,0},{4,2},{6,4},{7,6},{5,7},{3,5},{1,3},{0,1},{10,8},{12,10},{14... | collective-permute-start | bytes 1572872 | tf_op jit(solution)/shard_map/ppermute | solution.py:273
  22.1 1.7 %collective-permute-start.9 = (bf16[3,64,1024]{2,1,0:T(8,128)(2,1)S(1)}, bf16[3,64,1024]{2,1,0:T(8,128)(2,1)S(1)}, u32[]{:S(2)}, u32[]{:S(2)}) collective-permute-start(bf16[3,64,1024]{2,1,0:T(8,128)(2,1)S(1)} %get-tuple-element.98), channel_id=1, source_target_pairs={{0,16},{8,24},{16,0},{24,8},{1,17},{9,25},{17,1},{25,9},{2,18},{10... | collective-permute-start | bytes 1179656 | tf_op jit(solution)/shard_map/ppermute | solution.py:297
  23.8 2.9 %shard_map.47 = (bf16[3,64,1024]{2,1,0:T(8,128)(2,1)S(1)}, f32[3,64,1024]{2,1,0:T(8,128)S(1)}, f32[8,128]{1,0:T(8,128)S(1)}) custom-call(s32[1,6]{1,0:T(1,128)S(1)} %get-tuple-element.85.refs_0_, bf16[2048,1024]{1,0:T(8,128)(2,1)S(1)} %get-tuple-element.86.refs_1_, f32[32,128]{1,0:T(8,128)S(1)} %get-tuple-element.87.refs_2_, ...), custom_call_target="tpu_custom_call" | custom-call | flops 3000000000 | bytes 1000 | tf_op jit(solution)/shard_map/pallas_call | solution.py:224
  26.8 7.2 %collective-permute-done.6.refs_4_ = bf16[2,4,32,1024]{3,2,1,0:T(8,128)(2,1)S(1)} collective-permute-done((bf16[2,4,32,1024]{3,2,1,0:T(8,128)(2,1)}, bf16[2,4,32,1024]{3,2,1,0:T(8,128)(2,1)S(1)}, u32[]{:S(2)}, u32[]{:S(2)}) %collective-permute-start.6) | collective-permute-done | bytes 524320 | tf_op jit(solution)/shard_map/ppermute | solution.py:273
  34.0 1.4 %collective-permute-start.8 = (bf16[2,4,32,1024]{3,2,1,0:T(8,128)(2,1)S(1)}, bf16[2,4,32,1024]{3,2,1,0:T(8,128)(2,1)S(1)}, u32[]{:S(2)}, u32[]{:S(2)}) collective-permute-start(bf16[2,4,32,1024]{3,2,1,0:T(8,128)(2,1)S(1)} %collective-permute-done.6.refs_4_), channel_id=1, source_target_pairs={{2,0},{4,2},{6,4},{7,6},{5,7},{3,5},{1,3},{0,1},{10,8},{12,10},{14... | collective-permute-start | bytes 1572872 | tf_op jit(solution)/shard_map/ppermute | solution.py:273
  36.0 1.4 %collective-permute-start.12 = (bf16[3,64,1024]{2,1,0:T(8,128)(2,1)S(1)}, bf16[3,64,1024]{2,1,0:T(8,128)(2,1)S(1)}, u32[]{:S(2)}, u32[]{:S(2)}) collective-permute-start(bf16[3,64,1024]{2,1,0:T(8,128)(2,1)S(1)} %get-tuple-element.105), channel_id=1, source_target_pairs={{0,16},{8,24},{16,0},{24,8},{1,17},{9,25},{17,1},{25,9},{2,18},{10... | collective-permute-start | bytes 1179656 | tf_op jit(solution)/shard_map/ppermute | solution.py:297
  37.4 3.2 %shard_map.48 = (bf16[3,64,1024]{2,1,0:T(8,128)(2,1)S(1)}, f32[3,64,1024]{2,1,0:T(8,128)S(1)}, bf16[2,64,1024]{2,1,0:T(8,128)(2,1)S(1)}, f32[8,128]{1,0:T(8,128)S(1)}, f32[2,1024,1024]{2,1,0:T(8,128)}) custom-call(s32[1,6]{1,0:T(1,128)S(1)} %get-tuple-element.85.refs_0_, bf16[2048,1024]{1,0:T(8,128)(2,1)S(1)} %get-tuple-element.86.refs_1_, ...), custom_call_target="tpu_custom_call" | custom-call | flops 3000000000 | bytes 1000 | tf_op jit(solution)/shard_map/pallas_call | solution.py:224
  40.7 6.0 %collective-permute-done.8.refs_4_ = bf16[2,4,32,1024]{3,2,1,0:T(8,128)(2,1)S(1)} collective-permute-done((bf16[2,4,32,1024]{3,2,1,0:T(8,128)(2,1)S(1)}, bf16[2,4,32,1024]{3,2,1,0:T(8,128)(2,1)S(1)}, u32[]{:S(2)}, u32[]{:S(2)}) %collective-permute-start.8) | collective-permute-done | bytes 524320 | tf_op jit(solution)/shard_map/ppermute | solution.py:273
  49.9 3.4 %shard_map.49 = (bf16[3,64,1024]{2,1,0:T(8,128)(2,1)S(1)}, f32[3,64,1024]{2,1,0:T(8,128)S(1)}, bf16[2,64,1024]{2,1,0:T(8,128)(2,1)S(1)}, f32[8,128]{1,0:T(8,128)S(1)}, f32[2,1024,1024]{2,1,0:T(8,128)}) custom-call(s32[1,6]{1,0:T(1,128)S(1)} %get-tuple-element.85.refs_0_, ...), custom_call_target="tpu_custom_call", output_to_operand_aliasing={{4}: (9, {})} | custom-call | flops 3000000000 | bytes 1000 | tf_op jit(solution)/shard_map/pallas_call | solution.py:224
  53.4 5.4 %collective-permute-done.11.refs_4_ = bf16[2,4,32,1024]{3,2,1,0:T(8,128)(2,1)S(1)} collective-permute-done((bf16[2,4,32,1024]{3,2,1,0:T(8,128)(2,1)S(1)}, bf16[2,4,32,1024]{3,2,1,0:T(8,128)(2,1)S(1)}, u32[]{:S(2)}, u32[]{:S(2)}) %collective-permute-start.11) | collective-permute-done | bytes 524320 | tf_op jit(solution)/shard_map/ppermute | solution.py:273
  62.0 3.4 %shard_map.50 = (bf16[3,64,1024]{2,1,0:T(8,128)(2,1)S(1)}, f32[3,64,1024]{2,1,0:T(8,128)S(1)}, bf16[2,64,1024]{2,1,0:T(8,128)(2,1)S(1)}, f32[8,128]{1,0:T(8,128)S(1)}, f32[2,1024,1024]{2,1,0:T(8,128)}) custom-call(s32[1,6]{1,0:T(1,128)S(1)} %get-tuple-element.85.refs_0_, ...), custom_call_target="tpu_custom_call", output_to_operand_aliasing={{4}: (9, {})} | custom-call | flops 3000000000 | bytes 1000 | tf_op jit(solution)/shard_map/pallas_call | solution.py:224
  65.4 5.4 %collective-permute-done.15.refs_4_ = bf16[2,4,32,1024]{3,2,1,0:T(8,128)(2,1)S(1)} collective-permute-done((bf16[2,4,32,1024]{3,2,1,0:T(8,128)(2,1)S(1)}, bf16[2,4,32,1024]{3,2,1,0:T(8,128)(2,1)S(1)}, u32[]{:S(2)}, u32[]{:S(2)}) %collective-permute-start.15) | collective-permute-done | bytes 524320 | tf_op jit(solution)/shard_map/ppermute | solution.py:273
  71.2 1.7 %collective-permute-start.18 = (bf16[2,4,32,1024]{3,2,1,0:T(8,128)(2,1)S(1)}, bf16[2,4,32,1024]{3,2,1,0:T(8,128)(2,1)S(1)}, u32[]{:S(2)}, u32[]{:S(2)}) collective-permute-start(bf16[2,4,32,1024]{3,2,1,0:T(8,128)(2,1)S(1)} %collective-permute-done.14.refs_3_), channel_id=1, source_target_pairs={{0,2},{2,4},{4,6},{6,7},{7,5},{5,3},{3,1},{1,0},{8,10},{10,12},{12... | collective-permute-start | bytes 1572872 | tf_op jit(solution)/shard_map/ppermute | solution.py:273
  73.9 3.4 %shard_map.51 = (bf16[3,64,1024]{2,1,0:T(8,128)(2,1)S(1)}, f32[3,64,1024]{2,1,0:T(8,128)S(1)}, bf16[2,64,1024]{2,1,0:T(8,128)(2,1)S(1)}, f32[8,128]{1,0:T(8,128)S(1)}, f32[2,1024,1024]{2,1,0:T(8,128)}) custom-call(s32[1,6]{1,0:T(1,128)S(1)} %get-tuple-element.85.refs_0_, ...), custom_call_target="tpu_custom_call", output_to_operand_aliasing={{4}: (9, {})} | custom-call | flops 3000000000 | bytes 1000 | tf_op jit(solution)/shard_map/pallas_call | solution.py:224
  78.5 2.5 %collective-permute-done.19.refs_4_ = bf16[2,4,32,1024]{3,2,1,0:T(8,128)(2,1)S(1)} collective-permute-done((bf16[2,4,32,1024]{3,2,1,0:T(8,128)(2,1)S(1)}, bf16[2,4,32,1024]{3,2,1,0:T(8,128)(2,1)S(1)}, u32[]{:S(2)}, u32[]{:S(2)}) %collective-permute-start.19) | collective-permute-done | bytes 524320 | tf_op jit(solution)/shard_map/ppermute | solution.py:273
  81.8 1.4 %collective-permute-start.24 = (bf16[2,4,16,1024]{3,2,1,0:T(8,128)(2,1)S(1)}, bf16[2,4,16,1024]{3,2,1,0:T(8,128)(2,1)S(1)}, u32[]{:S(2)}, u32[]{:S(2)}) collective-permute-start(bf16[2,4,16,1024]{3,2,1,0:T(8,128)(2,1)S(1)} %get-tuple-element.163), channel_id=1, source_target_pairs={{0,2},{2,4},{4,6},{6,7},{7,5},{5,3},{3,1},{1,0},{8,10},{10,12},{12... | collective-permute-start | bytes 786440 | tf_op jit(solution)/shard_map/ppermute | solution.py:273
  84.4 2.3 %shard_map.52 = (bf16[3,64,1024]{2,1,0:T(8,128)(2,1)S(1)}, f32[3,64,1024]{2,1,0:T(8,128)S(1)}, f32[8,128]{1,0:T(8,128)S(1)}) custom-call(s32[1,6]{1,0:T(1,128)S(1)} %get-tuple-element.85.refs_0_, bf16[2048,1024]{1,0:T(8,128)(2,1)S(1)} %get-tuple-element.86.refs_1_, f32[32,128]{1,0:T(8,128)S(1)} %get-tuple-element.87.refs_2_, ...), custom_call_target="tpu_custom_call" | custom-call | flops 3000000000 | bytes 1000 | tf_op jit(solution)/shard_map/pallas_call | solution.py:224
  86.7 1.9 %collective-permute-start.29 = (bf16[3,64,1024]{2,1,0:T(8,128)(2,1)S(1)}, bf16[3,64,1024]{2,1,0:T(8,128)(2,1)S(1)}, u32[]{:S(2)}, u32[]{:S(2)}) collective-permute-start(bf16[3,64,1024]{2,1,0:T(8,128)(2,1)S(1)} %get-tuple-element.144), channel_id=1, source_target_pairs={{0,16},{8,24},{16,0},{24,8},{1,17},{9,25},{17,1},{25,9},{2,18},{10... | collective-permute-start | bytes 1179656 | tf_op jit(solution)/shard_map/ppermute | solution.py:297
  88.6 1.5 %collective-permute-start.23 = (bf16[2,4,16,1024]{3,2,1,0:T(8,128)(2,1)S(1)}, bf16[2,4,16,1024]{3,2,1,0:T(8,128)(2,1)S(1)}, u32[]{:S(2)}, u32[]{:S(2)}) collective-permute-start(bf16[2,4,16,1024]{3,2,1,0:T(8,128)(2,1)S(1)} %get-tuple-element.135), channel_id=1, source_target_pairs={{2,0},{4,2},{6,4},{7,6},{5,7},{3,5},{1,3},{0,1},{10,8},{12,10},{14... | collective-permute-start | bytes 786440 | tf_op jit(solution)/shard_map/ppermute | solution.py:273
  91.8 2.8 %shard_map.53 = (bf16[3,32,1024]{2,1,0:T(8,128)(2,1)S(1)}, f32[3,32,1024]{2,1,0:T(8,128)S(1)}, bf16[2,64,1024]{2,1,0:T(8,128)(2,1)S(1)}, bf16[2,64,1024]{2,1,0:T...) custom-call(s32[1,6]{1,0:T(1,128)S(1)} %get-tuple-element.85.refs_0_, ...), custom_call_target="tpu_custom_call", output_to_operand_aliasing={{5}: (11, {})} | custom-call | flops 3000000000 | bytes 1000 | tf_op jit(solution)/shard_map/pallas_call | solution.py:224
  97.2 1.7 %collective-permute-done.29.refs_6_.refs_2_ = bf16[3,64,1024]{2,1,0:T(8,128)(2,1)S(1)} collective-permute-done((bf16[3,64,1024]{2,1,0:T(8,128)(2,1)S(1)}, bf16[3,64,1024]{2,1,0:T(8,128)(2,1)S(1)}, u32[]{:S(2)}, u32[]{:S(2)}) %collective-permute-start.29) | collective-permute-done | bytes 393248 | tf_op jit(solution)/shard_map/ppermute | solution.py:297
  98.8 1.6 %shard_map.54 = (bf16[3,32,1024]{2,1,0:T(8,128)(2,1)S(1)}, f32[3,32,1024]{2,1,0:T(8,128)S(1)}, f32[8,128]{1,0:T(8,128)S(1)}) custom-call(s32[1,6]{1,0:T(1,128)S(1)} %get-tuple-element.85.refs_0_, bf16[2048,1024]{1,0:T(8,128)(2,1)S(1)} %get-tuple-element.86.refs_1_, f32[32,128]{1,0:T(8,128)S(1)} %get-tuple-element.87.refs_2_, ...), custom_call_target="tpu_custom_call" | custom-call | flops 3000000000 | bytes 1000 | tf_op jit(solution)/shard_map/pallas_call | solution.py:224
  100.4 1.9 %collective-permute-start.30 = (bf16[3,32,1024]{2,1,0:T(8,128)(2,1)S(1)}, bf16[3,32,1024]{2,1,0:T(8,128)(2,1)S(1)}, u32[]{:S(2)}, u32[]{:S(2)}) collective-permute-start(bf16[3,32,1024]{2,1,0:T(8,128)(2,1)S(1)} %get-tuple-element.146), channel_id=1, source_target_pairs={{0,16},{8,24},{16,0},{24,8},{1,17},{9,25},{17,1},{25,9},{2,18},{10... | collective-permute-start | bytes 589832 | tf_op jit(solution)/shard_map/ppermute | solution.py:297
  102.8 1.9 %shard_map.55 = (bf16[2,64,1024]{2,1,0:T(8,128)(2,1)S(1)}, bf16[2,32,1024]{2,1,0:T(8,128)(2,1)S(1)}, f32[2,1024,1024]{2,1,0:T(8,128)}) custom-call(s32[1,6]{1,0:T(1,128)S(1)} %get-tuple-element.85.refs_0_, f32[3,64,1024]{2,1,0:T(8,128)S(1)} %get-tuple-element.147.refs_1_, ...), custom_call_target="tpu_custom_call", output_to_operand_aliasing={{2}: (8, {})} | custom-call | flops 3000000000 | bytes 1000 | tf_op jit(solution)/shard_map/pallas_call | solution.py:224
  106.1 1.3 %shard_map.56 = (bf16[2,32,1024]{2,1,0:T(8,128)(2,1)S(1)}, f32[2,1024,1024]{2,1,0:T(8,128)}) custom-call(s32[1,6]{1,0:T(1,128)S(1)} %get-tuple-element.85.refs_0_, f32[3,32,1024]{2,1,0:T(8,128)S(1)} %get-tuple-element.145.refs_1_, bf16[3,32,1024]{2,1,0:T(8,128)(2,1)S(1)} %collective-permute-done.30.refs_2_, ...), custom_call_target="tpu_custom_call", output_to_operand_aliasing={{1}: (3, {})} | custom-call | flops 3000000000 | bytes 1000 | tf_op jit(solution)/shard_map/pallas_call | solution.py:224
  107.5 1.5 %shard_map.57.refs_2_ = f32[2,1024,1024]{2,1,0:T(8,128)} custom-call(s32[1,6]{1,0:T(1,128)S(1)} %get-tuple-element.85.refs_0_, bf16[2,64,1024]{2,1,0:T(8,128)(2,1)S(1)} %collective-permute-done.35.refs_1_, bf16[2,32,1024]{2,1,0:T(8,128)(2,1)S(1)} %collective-permute-done.36.refs_2_, ...), custom_call_target="tpu_custom_call", output_to_operand_aliasing={{}: (3, {})} | custom-call | flops 3000000000 | bytes 1000 | tf_op jit(solution)/shard_map/pallas_call | solution.py:224
  109.0 1.3 %shard_map.58 = f32[2,1024,1024]{2,1,0:T(8,128)} custom-call(s32[1,6]{1,0:T(1,128)S(1)} %get-tuple-element.85.refs_0_, bf16[2,32,1024]{2,1,0:T(8,128)(2,1)S(1)} %collective-permute-done.34.refs_1_, f32[2,1024,1024]{2,1,0:T(8,128)} %shard_map.57.refs_2_), custom_call_target="tpu_custom_call", output_to_operand_aliasing={{}: (2, {})} | custom-call | flops 3000000000 | bytes 1000 | tf_op jit(solution)/shard_map/pallas_call | solution.py:224
  (69 shorter events, 21.1 us)
Async XLA Ops:
  4.4 4.4 %collective-permute-start.2 = (bf16[1024,1024]{1,0:T(8,128)(2,1)S(1)}, bf16[1024,1024]{1,0:T(8,128)(2,1)}, u32[]{:S(2)}, u32[]{:S(2)}) collective-permute-start(bf16[1024,1024]{1,0:T(8,128)(2,1)S(1)} %convert_element_type.19.refs_4_), channel_id=1, source_target_pairs={{0,8},{8,0},{16,24},{24,16},{1,9},{9,1},{17,25},{25,17},{2,10},{10... | collective-permute-start | bytes 6291464 | tf_op jit(solution)/shard_map/ppermute | solution.py:267
  4.8 15.3 %collective-permute-start.4 = (bf16[2,4,32,1024]{3,2,1,0:T(8,128)(2,1)S(1)}, bf16[2,4,32,1024]{3,2,1,0:T(8,128)(2,1)}, u32[]{:S(2)}, u32[]{:S(2)}) collective-permute-start(bf16[2,4,32,1024]{3,2,1,0:T(8,128)(2,1)S(1)} %get-tuple-element.84.refs_7_), channel_id=1, source_target_pairs={{2,0},{4,2},{6,4},{7,6},{5,7},{3,5},{1,3},{0,1},{10,8},{12,10},{14... | collective-permute-start | bytes 1572872 | tf_op jit(solution)/shard_map/ppermute | solution.py:273
  7.5 14.3 %collective-permute-start.3 = (bf16[2,4,32,1024]{3,2,1,0:T(8,128)(2,1)S(1)}, bf16[2,4,32,1024]{3,2,1,0:T(8,128)(2,1)}, u32[]{:S(2)}, u32[]{:S(2)}) collective-permute-start(bf16[2,4,32,1024]{3,2,1,0:T(8,128)(2,1)S(1)} %get-tuple-element.83.refs_6_), channel_id=1, source_target_pairs={{0,2},{2,4},{4,6},{6,7},{7,5},{5,3},{3,1},{1,0},{8,10},{10,12},{12... | collective-permute-start | bytes 1572872 | tf_op jit(solution)/shard_map/ppermute | solution.py:273
  20.1 13.8 %collective-permute-start.6 = (bf16[2,4,32,1024]{3,2,1,0:T(8,128)(2,1)}, bf16[2,4,32,1024]{3,2,1,0:T(8,128)(2,1)S(1)}, u32[]{:S(2)}, u32[]{:S(2)}) collective-permute-start(bf16[2,4,32,1024]{3,2,1,0:T(8,128)(2,1)} %collective-permute-done.4.refs_4_), channel_id=1, source_target_pairs={{2,0},{4,2},{6,4},{7,6},{5,7},{3,5},{1,3},{0,1},{10,8},{12,10},{14... | collective-permute-start | bytes 1572872 | tf_op jit(solution)/shard_map/ppermute | solution.py:273
  21.8 13.6 %collective-permute-start.5 = (bf16[2,4,32,1024]{3,2,1,0:T(8,128)(2,1)}, bf16[2,4,32,1024]{3,2,1,0:T(8,128)(2,1)S(1)}, u32[]{:S(2)}, u32[]{:S(2)}) collective-permute-start(bf16[2,4,32,1024]{3,2,1,0:T(8,128)(2,1)} %collective-permute-done.3.refs_3_), channel_id=1, source_target_pairs={{0,2},{2,4},{4,6},{6,7},{7,5},{5,3},{3,1},{1,0},{8,10},{10,12},{12... | collective-permute-start | bytes 1572872 | tf_op jit(solution)/shard_map/ppermute | solution.py:273
  22.1 15.3 %collective-permute-start.9 = (bf16[3,64,1024]{2,1,0:T(8,128)(2,1)S(1)}, bf16[3,64,1024]{2,1,0:T(8,128)(2,1)S(1)}, u32[]{:S(2)}, u32[]{:S(2)}) collective-permute-start(bf16[3,64,1024]{2,1,0:T(8,128)(2,1)S(1)} %get-tuple-element.98), channel_id=1, source_target_pairs={{0,16},{8,24},{16,0},{24,8},{1,17},{9,25},{17,1},{25,9},{2,18},{10... | collective-permute-start | bytes 1179656 | tf_op jit(solution)/shard_map/ppermute | solution.py:297
  34.0 12.7 %collective-permute-start.8 = (bf16[2,4,32,1024]{3,2,1,0:T(8,128)(2,1)S(1)}, bf16[2,4,32,1024]{3,2,1,0:T(8,128)(2,1)S(1)}, u32[]{:S(2)}, u32[]{:S(2)}) collective-permute-start(bf16[2,4,32,1024]{3,2,1,0:T(8,128)(2,1)S(1)} %collective-permute-done.6.refs_4_), channel_id=1, source_target_pairs={{2,0},{4,2},{6,4},{7,6},{5,7},{3,5},{1,3},{0,1},{10,8},{12,10},{14... | collective-permute-start | bytes 1572872 | tf_op jit(solution)/shard_map/ppermute | solution.py:273
  35.4 12.5 %collective-permute-start.7 = (bf16[2,4,32,1024]{3,2,1,0:T(8,128)(2,1)S(1)}, bf16[2,4,32,1024]{3,2,1,0:T(8,128)(2,1)S(1)}, u32[]{:S(2)}, u32[]{:S(2)}) collective-permute-start(bf16[2,4,32,1024]{3,2,1,0:T(8,128)(2,1)S(1)} %collective-permute-done.5.refs_3_), channel_id=1, source_target_pairs={{0,2},{2,4},{4,6},{6,7},{7,5},{5,3},{3,1},{1,0},{8,10},{10,12},{12... | collective-permute-start | bytes 1572872 | tf_op jit(solution)/shard_map/ppermute | solution.py:273
  36.0 13.9 %collective-permute-start.12 = (bf16[3,64,1024]{2,1,0:T(8,128)(2,1)S(1)}, bf16[3,64,1024]{2,1,0:T(8,128)(2,1)S(1)}, u32[]{:S(2)}, u32[]{:S(2)}) collective-permute-start(bf16[3,64,1024]{2,1,0:T(8,128)(2,1)S(1)} %get-tuple-element.105), channel_id=1, source_target_pairs={{0,16},{8,24},{16,0},{24,8},{1,17},{9,25},{17,1},{25,9},{2,18},{10... | collective-permute-start | bytes 1179656 | tf_op jit(solution)/shard_map/ppermute | solution.py:297
  40.6 9.3 %collective-permute-start.13 = (bf16[2,64,1024]{2,1,0:T(8,128)(2,1)S(1)}, bf16[2,64,1024]{2,1,0:T(8,128)(2,1)S(1)}, u32[]{:S(2)}, u32[]{:S(2)}) collective-permute-start(bf16[2,64,1024]{2,1,0:T(8,128)(2,1)S(1)} %get-tuple-element.106), channel_id=1, source_target_pairs={{0,8},{8,0},{16,24},{24,16},{1,9},{9,1},{17,25},{25,17},{2,10},{10... | collective-permute-start | bytes 786440 | tf_op jit(solution)/shard_map/ppermute | solution.py:300
  46.7 12.1 %collective-permute-start.11 = (bf16[2,4,32,1024]{3,2,1,0:T(8,128)(2,1)S(1)}, bf16[2,4,32,1024]{3,2,1,0:T(8,128)(2,1)S(1)}, u32[]{:S(2)}, u32[]{:S(2)}) collective-permute-start(bf16[2,4,32,1024]{3,2,1,0:T(8,128)(2,1)S(1)} %collective-permute-done.8.refs_4_), channel_id=1, source_target_pairs={{2,0},{4,2},{6,4},{7,6},{5,7},{3,5},{1,3},{0,1},{10,8},{12,10},{14... | collective-permute-start | bytes 1572872 | tf_op jit(solution)/shard_map/ppermute | solution.py:273
  47.9 12.1 %collective-permute-start.10 = (bf16[2,4,32,1024]{3,2,1,0:T(8,128)(2,1)S(1)}, bf16[2,4,32,1024]{3,2,1,0:T(8,128)(2,1)S(1)}, u32[]{:S(2)}, u32[]{:S(2)}) collective-permute-start(bf16[2,4,32,1024]{3,2,1,0:T(8,128)(2,1)S(1)} %collective-permute-done.7.refs_3_), channel_id=1, source_target_pairs={{0,2},{2,4},{4,6},{6,7},{7,5},{5,3},{3,1},{1,0},{8,10},{10,12},{12... | collective-permute-start | bytes 1572872 | tf_op jit(solution)/shard_map/ppermute | solution.py:273
  48.7 13.3 %collective-permute-start.16 = (bf16[3,64,1024]{2,1,0:T(8,128)(2,1)S(1)}, bf16[3,64,1024]{2,1,0:T(8,128)(2,1)S(1)}, u32[]{:S(2)}, u32[]{:S(2)}) collective-permute-start(bf16[3,64,1024]{2,1,0:T(8,128)(2,1)S(1)} %get-tuple-element.114), channel_id=1, source_target_pairs={{0,16},{8,24},{16,0},{24,8},{1,17},{9,25},{17,1},{25,9},{2,18},{10... | collective-permute-start | bytes 1179656 | tf_op jit(solution)/shard_map/ppermute | solution.py:297
  53.3 8.7 %collective-permute-start.17 = (bf16[2,64,1024]{2,1,0:T(8,128)(2,1)S(1)}, bf16[2,64,1024]{2,1,0:T(8,128)(2,1)S(1)}, u32[]{:S(2)}, u32[]{:S(2)}) collective-permute-start(bf16[2,64,1024]{2,1,0:T(8,128)(2,1)S(1)} %get-tuple-element.115), channel_id=1, source_target_pairs={{0,8},{8,0},{16,24},{24,16},{1,9},{9,1},{17,25},{25,17},{2,10},{10... | collective-permute-start | bytes 786440 | tf_op jit(solution)/shard_map/ppermute | solution.py:300
  58.8 12.1 %collective-permute-start.15 = (bf16[2,4,32,1024]{3,2,1,0:T(8,128)(2,1)S(1)}, bf16[2,4,32,1024]{3,2,1,0:T(8,128)(2,1)S(1)}, u32[]{:S(2)}, u32[]{:S(2)}) collective-permute-start(bf16[2,4,32,1024]{3,2,1,0:T(8,128)(2,1)S(1)} %collective-permute-done.11.refs_4_), channel_id=1, source_target_pairs={{2,0},{4,2},{6,4},{7,6},{5,7},{3,5},{1,3},{0,1},{10,8},{12,10},{14... | collective-permute-start | bytes 1572872 | tf_op jit(solution)/shard_map/ppermute | solution.py:273
  59.9 11.2 %collective-permute-start.14 = (bf16[2,4,32,1024]{3,2,1,0:T(8,128)(2,1)S(1)}, bf16[2,4,32,1024]{3,2,1,0:T(8,128)(2,1)S(1)}, u32[]{:S(2)}, u32[]{:S(2)}) collective-permute-start(bf16[2,4,32,1024]{3,2,1,0:T(8,128)(2,1)S(1)} %collective-permute-done.10.refs_3_), channel_id=1, source_target_pairs={{0,2},{2,4},{4,6},{6,7},{7,5},{5,3},{3,1},{1,0},{8,10},{10,12},{12... | collective-permute-start | bytes 1572872 | tf_op jit(solution)/shard_map/ppermute | solution.py:273
  60.8 13.1 %collective-permute-start.20 = (bf16[3,64,1024]{2,1,0:T(8,128)(2,1)S(1)}, bf16[3,64,1024]{2,1,0:T(8,128)(2,1)S(1)}, u32[]{:S(2)}, u32[]{:S(2)}) collective-permute-start(bf16[3,64,1024]{2,1,0:T(8,128)(2,1)S(1)} %get-tuple-element.123), channel_id=1, source_target_pairs={{0,16},{8,24},{16,0},{24,8},{1,17},{9,25},{17,1},{25,9},{2,18},{10... | collective-permute-start | bytes 1179656 | tf_op jit(solution)/shard_map/ppermute | solution.py:297
  65.4 8.5 %collective-permute-start.21 = (bf16[2,64,1024]{2,1,0:T(8,128)(2,1)S(1)}, bf16[2,64,1024]{2,1,0:T(8,128)(2,1)S(1)}, u32[]{:S(2)}, u32[]{:S(2)}) collective-permute-start(bf16[2,64,1024]{2,1,0:T(8,128)(2,1)S(1)} %get-tuple-element.124), channel_id=1, source_target_pairs={{0,8},{8,0},{16,24},{24,16},{1,9},{9,1},{17,25},{25,17},{2,10},{10... | collective-permute-start | bytes 786440 | tf_op jit(solution)/shard_map/ppermute | solution.py:300
  70.9 10.1 %collective-permute-start.19 = (bf16[2,4,32,1024]{3,2,1,0:T(8,128)(2,1)S(1)}, bf16[2,4,32,1024]{3,2,1,0:T(8,128)(2,1)S(1)}, u32[]{:S(2)}, u32[]{:S(2)}) collective-permute-start(bf16[2,4,32,1024]{3,2,1,0:T(8,128)(2,1)S(1)} %collective-permute-done.15.refs_4_), channel_id=1, source_target_pairs={{2,0},{4,2},{6,4},{7,6},{5,7},{3,5},{1,3},{0,1},{10,8},{12,10},{14... | collective-permute-start | bytes 1572872 | tf_op jit(solution)/shard_map/ppermute | solution.py:273
  71.2 10.6 %collective-permute-start.18 = (bf16[2,4,32,1024]{3,2,1,0:T(8,128)(2,1)S(1)}, bf16[2,4,32,1024]{3,2,1,0:T(8,128)(2,1)S(1)}, u32[]{:S(2)}, u32[]{:S(2)}) collective-permute-start(bf16[2,4,32,1024]{3,2,1,0:T(8,128)(2,1)S(1)} %collective-permute-done.14.refs_3_), channel_id=1, source_target_pairs={{0,2},{2,4},{4,6},{6,7},{7,5},{5,3},{3,1},{1,0},{8,10},{10,12},{12... | collective-permute-start | bytes 1572872 | tf_op jit(solution)/shard_map/ppermute | solution.py:273
  72.9 13.8 %collective-permute-start.26 = (bf16[3,64,1024]{2,1,0:T(8,128)(2,1)S(1)}, bf16[3,64,1024]{2,1,0:T(8,128)(2,1)S(1)}, u32[]{:S(2)}, u32[]{:S(2)}) collective-permute-start(bf16[3,64,1024]{2,1,0:T(8,128)(2,1)S(1)} %get-tuple-element.137), channel_id=1, source_target_pairs={{0,16},{8,24},{16,0},{24,8},{1,17},{9,25},{17,1},{25,9},{2,18},{10... | collective-permute-start | bytes 1179656 | tf_op jit(solution)/shard_map/ppermute | solution.py:297
  77.3 11.3 %collective-permute-start.28 = (bf16[2,64,1024]{2,1,0:T(8,128)(2,1)S(1)}, bf16[2,64,1024]{2,1,0:T(8,128)(2,1)S(1)}, u32[]{:S(2)}, u32[]{:S(2)}) collective-permute-start(bf16[2,64,1024]{2,1,0:T(8,128)(2,1)S(1)} %get-tuple-element.140), channel_id=1, source_target_pairs={{0,8},{8,0},{16,24},{24,16},{1,9},{9,1},{17,25},{25,17},{2,10},{10... | collective-permute-start | bytes 786440 | tf_op jit(solution)/shard_map/ppermute | solution.py:300
  77.4 12.7 %collective-permute-start.27 = (bf16[3,64,1024]{2,1,0:T(8,128)(2,1)S(1)}, bf16[3,64,1024]{2,1,0:T(8,128)(2,1)S(1)}, u32[]{:S(2)}, u32[]{:S(2)}) collective-permute-start(bf16[3,64,1024]{2,1,0:T(8,128)(2,1)S(1)} %get-tuple-element.139), channel_id=1, source_target_pairs={{0,16},{8,24},{16,0},{24,8},{1,17},{9,25},{17,1},{25,9},{2,18},{10... | collective-permute-start | bytes 1179656 | tf_op jit(solution)/shard_map/ppermute | solution.py:297
  81.8 9.3 %collective-permute-start.24 = (bf16[2,4,16,1024]{3,2,1,0:T(8,128)(2,1)S(1)}, bf16[2,4,16,1024]{3,2,1,0:T(8,128)(2,1)S(1)}, u32[]{:S(2)}, u32[]{:S(2)}) collective-permute-start(bf16[2,4,16,1024]{3,2,1,0:T(8,128)(2,1)S(1)} %get-tuple-element.163), channel_id=1, source_target_pairs={{0,2},{2,4},{4,6},{6,7},{7,5},{5,3},{3,1},{1,0},{8,10},{10,12},{12... | collective-permute-start | bytes 786440 | tf_op jit(solution)/shard_map/ppermute | solution.py:273
  83.3 8.5 %collective-permute-start.25 = (bf16[2,4,16,1024]{3,2,1,0:T(8,128)(2,1)S(1)}, bf16[2,4,16,1024]{3,2,1,0:T(8,128)(2,1)S(1)}, u32[]{:S(2)}, u32[]{:S(2)}) collective-permute-start(bf16[2,4,16,1024]{3,2,1,0:T(8,128)(2,1)S(1)} %get-tuple-element.161), channel_id=1, source_target_pairs={{2,0},{4,2},{6,4},{7,6},{5,7},{3,5},{1,3},{0,1},{10,8},{12,10},{14... | collective-permute-start | bytes 786440 | tf_op jit(solution)/shard_map/ppermute | solution.py:273
  86.7 12.1 %collective-permute-start.29 = (bf16[3,64,1024]{2,1,0:T(8,128)(2,1)S(1)}, bf16[3,64,1024]{2,1,0:T(8,128)(2,1)S(1)}, u32[]{:S(2)}, u32[]{:S(2)}) collective-permute-start(bf16[3,64,1024]{2,1,0:T(8,128)(2,1)S(1)} %get-tuple-element.144), channel_id=1, source_target_pairs={{0,16},{8,24},{16,0},{24,8},{1,17},{9,25},{17,1},{25,9},{2,18},{10... | collective-permute-start | bytes 1179656 | tf_op jit(solution)/shard_map/ppermute | solution.py:297
  88.6 7.1 %collective-permute-start.23 = (bf16[2,4,16,1024]{3,2,1,0:T(8,128)(2,1)S(1)}, bf16[2,4,16,1024]{3,2,1,0:T(8,128)(2,1)S(1)}, u32[]{:S(2)}, u32[]{:S(2)}) collective-permute-start(bf16[2,4,16,1024]{3,2,1,0:T(8,128)(2,1)S(1)} %get-tuple-element.135), channel_id=1, source_target_pairs={{2,0},{4,2},{6,4},{7,6},{5,7},{3,5},{1,3},{0,1},{10,8},{12,10},{14... | collective-permute-start | bytes 786440 | tf_op jit(solution)/shard_map/ppermute | solution.py:273
  90.1 7.1 %collective-permute-start.22 = (bf16[2,4,16,1024]{3,2,1,0:T(8,128)(2,1)S(1)}, bf16[2,4,16,1024]{3,2,1,0:T(8,128)(2,1)S(1)}, u32[]{:S(2)}, u32[]{:S(2)}) collective-permute-start(bf16[2,4,16,1024]{3,2,1,0:T(8,128)(2,1)S(1)} %get-tuple-element.133), channel_id=1, source_target_pairs={{0,2},{2,4},{4,6},{6,7},{7,5},{5,3},{3,1},{1,0},{8,10},{10,12},{12... | collective-permute-start | bytes 786440 | tf_op jit(solution)/shard_map/ppermute | solution.py:273
  94.6 8.2 %collective-permute-start.31 = (bf16[3,32,1024]{2,1,0:T(8,128)(2,1)S(1)}, bf16[3,32,1024]{2,1,0:T(8,128)(2,1)S(1)}, u32[]{:S(2)}, u32[]{:S(2)}) collective-permute-start(bf16[3,32,1024]{2,1,0:T(8,128)(2,1)S(1)} %get-tuple-element.149), channel_id=1, source_target_pairs={{0,16},{8,24},{16,0},{24,8},{1,17},{9,25},{17,1},{25,9},{2,18},{10... | collective-permute-start | bytes 589832 | tf_op jit(solution)/shard_map/ppermute | solution.py:297
  95.7 7.1 %collective-permute-start.32 = (bf16[2,64,1024]{2,1,0:T(8,128)(2,1)S(1)}, bf16[2,64,1024]{2,1,0:T(8,128)(2,1)S(1)}, u32[]{:S(2)}, u32[]{:S(2)}) collective-permute-start(bf16[2,64,1024]{2,1,0:T(8,128)(2,1)S(1)} %get-tuple-element.150), channel_id=1, source_target_pairs={{0,8},{8,0},{16,24},{24,16},{1,9},{9,1},{17,25},{25,17},{2,10},{10... | collective-permute-start | bytes 786440 | tf_op jit(solution)/shard_map/ppermute | solution.py:300
  95.7 7.1 %collective-permute-start.33 = (bf16[2,64,1024]{2,1,0:T(8,128)(2,1)S(1)}, bf16[2,64,1024]{2,1,0:T(8,128)(2,1)S(1)}, u32[]{:S(2)}, u32[]{:S(2)}) collective-permute-start(bf16[2,64,1024]{2,1,0:T(8,128)(2,1)S(1)} %get-tuple-element.151), channel_id=1, source_target_pairs={{0,8},{8,0},{16,24},{24,16},{1,9},{9,1},{17,25},{25,17},{2,10},{10... | collective-permute-start | bytes 786440 | tf_op jit(solution)/shard_map/ppermute | solution.py:300
  100.4 5.7 %collective-permute-start.30 = (bf16[3,32,1024]{2,1,0:T(8,128)(2,1)S(1)}, bf16[3,32,1024]{2,1,0:T(8,128)(2,1)S(1)}, u32[]{:S(2)}, u32[]{:S(2)}) collective-permute-start(bf16[3,32,1024]{2,1,0:T(8,128)(2,1)S(1)} %get-tuple-element.146), channel_id=1, source_target_pairs={{0,16},{8,24},{16,0},{24,8},{1,17},{9,25},{17,1},{25,9},{2,18},{10... | collective-permute-start | bytes 589832 | tf_op jit(solution)/shard_map/ppermute | solution.py:297
  (8 other events, 30.7 us)

commit v6 on v5

--- a/solution.py
+++ b/solution.py
@@ -234,6 +234,34 @@
     return dict(zip(outs, got, strict=True))
 
 
+def cast_kernel(own, shared, *refs):
+    out, buf, sems = refs[-3:]
+    core = lax.rem(lax.axis_index("sector"), 2)
+    nb, half = out.shape[:2]
+    start = pl.multiple_of((core if own else 1 - core) * half, 8)
+    copies = [
+        pltpu.make_async_copy(shared.at[k, pl.ds(start, half), :], buf.at[k], sems.at[k]) for k in range(nb)
+    ]
+    for c in copies:
+        c.start()
+    for k, c in enumerate(copies):
+        c.wait()
+        out[k] = buf[k].astype(BF16)
+
+
+def cast_half(shared, own, *after):
+    nb, rows, m = shared.shape
+    anym = pl.BlockSpec(memory_space=pltpu.HBM)
+    return pl.pallas_call(
+        functools.partial(cast_kernel, own),
+        in_specs=[anym] + [pl.BlockSpec(memory_space=pl.ANY)] * len(after),
+        out_specs=pl.BlockSpec(memory_space=pltpu.VMEM),
+        out_shape=jax.ShapeDtypeStruct((nb, rows // 2, m), BF16),
+        scratch_shapes=[pltpu.VMEM((nb, rows // 2, m), F32), pltpu.SemaphoreType.DMA((nb,))],
+        compiler_params=pltpu.CompilerParams(vmem_limit_bytes=50 * 1024 * 1024),
+    )(shared, *after)
+
+
 def shards(broadcast_ops, resident_ops, integrals, owner_list):
     n_sector = lax.axis_size("sector")
     n_owner = lax.axis_size("owner")
@@ -256,9 +284,9 @@
     static = dict(m=m, nb=nb, half=half, n_owner=n_owner, pairs=pairs, sent=min(pairs, CAP + 1))
 
     shared = broadcast_ops[0]
-    theirs = lax.dynamic_slice_in_dim(shared, (1 - core) * half, half, 1).astype(BF16)
+    theirs = cast_half(shared, False)
     arrived = lax.ppermute(theirs, "sector", swap_core)
-    mine = lax.dynamic_slice_in_dim(shared, core * half, half, 1).astype(BF16)
+    mine = cast_half(shared, True, theirs)
     xs = [jnp.stack([mine[:, a : a + n], arrived[:, a : a + n]]) for _, a, n in lanes]
     resident, *xs = lax.optimization_barrier((resident_ops[0, 0], *xs))
     res_own = resident.astype(BF16)

time: 111 us -> 111 us (level)
    convert_element_type x1 -> x0, local copies, waits for them, and re-layouts: 1.84 us -> none  [shards(): mine = lax.dynamic_slice_in_dim(shared, core * half, half, 1).astype(BF16)]
    unnamed x6 -> x8, local copies, waits for them, and re-layouts: 0.01 us -> 1.62 us
  transfers between devices with their start and end apart: 37 -> 37, of which waited for: 14 -> 14; matrix products, arithmetic and copies ran while one was open for 0% -> 0% of each run, Pallas kernels for 28% -> 29%
where the time goes in v6:
time: 111 us; the launch traced here: 110 us
  waiting for transfers between devices  42.1 us (38%)
  Pallas kernels  32.9 us (30%)
  starting transfers between devices  32.7 us (29%)
  local copies, waits for them, and re-layouts  1.76 us (2%)
    ppermute x16, waiting for transfers between devices, send_on(): return lax.ppermute(x, 'owner', up if turn == 1 else down)  36.6 us
    pallas_call x13, Pallas kernels, step_call(): pl.pallas_call(functools.partial(step_kernel, cfg), in_specs=specs, out_s...  32.6 us
    ppermute x16, starting transfers between devices, send_on(): return lax.ppermute(x, 'owner', up if turn == 1 else down)  17.9 us
    ppermute x9, starting transfers between devices, call(): crossed[i] = lax.ppermute(got['send'], 'sector', swap_side)  12.4 us
    ppermute x9, waiting for transfers between devices, call(): crossed[i] = lax.ppermute(got['send'], 'sector', swap_side)  3.07 us
  transfers between devices with their start and end apart: 37, of which 14 were waited for; matrix products, arithmetic and copies ran while one was open for 0% of the time, Pallas kernels for 29%

profile of v6, /device:TPU:0, one launch (start us, length us, event | category | flops | bytes accessed | tf_op | source)
XLA Modules:
  0.0 110.4 jit_solution(13357626708770728798)
XLA Ops:
  0.0 1.6 %copy-done = f32[1,4,128,1024]{3,2,1,0:T(8,128)S(1)} copy-done((f32[1,4,128,1024]{3,2,1,0:T(8,128)S(1)}, f32[1,4,128,1024]{3,2,1,0:T(8,128)}, u32[]{:S(2)}) %copy-start) | copy-done | bytes 2097176
  2.5 1.3 %collective-permute-done.1 = bf16[4,64,1024]{2,1,0:T(8,128)(2,1)S(1)} collective-permute-done((bf16[4,64,1024]{2,1,0:T(8,128)(2,1)S(1)}, bf16[4,64,1024]{2,1,0:T(8,128)(2,1)S(1)}, u32[]{:S(2)}, u32[]{:S(2)}) %collective-permute-start.1) | collective-permute-done | bytes 524320 | tf_op jit(solution)/shard_map/ppermute | solution.py:288
  4.8 2.6 %collective-permute-start.4 = (bf16[2,4,32,1024]{3,2,1,0:T(8,128)(2,1)S(1)}, bf16[2,4,32,1024]{3,2,1,0:T(8,128)(2,1)}, u32[]{:S(2)}, u32[]{:S(2)}) collective-permute-start(bf16[2,4,32,1024]{3,2,1,0:T(8,128)(2,1)S(1)} %get-tuple-element.84.refs_7_), channel_id=1, source_target_pairs={{2,0},{4,2},{6,4},{7,6},{5,7},{3,5},{1,3},{0,1},{10,8},{12,10},{14... | collective-permute-start | bytes 1572872 | tf_op jit(solution)/shard_map/ppermute | solution.py:301
  8.7 3.7 %shard_map.48 = (s32[1,6]{1,0:T(1,128)S(1)}, f32[32,128]{1,0:T(8,128)S(1)}, bf16[2048,1024]{1,0:T(8,128)(2,1)S(1)}, bf16[3,64,1024]{2,1,0:T(8,128)(2,1)S(1)}, f3...) custom-call(s32[3]{0:T(128)S(1)} %pad_add_fusion.refs_0_, s32[1,4]{1,0:T(1,128)S(1)} %copy-done.2, f32[4,4]{1,0:T(4,128)S(1)} %bitcast.18, ...), custom_call_target="tpu_custom_call" | custom-call | flops 3000000000 | bytes 1000 | tf_op jit(solution)/shard_map/pallas_call | solution.py:224
  12.4 7.6 %collective-permute-done.4.refs_4_ = bf16[2,4,32,1024]{3,2,1,0:T(8,128)(2,1)} collective-permute-done((bf16[2,4,32,1024]{3,2,1,0:T(8,128)(2,1)S(1)}, bf16[2,4,32,1024]{3,2,1,0:T(8,128)(2,1)}, u32[]{:S(2)}, u32[]{:S(2)}) %collective-permute-start.4) | collective-permute-done | bytes 524320 | tf_op jit(solution)/shard_map/ppermute | solution.py:301
  20.0 1.7 %collective-permute-start.6 = (bf16[2,4,32,1024]{3,2,1,0:T(8,128)(2,1)}, bf16[2,4,32,1024]{3,2,1,0:T(8,128)(2,1)S(1)}, u32[]{:S(2)}, u32[]{:S(2)}) collective-permute-start(bf16[2,4,32,1024]{3,2,1,0:T(8,128)(2,1)} %collective-permute-done.4.refs_4_), channel_id=1, source_target_pairs={{2,0},{4,2},{6,4},{7,6},{5,7},{3,5},{1,3},{0,1},{10,8},{12,10},{14... | collective-permute-start | bytes 1572872 | tf_op jit(solution)/shard_map/ppermute | solution.py:301
  22.1 1.7 %collective-permute-start.9 = (bf16[3,64,1024]{2,1,0:T(8,128)(2,1)S(1)}, bf16[3,64,1024]{2,1,0:T(8,128)(2,1)S(1)}, u32[]{:S(2)}, u32[]{:S(2)}) collective-permute-start(bf16[3,64,1024]{2,1,0:T(8,128)(2,1)S(1)} %get-tuple-element.98), channel_id=1, source_target_pairs={{0,16},{8,24},{16,0},{24,8},{1,17},{9,25},{17,1},{25,9},{2,18},{10... | collective-permute-start | bytes 1179656 | tf_op jit(solution)/shard_map/ppermute | solution.py:325
  23.8 2.9 %shard_map.49 = (bf16[3,64,1024]{2,1,0:T(8,128)(2,1)S(1)}, f32[3,64,1024]{2,1,0:T(8,128)S(1)}, f32[8,128]{1,0:T(8,128)S(1)}) custom-call(s32[1,6]{1,0:T(1,128)S(1)} %get-tuple-element.85.refs_0_, bf16[2048,1024]{1,0:T(8,128)(2,1)S(1)} %get-tuple-element.86.refs_1_, f32[32,128]{1,0:T(8,128)S(1)} %get-tuple-element.87.refs_2_, ...), custom_call_target="tpu_custom_call" | custom-call | flops 3000000000 | bytes 1000 | tf_op jit(solution)/shard_map/pallas_call | solution.py:224
  26.7 7.2 %collective-permute-done.6.refs_4_ = bf16[2,4,32,1024]{3,2,1,0:T(8,128)(2,1)S(1)} collective-permute-done((bf16[2,4,32,1024]{3,2,1,0:T(8,128)(2,1)}, bf16[2,4,32,1024]{3,2,1,0:T(8,128)(2,1)S(1)}, u32[]{:S(2)}, u32[]{:S(2)}) %collective-permute-start.6) | collective-permute-done | bytes 524320 | tf_op jit(solution)/shard_map/ppermute | solution.py:301
  33.9 1.4 %collective-permute-start.8 = (bf16[2,4,32,1024]{3,2,1,0:T(8,128)(2,1)S(1)}, bf16[2,4,32,1024]{3,2,1,0:T(8,128)(2,1)S(1)}, u32[]{:S(2)}, u32[]{:S(2)}) collective-permute-start(bf16[2,4,32,1024]{3,2,1,0:T(8,128)(2,1)S(1)} %collective-permute-done.6.refs_4_), channel_id=1, source_target_pairs={{2,0},{4,2},{6,4},{7,6},{5,7},{3,5},{1,3},{0,1},{10,8},{12,10},{14... | collective-permute-start | bytes 1572872 | tf_op jit(solution)/shard_map/ppermute | solution.py:301
  35.9 1.4 %collective-permute-start.12 = (bf16[3,64,1024]{2,1,0:T(8,128)(2,1)S(1)}, bf16[3,64,1024]{2,1,0:T(8,128)(2,1)S(1)}, u32[]{:S(2)}, u32[]{:S(2)}) collective-permute-start(bf16[3,64,1024]{2,1,0:T(8,128)(2,1)S(1)} %get-tuple-element.105), channel_id=1, source_target_pairs={{0,16},{8,24},{16,0},{24,8},{1,17},{9,25},{17,1},{25,9},{2,18},{10... | collective-permute-start | bytes 1179656 | tf_op jit(solution)/shard_map/ppermute | solution.py:325
  37.4 3.2 %shard_map.50 = (bf16[3,64,1024]{2,1,0:T(8,128)(2,1)S(1)}, f32[3,64,1024]{2,1,0:T(8,128)S(1)}, bf16[2,64,1024]{2,1,0:T(8,128)(2,1)S(1)}, f32[8,128]{1,0:T(8,128)S(1)}, f32[2,1024,1024]{2,1,0:T(8,128)}) custom-call(s32[1,6]{1,0:T(1,128)S(1)} %get-tuple-element.85.refs_0_, bf16[2048,1024]{1,0:T(8,128)(2,1)S(1)} %get-tuple-element.86.refs_1_, ...), custom_call_target="tpu_custom_call" | custom-call | flops 3000000000 | bytes 1000 | tf_op jit(solution)/shard_map/pallas_call | solution.py:224
  40.6 6.0 %collective-permute-done.8.refs_4_ = bf16[2,4,32,1024]{3,2,1,0:T(8,128)(2,1)S(1)} collective-permute-done((bf16[2,4,32,1024]{3,2,1,0:T(8,128)(2,1)S(1)}, bf16[2,4,32,1024]{3,2,1,0:T(8,128)(2,1)S(1)}, u32[]{:S(2)}, u32[]{:S(2)}) %collective-permute-start.8) | collective-permute-done | bytes 524320 | tf_op jit(solution)/shard_map/ppermute | solution.py:301
  49.8 3.4 %shard_map.51 = (bf16[3,64,1024]{2,1,0:T(8,128)(2,1)S(1)}, f32[3,64,1024]{2,1,0:T(8,128)S(1)}, bf16[2,64,1024]{2,1,0:T(8,128)(2,1)S(1)}, f32[8,128]{1,0:T(8,128)S(1)}, f32[2,1024,1024]{2,1,0:T(8,128)}) custom-call(s32[1,6]{1,0:T(1,128)S(1)} %get-tuple-element.85.refs_0_, ...), custom_call_target="tpu_custom_call", output_to_operand_aliasing={{4}: (9, {})} | custom-call | flops 3000000000 | bytes 1000 | tf_op jit(solution)/shard_map/pallas_call | solution.py:224
  53.3 5.4 %collective-permute-done.11.refs_4_ = bf16[2,4,32,1024]{3,2,1,0:T(8,128)(2,1)S(1)} collective-permute-done((bf16[2,4,32,1024]{3,2,1,0:T(8,128)(2,1)S(1)}, bf16[2,4,32,1024]{3,2,1,0:T(8,128)(2,1)S(1)}, u32[]{:S(2)}, u32[]{:S(2)}) %collective-permute-start.11) | collective-permute-done | bytes 524320 | tf_op jit(solution)/shard_map/ppermute | solution.py:301
  61.9 3.4 %shard_map.52 = (bf16[3,64,1024]{2,1,0:T(8,128)(2,1)S(1)}, f32[3,64,1024]{2,1,0:T(8,128)S(1)}, bf16[2,64,1024]{2,1,0:T(8,128)(2,1)S(1)}, f32[8,128]{1,0:T(8,128)S(1)}, f32[2,1024,1024]{2,1,0:T(8,128)}) custom-call(s32[1,6]{1,0:T(1,128)S(1)} %get-tuple-element.85.refs_0_, ...), custom_call_target="tpu_custom_call", output_to_operand_aliasing={{4}: (9, {})} | custom-call | flops 3000000000 | bytes 1000 | tf_op jit(solution)/shard_map/pallas_call | solution.py:224
  65.4 5.4 %collective-permute-done.15.refs_4_ = bf16[2,4,32,1024]{3,2,1,0:T(8,128)(2,1)S(1)} collective-permute-done((bf16[2,4,32,1024]{3,2,1,0:T(8,128)(2,1)S(1)}, bf16[2,4,32,1024]{3,2,1,0:T(8,128)(2,1)S(1)}, u32[]{:S(2)}, u32[]{:S(2)}) %collective-permute-start.15) | collective-permute-done | bytes 524320 | tf_op jit(solution)/shard_map/ppermute | solution.py:301
  71.1 1.7 %collective-permute-start.18 = (bf16[2,4,32,1024]{3,2,1,0:T(8,128)(2,1)S(1)}, bf16[2,4,32,1024]{3,2,1,0:T(8,128)(2,1)S(1)}, u32[]{:S(2)}, u32[]{:S(2)}) collective-permute-start(bf16[2,4,32,1024]{3,2,1,0:T(8,128)(2,1)S(1)} %collective-permute-done.14.refs_3_), channel_id=1, source_target_pairs={{0,2},{2,4},{4,6},{6,7},{7,5},{5,3},{3,1},{1,0},{8,10},{10,12},{12... | collective-permute-start | bytes 1572872 | tf_op jit(solution)/shard_map/ppermute | solution.py:301
  73.8 3.4 %shard_map.53 = (bf16[3,64,1024]{2,1,0:T(8,128)(2,1)S(1)}, f32[3,64,1024]{2,1,0:T(8,128)S(1)}, bf16[2,64,1024]{2,1,0:T(8,128)(2,1)S(1)}, f32[8,128]{1,0:T(8,128)S(1)}, f32[2,1024,1024]{2,1,0:T(8,128)}) custom-call(s32[1,6]{1,0:T(1,128)S(1)} %get-tuple-element.85.refs_0_, ...), custom_call_target="tpu_custom_call", output_to_operand_aliasing={{4}: (9, {})} | custom-call | flops 3000000000 | bytes 1000 | tf_op jit(solution)/shard_map/pallas_call | solution.py:224
  78.4 2.5 %collective-permute-done.19.refs_4_ = bf16[2,4,32,1024]{3,2,1,0:T(8,128)(2,1)S(1)} collective-permute-done((bf16[2,4,32,1024]{3,2,1,0:T(8,128)(2,1)S(1)}, bf16[2,4,32,1024]{3,2,1,0:T(8,128)(2,1)S(1)}, u32[]{:S(2)}, u32[]{:S(2)}) %collective-permute-start.19) | collective-permute-done | bytes 524320 | tf_op jit(solution)/shard_map/ppermute | solution.py:301
  81.8 1.4 %collective-permute-start.24 = (bf16[2,4,16,1024]{3,2,1,0:T(8,128)(2,1)S(1)}, bf16[2,4,16,1024]{3,2,1,0:T(8,128)(2,1)S(1)}, u32[]{:S(2)}, u32[]{:S(2)}) collective-permute-start(bf16[2,4,16,1024]{3,2,1,0:T(8,128)(2,1)S(1)} %get-tuple-element.161), channel_id=1, source_target_pairs={{0,2},{2,4},{4,6},{6,7},{7,5},{5,3},{3,1},{1,0},{8,10},{10,12},{12... | collective-permute-start | bytes 786440 | tf_op jit(solution)/shard_map/ppermute | solution.py:301
  84.3 2.3 %shard_map.54 = (bf16[3,64,1024]{2,1,0:T(8,128)(2,1)S(1)}, f32[3,64,1024]{2,1,0:T(8,128)S(1)}, f32[8,128]{1,0:T(8,128)S(1)}) custom-call(s32[1,6]{1,0:T(1,128)S(1)} %get-tuple-element.85.refs_0_, bf16[2048,1024]{1,0:T(8,128)(2,1)S(1)} %get-tuple-element.86.refs_1_, f32[32,128]{1,0:T(8,128)S(1)} %get-tuple-element.87.refs_2_, ...), custom_call_target="tpu_custom_call" | custom-call | flops 3000000000 | bytes 1000 | tf_op jit(solution)/shard_map/pallas_call | solution.py:224
  86.6 1.9 %collective-permute-start.29 = (bf16[3,64,1024]{2,1,0:T(8,128)(2,1)S(1)}, bf16[3,64,1024]{2,1,0:T(8,128)(2,1)S(1)}, u32[]{:S(2)}, u32[]{:S(2)}) collective-permute-start(bf16[3,64,1024]{2,1,0:T(8,128)(2,1)S(1)} %get-tuple-element.144), channel_id=1, source_target_pairs={{0,16},{8,24},{16,0},{24,8},{1,17},{9,25},{17,1},{25,9},{2,18},{10... | collective-permute-start | bytes 1179656 | tf_op jit(solution)/shard_map/ppermute | solution.py:325
  88.5 1.5 %collective-permute-start.23 = (bf16[2,4,16,1024]{3,2,1,0:T(8,128)(2,1)S(1)}, bf16[2,4,16,1024]{3,2,1,0:T(8,128)(2,1)S(1)}, u32[]{:S(2)}, u32[]{:S(2)}) collective-permute-start(bf16[2,4,16,1024]{3,2,1,0:T(8,128)(2,1)S(1)} %get-tuple-element.135), channel_id=1, source_target_pairs={{2,0},{4,2},{6,4},{7,6},{5,7},{3,5},{1,3},{0,1},{10,8},{12,10},{14... | collective-permute-start | bytes 786440 | tf_op jit(solution)/shard_map/ppermute | solution.py:301
  91.7 2.8 %shard_map.55 = (bf16[3,32,1024]{2,1,0:T(8,128)(2,1)S(1)}, f32[3,32,1024]{2,1,0:T(8,128)S(1)}, bf16[2,64,1024]{2,1,0:T(8,128)(2,1)S(1)}, bf16[2,64,1024]{2,1,0:T...) custom-call(s32[1,6]{1,0:T(1,128)S(1)} %get-tuple-element.85.refs_0_, ...), custom_call_target="tpu_custom_call", output_to_operand_aliasing={{5}: (11, {})} | custom-call | flops 3000000000 | bytes 1000 | tf_op jit(solution)/shard_map/pallas_call | solution.py:224
  97.1 1.7 %collective-permute-done.29.refs_6_.refs_2_ = bf16[3,64,1024]{2,1,0:T(8,128)(2,1)S(1)} collective-permute-done((bf16[3,64,1024]{2,1,0:T(8,128)(2,1)S(1)}, bf16[3,64,1024]{2,1,0:T(8,128)(2,1)S(1)}, u32[]{:S(2)}, u32[]{:S(2)}) %collective-permute-start.29) | collective-permute-done | bytes 393248 | tf_op jit(solution)/shard_map/ppermute | solution.py:325
  98.7 1.6 %shard_map.56 = (bf16[3,32,1024]{2,1,0:T(8,128)(2,1)S(1)}, f32[3,32,1024]{2,1,0:T(8,128)S(1)}, f32[8,128]{1,0:T(8,128)S(1)}) custom-call(s32[1,6]{1,0:T(1,128)S(1)} %get-tuple-element.85.refs_0_, bf16[2048,1024]{1,0:T(8,128)(2,1)S(1)} %get-tuple-element.86.refs_1_, f32[32,128]{1,0:T(8,128)S(1)} %get-tuple-element.87.refs_2_, ...), custom_call_target="tpu_custom_call" | custom-call | flops 3000000000 | bytes 1000 | tf_op jit(solution)/shard_map/pallas_call | solution.py:224
  100.3 1.9 %collective-permute-start.30 = (bf16[3,32,1024]{2,1,0:T(8,128)(2,1)S(1)}, bf16[3,32,1024]{2,1,0:T(8,128)(2,1)S(1)}, u32[]{:S(2)}, u32[]{:S(2)}) collective-permute-start(bf16[3,32,1024]{2,1,0:T(8,128)(2,1)S(1)} %get-tuple-element.146), channel_id=1, source_target_pairs={{0,16},{8,24},{16,0},{24,8},{1,17},{9,25},{17,1},{25,9},{2,18},{10... | collective-permute-start | bytes 589832 | tf_op jit(solution)/shard_map/ppermute | solution.py:325
  102.7 1.9 %shard_map.57 = (bf16[2,64,1024]{2,1,0:T(8,128)(2,1)S(1)}, bf16[2,32,1024]{2,1,0:T(8,128)(2,1)S(1)}, f32[2,1024,1024]{2,1,0:T(8,128)}) custom-call(s32[1,6]{1,0:T(1,128)S(1)} %get-tuple-element.85.refs_0_, f32[3,64,1024]{2,1,0:T(8,128)S(1)} %get-tuple-element.147.refs_1_, ...), custom_call_target="tpu_custom_call", output_to_operand_aliasing={{2}: (8, {})} | custom-call | flops 3000000000 | bytes 1000 | tf_op jit(solution)/shard_map/pallas_call | solution.py:224
  106.1 1.3 %shard_map.58 = (bf16[2,32,1024]{2,1,0:T(8,128)(2,1)S(1)}, f32[2,1024,1024]{2,1,0:T(8,128)}) custom-call(s32[1,6]{1,0:T(1,128)S(1)} %get-tuple-element.85.refs_0_, f32[3,32,1024]{2,1,0:T(8,128)S(1)} %get-tuple-element.145.refs_1_, bf16[3,32,1024]{2,1,0:T(8,128)(2,1)S(1)} %collective-permute-done.30.refs_2_, ...), custom_call_target="tpu_custom_call", output_to_operand_aliasing={{1}: (3, {})} | custom-call | flops 3000000000 | bytes 1000 | tf_op jit(solution)/shard_map/pallas_call | solution.py:224
  107.5 1.5 %shard_map.59.refs_2_ = f32[2,1024,1024]{2,1,0:T(8,128)} custom-call(s32[1,6]{1,0:T(1,128)S(1)} %get-tuple-element.85.refs_0_, bf16[2,64,1024]{2,1,0:T(8,128)(2,1)S(1)} %collective-permute-done.35.refs_1_, bf16[2,32,1024]{2,1,0:T(8,128)(2,1)S(1)} %collective-permute-done.36.refs_2_, ...), custom_call_target="tpu_custom_call", output_to_operand_aliasing={{}: (3, {})} | custom-call | flops 3000000000 | bytes 1000 | tf_op jit(solution)/shard_map/pallas_call | solution.py:224
  109.0 1.3 %shard_map.60 = f32[2,1024,1024]{2,1,0:T(8,128)} custom-call(s32[1,6]{1,0:T(1,128)S(1)} %get-tuple-element.85.refs_0_, bf16[2,32,1024]{2,1,0:T(8,128)(2,1)S(1)} %collective-permute-done.34.refs_1_, f32[2,1024,1024]{2,1,0:T(8,128)} %shard_map.59.refs_2_), custom_call_target="tpu_custom_call", output_to_operand_aliasing={{}: (2, {})} | custom-call | flops 3000000000 | bytes 1000 | tf_op jit(solution)/shard_map/pallas_call | solution.py:224
  (72 shorter events, 21.5 us)
Async XLA Ops:
  4.3 4.4 %collective-permute-start.2 = (bf16[1024,1024]{1,0:T(8,128)(2,1)S(1)}, bf16[1024,1024]{1,0:T(8,128)(2,1)}, u32[]{:S(2)}, u32[]{:S(2)}) collective-permute-start(bf16[1024,1024]{1,0:T(8,128)(2,1)S(1)} %convert_element_type.3.refs_4_), channel_id=1, source_target_pairs={{0,8},{8,0},{16,24},{24,16},{1,9},{9,1},{17,25},{25,17},{2,10},{10... | collective-permute-start | bytes 6291464 | tf_op jit(solution)/shard_map/ppermute | solution.py:295
  4.8 15.3 %collective-permute-start.4 = (bf16[2,4,32,1024]{3,2,1,0:T(8,128)(2,1)S(1)}, bf16[2,4,32,1024]{3,2,1,0:T(8,128)(2,1)}, u32[]{:S(2)}, u32[]{:S(2)}) collective-permute-start(bf16[2,4,32,1024]{3,2,1,0:T(8,128)(2,1)S(1)} %get-tuple-element.84.refs_7_), channel_id=1, source_target_pairs={{2,0},{4,2},{6,4},{7,6},{5,7},{3,5},{1,3},{0,1},{10,8},{12,10},{14... | collective-permute-start | bytes 1572872 | tf_op jit(solution)/shard_map/ppermute | solution.py:301
  7.4 14.3 %collective-permute-start.3 = (bf16[2,4,32,1024]{3,2,1,0:T(8,128)(2,1)S(1)}, bf16[2,4,32,1024]{3,2,1,0:T(8,128)(2,1)}, u32[]{:S(2)}, u32[]{:S(2)}) collective-permute-start(bf16[2,4,32,1024]{3,2,1,0:T(8,128)(2,1)S(1)} %get-tuple-element.83.refs_6_), channel_id=1, source_target_pairs={{0,2},{2,4},{4,6},{6,7},{7,5},{5,3},{3,1},{1,0},{8,10},{10,12},{12... | collective-permute-start | bytes 1572872 | tf_op jit(solution)/shard_map/ppermute | solution.py:301
  20.0 13.8 %collective-permute-start.6 = (bf16[2,4,32,1024]{3,2,1,0:T(8,128)(2,1)}, bf16[2,4,32,1024]{3,2,1,0:T(8,128)(2,1)S(1)}, u32[]{:S(2)}, u32[]{:S(2)}) collective-permute-start(bf16[2,4,32,1024]{3,2,1,0:T(8,128)(2,1)} %collective-permute-done.4.refs_4_), channel_id=1, source_target_pairs={{2,0},{4,2},{6,4},{7,6},{5,7},{3,5},{1,3},{0,1},{10,8},{12,10},{14... | collective-permute-start | bytes 1572872 | tf_op jit(solution)/shard_map/ppermute | solution.py:301
  21.7 13.6 %collective-permute-start.5 = (bf16[2,4,32,1024]{3,2,1,0:T(8,128)(2,1)}, bf16[2,4,32,1024]{3,2,1,0:T(8,128)(2,1)S(1)}, u32[]{:S(2)}, u32[]{:S(2)}) collective-permute-start(bf16[2,4,32,1024]{3,2,1,0:T(8,128)(2,1)} %collective-permute-done.3.refs_3_), channel_id=1, source_target_pairs={{0,2},{2,4},{4,6},{6,7},{7,5},{5,3},{3,1},{1,0},{8,10},{10,12},{12... | collective-permute-start | bytes 1572872 | tf_op jit(solution)/shard_map/ppermute | solution.py:301
  22.1 15.3 %collective-permute-start.9 = (bf16[3,64,1024]{2,1,0:T(8,128)(2,1)S(1)}, bf16[3,64,1024]{2,1,0:T(8,128)(2,1)S(1)}, u32[]{:S(2)}, u32[]{:S(2)}) collective-permute-start(bf16[3,64,1024]{2,1,0:T(8,128)(2,1)S(1)} %get-tuple-element.98), channel_id=1, source_target_pairs={{0,16},{8,24},{16,0},{24,8},{1,17},{9,25},{17,1},{25,9},{2,18},{10... | collective-permute-start | bytes 1179656 | tf_op jit(solution)/shard_map/ppermute | solution.py:325
  33.9 12.7 %collective-permute-start.8 = (bf16[2,4,32,1024]{3,2,1,0:T(8,128)(2,1)S(1)}, bf16[2,4,32,1024]{3,2,1,0:T(8,128)(2,1)S(1)}, u32[]{:S(2)}, u32[]{:S(2)}) collective-permute-start(bf16[2,4,32,1024]{3,2,1,0:T(8,128)(2,1)S(1)} %collective-permute-done.6.refs_4_), channel_id=1, source_target_pairs={{2,0},{4,2},{6,4},{7,6},{5,7},{3,5},{1,3},{0,1},{10,8},{12,10},{14... | collective-permute-start | bytes 1572872 | tf_op jit(solution)/shard_map/ppermute | solution.py:301
  35.3 12.5 %collective-permute-start.7 = (bf16[2,4,32,1024]{3,2,1,0:T(8,128)(2,1)S(1)}, bf16[2,4,32,1024]{3,2,1,0:T(8,128)(2,1)S(1)}, u32[]{:S(2)}, u32[]{:S(2)}) collective-permute-start(bf16[2,4,32,1024]{3,2,1,0:T(8,128)(2,1)S(1)} %collective-permute-done.5.refs_3_), channel_id=1, source_target_pairs={{0,2},{2,4},{4,6},{6,7},{7,5},{5,3},{3,1},{1,0},{8,10},{10,12},{12... | collective-permute-start | bytes 1572872 | tf_op jit(solution)/shard_map/ppermute | solution.py:301
  35.9 13.9 %collective-permute-start.12 = (bf16[3,64,1024]{2,1,0:T(8,128)(2,1)S(1)}, bf16[3,64,1024]{2,1,0:T(8,128)(2,1)S(1)}, u32[]{:S(2)}, u32[]{:S(2)}) collective-permute-start(bf16[3,64,1024]{2,1,0:T(8,128)(2,1)S(1)} %get-tuple-element.105), channel_id=1, source_target_pairs={{0,16},{8,24},{16,0},{24,8},{1,17},{9,25},{17,1},{25,9},{2,18},{10... | collective-permute-start | bytes 1179656 | tf_op jit(solution)/shard_map/ppermute | solution.py:325
  40.6 9.3 %collective-permute-start.13 = (bf16[2,64,1024]{2,1,0:T(8,128)(2,1)S(1)}, bf16[2,64,1024]{2,1,0:T(8,128)(2,1)S(1)}, u32[]{:S(2)}, u32[]{:S(2)}) collective-permute-start(bf16[2,64,1024]{2,1,0:T(8,128)(2,1)S(1)} %get-tuple-element.106), channel_id=1, source_target_pairs={{0,8},{8,0},{16,24},{24,16},{1,9},{9,1},{17,25},{25,17},{2,10},{10... | collective-permute-start | bytes 786440 | tf_op jit(solution)/shard_map/ppermute | solution.py:328
  46.6 12.1 %collective-permute-start.11 = (bf16[2,4,32,1024]{3,2,1,0:T(8,128)(2,1)S(1)}, bf16[2,4,32,1024]{3,2,1,0:T(8,128)(2,1)S(1)}, u32[]{:S(2)}, u32[]{:S(2)}) collective-permute-start(bf16[2,4,32,1024]{3,2,1,0:T(8,128)(2,1)S(1)} %collective-permute-done.8.refs_4_), channel_id=1, source_target_pairs={{2,0},{4,2},{6,4},{7,6},{5,7},{3,5},{1,3},{0,1},{10,8},{12,10},{14... | collective-permute-start | bytes 1572872 | tf_op jit(solution)/shard_map/ppermute | solution.py:301
  47.8 12.1 %collective-permute-start.10 = (bf16[2,4,32,1024]{3,2,1,0:T(8,128)(2,1)S(1)}, bf16[2,4,32,1024]{3,2,1,0:T(8,128)(2,1)S(1)}, u32[]{:S(2)}, u32[]{:S(2)}) collective-permute-start(bf16[2,4,32,1024]{3,2,1,0:T(8,128)(2,1)S(1)} %collective-permute-done.7.refs_3_), channel_id=1, source_target_pairs={{0,2},{2,4},{4,6},{6,7},{7,5},{5,3},{3,1},{1,0},{8,10},{10,12},{12... | collective-permute-start | bytes 1572872 | tf_op jit(solution)/shard_map/ppermute | solution.py:301
  48.7 13.3 %collective-permute-start.16 = (bf16[3,64,1024]{2,1,0:T(8,128)(2,1)S(1)}, bf16[3,64,1024]{2,1,0:T(8,128)(2,1)S(1)}, u32[]{:S(2)}, u32[]{:S(2)}) collective-permute-start(bf16[3,64,1024]{2,1,0:T(8,128)(2,1)S(1)} %get-tuple-element.114), channel_id=1, source_target_pairs={{0,16},{8,24},{16,0},{24,8},{1,17},{9,25},{17,1},{25,9},{2,18},{10... | collective-permute-start | bytes 1179656 | tf_op jit(solution)/shard_map/ppermute | solution.py:325
  53.2 8.7 %collective-permute-start.17 = (bf16[2,64,1024]{2,1,0:T(8,128)(2,1)S(1)}, bf16[2,64,1024]{2,1,0:T(8,128)(2,1)S(1)}, u32[]{:S(2)}, u32[]{:S(2)}) collective-permute-start(bf16[2,64,1024]{2,1,0:T(8,128)(2,1)S(1)} %get-tuple-element.115), channel_id=1, source_target_pairs={{0,8},{8,0},{16,24},{24,16},{1,9},{9,1},{17,25},{25,17},{2,10},{10... | collective-permute-start | bytes 786440 | tf_op jit(solution)/shard_map/ppermute | solution.py:328
  58.7 12.1 %collective-permute-start.15 = (bf16[2,4,32,1024]{3,2,1,0:T(8,128)(2,1)S(1)}, bf16[2,4,32,1024]{3,2,1,0:T(8,128)(2,1)S(1)}, u32[]{:S(2)}, u32[]{:S(2)}) collective-permute-start(bf16[2,4,32,1024]{3,2,1,0:T(8,128)(2,1)S(1)} %collective-permute-done.11.refs_4_), channel_id=1, source_target_pairs={{2,0},{4,2},{6,4},{7,6},{5,7},{3,5},{1,3},{0,1},{10,8},{12,10},{14... | collective-permute-start | bytes 1572872 | tf_op jit(solution)/shard_map/ppermute | solution.py:301
  59.9 11.2 %collective-permute-start.14 = (bf16[2,4,32,1024]{3,2,1,0:T(8,128)(2,1)S(1)}, bf16[2,4,32,1024]{3,2,1,0:T(8,128)(2,1)S(1)}, u32[]{:S(2)}, u32[]{:S(2)}) collective-permute-start(bf16[2,4,32,1024]{3,2,1,0:T(8,128)(2,1)S(1)} %collective-permute-done.10.refs_3_), channel_id=1, source_target_pairs={{0,2},{2,4},{4,6},{6,7},{7,5},{5,3},{3,1},{1,0},{8,10},{10,12},{12... | collective-permute-start | bytes 1572872 | tf_op jit(solution)/shard_map/ppermute | solution.py:301
  60.7 13.1 %collective-permute-start.20 = (bf16[3,64,1024]{2,1,0:T(8,128)(2,1)S(1)}, bf16[3,64,1024]{2,1,0:T(8,128)(2,1)S(1)}, u32[]{:S(2)}, u32[]{:S(2)}) collective-permute-start(bf16[3,64,1024]{2,1,0:T(8,128)(2,1)S(1)} %get-tuple-element.123), channel_id=1, source_target_pairs={{0,16},{8,24},{16,0},{24,8},{1,17},{9,25},{17,1},{25,9},{2,18},{10... | collective-permute-start | bytes 1179656 | tf_op jit(solution)/shard_map/ppermute | solution.py:325
  65.3 8.5 %collective-permute-start.21 = (bf16[2,64,1024]{2,1,0:T(8,128)(2,1)S(1)}, bf16[2,64,1024]{2,1,0:T(8,128)(2,1)S(1)}, u32[]{:S(2)}, u32[]{:S(2)}) collective-permute-start(bf16[2,64,1024]{2,1,0:T(8,128)(2,1)S(1)} %get-tuple-element.124), channel_id=1, source_target_pairs={{0,8},{8,0},{16,24},{24,16},{1,9},{9,1},{17,25},{25,17},{2,10},{10... | collective-permute-start | bytes 786440 | tf_op jit(solution)/shard_map/ppermute | solution.py:328
  70.8 10.1 %collective-permute-start.19 = (bf16[2,4,32,1024]{3,2,1,0:T(8,128)(2,1)S(1)}, bf16[2,4,32,1024]{3,2,1,0:T(8,128)(2,1)S(1)}, u32[]{:S(2)}, u32[]{:S(2)}) collective-permute-start(bf16[2,4,32,1024]{3,2,1,0:T(8,128)(2,1)S(1)} %collective-permute-done.15.refs_4_), channel_id=1, source_target_pairs={{2,0},{4,2},{6,4},{7,6},{5,7},{3,5},{1,3},{0,1},{10,8},{12,10},{14... | collective-permute-start | bytes 1572872 | tf_op jit(solution)/shard_map/ppermute | solution.py:301
  71.1 10.6 %collective-permute-start.18 = (bf16[2,4,32,1024]{3,2,1,0:T(8,128)(2,1)S(1)}, bf16[2,4,32,1024]{3,2,1,0:T(8,128)(2,1)S(1)}, u32[]{:S(2)}, u32[]{:S(2)}) collective-permute-start(bf16[2,4,32,1024]{3,2,1,0:T(8,128)(2,1)S(1)} %collective-permute-done.14.refs_3_), channel_id=1, source_target_pairs={{0,2},{2,4},{4,6},{6,7},{7,5},{5,3},{3,1},{1,0},{8,10},{10,12},{12... | collective-permute-start | bytes 1572872 | tf_op jit(solution)/shard_map/ppermute | solution.py:301
  72.8 13.8 %collective-permute-start.26 = (bf16[3,64,1024]{2,1,0:T(8,128)(2,1)S(1)}, bf16[3,64,1024]{2,1,0:T(8,128)(2,1)S(1)}, u32[]{:S(2)}, u32[]{:S(2)}) collective-permute-start(bf16[3,64,1024]{2,1,0:T(8,128)(2,1)S(1)} %get-tuple-element.137), channel_id=1, source_target_pairs={{0,16},{8,24},{16,0},{24,8},{1,17},{9,25},{17,1},{25,9},{2,18},{10... | collective-permute-start | bytes 1179656 | tf_op jit(solution)/shard_map/ppermute | solution.py:325
  77.2 11.3 %collective-permute-start.28 = (bf16[2,64,1024]{2,1,0:T(8,128)(2,1)S(1)}, bf16[2,64,1024]{2,1,0:T(8,128)(2,1)S(1)}, u32[]{:S(2)}, u32[]{:S(2)}) collective-permute-start(bf16[2,64,1024]{2,1,0:T(8,128)(2,1)S(1)} %get-tuple-element.140), channel_id=1, source_target_pairs={{0,8},{8,0},{16,24},{24,16},{1,9},{9,1},{17,25},{25,17},{2,10},{10... | collective-permute-start | bytes 786440 | tf_op jit(solution)/shard_map/ppermute | solution.py:328
  77.3 12.7 %collective-permute-start.27 = (bf16[3,64,1024]{2,1,0:T(8,128)(2,1)S(1)}, bf16[3,64,1024]{2,1,0:T(8,128)(2,1)S(1)}, u32[]{:S(2)}, u32[]{:S(2)}) collective-permute-start(bf16[3,64,1024]{2,1,0:T(8,128)(2,1)S(1)} %get-tuple-element.139), channel_id=1, source_target_pairs={{0,16},{8,24},{16,0},{24,8},{1,17},{9,25},{17,1},{25,9},{2,18},{10... | collective-permute-start | bytes 1179656 | tf_op jit(solution)/shard_map/ppermute | solution.py:325
  81.8 9.3 %collective-permute-start.24 = (bf16[2,4,16,1024]{3,2,1,0:T(8,128)(2,1)S(1)}, bf16[2,4,16,1024]{3,2,1,0:T(8,128)(2,1)S(1)}, u32[]{:S(2)}, u32[]{:S(2)}) collective-permute-start(bf16[2,4,16,1024]{3,2,1,0:T(8,128)(2,1)S(1)} %get-tuple-element.161), channel_id=1, source_target_pairs={{0,2},{2,4},{4,6},{6,7},{7,5},{5,3},{3,1},{1,0},{8,10},{10,12},{12... | collective-permute-start | bytes 786440 | tf_op jit(solution)/shard_map/ppermute | solution.py:301
  83.2 8.5 %collective-permute-start.25 = (bf16[2,4,16,1024]{3,2,1,0:T(8,128)(2,1)S(1)}, bf16[2,4,16,1024]{3,2,1,0:T(8,128)(2,1)S(1)}, u32[]{:S(2)}, u32[]{:S(2)}) collective-permute-start(bf16[2,4,16,1024]{3,2,1,0:T(8,128)(2,1)S(1)} %get-tuple-element.159), channel_id=1, source_target_pairs={{2,0},{4,2},{6,4},{7,6},{5,7},{3,5},{1,3},{0,1},{10,8},{12,10},{14... | collective-permute-start | bytes 786440 | tf_op jit(solution)/shard_map/ppermute | solution.py:301
  86.6 12.1 %collective-permute-start.29 = (bf16[3,64,1024]{2,1,0:T(8,128)(2,1)S(1)}, bf16[3,64,1024]{2,1,0:T(8,128)(2,1)S(1)}, u32[]{:S(2)}, u32[]{:S(2)}) collective-permute-start(bf16[3,64,1024]{2,1,0:T(8,128)(2,1)S(1)} %get-tuple-element.144), channel_id=1, source_target_pairs={{0,16},{8,24},{16,0},{24,8},{1,17},{9,25},{17,1},{25,9},{2,18},{10... | collective-permute-start | bytes 1179656 | tf_op jit(solution)/shard_map/ppermute | solution.py:325
  88.5 7.1 %collective-permute-start.23 = (bf16[2,4,16,1024]{3,2,1,0:T(8,128)(2,1)S(1)}, bf16[2,4,16,1024]{3,2,1,0:T(8,128)(2,1)S(1)}, u32[]{:S(2)}, u32[]{:S(2)}) collective-permute-start(bf16[2,4,16,1024]{3,2,1,0:T(8,128)(2,1)S(1)} %get-tuple-element.135), channel_id=1, source_target_pairs={{2,0},{4,2},{6,4},{7,6},{5,7},{3,5},{1,3},{0,1},{10,8},{12,10},{14... | collective-permute-start | bytes 786440 | tf_op jit(solution)/shard_map/ppermute | solution.py:301
  90.0 7.1 %collective-permute-start.22 = (bf16[2,4,16,1024]{3,2,1,0:T(8,128)(2,1)S(1)}, bf16[2,4,16,1024]{3,2,1,0:T(8,128)(2,1)S(1)}, u32[]{:S(2)}, u32[]{:S(2)}) collective-permute-start(bf16[2,4,16,1024]{3,2,1,0:T(8,128)(2,1)S(1)} %get-tuple-element.133), channel_id=1, source_target_pairs={{0,2},{2,4},{4,6},{6,7},{7,5},{5,3},{3,1},{1,0},{8,10},{10,12},{12... | collective-permute-start | bytes 786440 | tf_op jit(solution)/shard_map/ppermute | solution.py:301
  94.5 8.2 %collective-permute-start.31 = (bf16[3,32,1024]{2,1,0:T(8,128)(2,1)S(1)}, bf16[3,32,1024]{2,1,0:T(8,128)(2,1)S(1)}, u32[]{:S(2)}, u32[]{:S(2)}) collective-permute-start(bf16[3,32,1024]{2,1,0:T(8,128)(2,1)S(1)} %get-tuple-element.149), channel_id=1, source_target_pairs={{0,16},{8,24},{16,0},{24,8},{1,17},{9,25},{17,1},{25,9},{2,18},{10... | collective-permute-start | bytes 589832 | tf_op jit(solution)/shard_map/ppermute | solution.py:325
  95.6 7.1 %collective-permute-start.32 = (bf16[2,64,1024]{2,1,0:T(8,128)(2,1)S(1)}, bf16[2,64,1024]{2,1,0:T(8,128)(2,1)S(1)}, u32[]{:S(2)}, u32[]{:S(2)}) collective-permute-start(bf16[2,64,1024]{2,1,0:T(8,128)(2,1)S(1)} %get-tuple-element.150), channel_id=1, source_target_pairs={{0,8},{8,0},{16,24},{24,16},{1,9},{9,1},{17,25},{25,17},{2,10},{10... | collective-permute-start | bytes 786440 | tf_op jit(solution)/shard_map/ppermute | solution.py:328
  95.6 7.1 %collective-permute-start.33 = (bf16[2,64,1024]{2,1,0:T(8,128)(2,1)S(1)}, bf16[2,64,1024]{2,1,0:T(8,128)(2,1)S(1)}, u32[]{:S(2)}, u32[]{:S(2)}) collective-permute-start(bf16[2,64,1024]{2,1,0:T(8,128)(2,1)S(1)} %get-tuple-element.151), channel_id=1, source_target_pairs={{0,8},{8,0},{16,24},{24,16},{1,9},{9,1},{17,25},{25,17},{2,10},{10... | collective-permute-start | bytes 786440 | tf_op jit(solution)/shard_map/ppermute | solution.py:328
  100.3 5.7 %collective-permute-start.30 = (bf16[3,32,1024]{2,1,0:T(8,128)(2,1)S(1)}, bf16[3,32,1024]{2,1,0:T(8,128)(2,1)S(1)}, u32[]{:S(2)}, u32[]{:S(2)}) collective-permute-start(bf16[3,32,1024]{2,1,0:T(8,128)(2,1)S(1)} %get-tuple-element.146), channel_id=1, source_target_pairs={{0,16},{8,24},{16,0},{24,8},{1,17},{9,25},{17,1},{25,9},{2,18},{10... | collective-permute-start | bytes 589832 | tf_op jit(solution)/shard_map/ppermute | solution.py:325
  (9 other events, 28.9 us)
